TPU v7x, 32 devices: a whole 2x2x4 slice. The times are simulated.
32 devices in a mesh: leaf: 8 (over y, x, core), row: 4 (over z).
Axes of the slice: x: 2, y: 2, z: 4, core: 2. Of those that a mesh axis runs over, the one named last changes fastest.
Arguments:
- leaf_cost: float32 [8, 2048, 2048], P('leaf', 'row'), as said below
- a_blocks: float32 [8, 16, 8, 128, 128], P('leaf'), may hold values from -0.046875 to 0.046875
- a_cols: int32 [8, 16, 8], P('leaf'), may hold values from 0 to 15, as said below
- b_blocks: float32 [8, 16, 2, 128, 128], P('leaf'), may hold values from -0.1875 to 0.1875
- b_cols: int32 [8, 16, 2], P('leaf'), may hold values from 0 to 3, as said below
- branch_prob: float32 [8], P('leaf'), may hold values from 0.3 to 0.7
- state_cost: float32 [2048], P('row'), may hold values from 0.5 to 2
- control_cost: float32 [512], replicated, may hold values from 0.5 to 2
- parent_state: float32 [4, 2048, 128], P(None, 'row'), may hold values from -6 to 6
Outputs:
- parent_cost: float32 [8, 2048, 2048], P('leaf', 'row')
- gains: float32 [8, 512, 2048], P('leaf', None, 'row')
- child_state: float32 [8, 2048, 128], P('leaf', 'row')
Inputs may be any that keep to these rules, and one draw needn't show every extreme that they name: a_cols[c, k, 0] equals k, and the 8 entries of one block row are distinct. `b_cols`: the 2 entries of one block row are distinct. Each leaf_cost[c] is symmetric with a diagonal of 2 to 4.
All inputs are finite; a program needn't handle non-finite values.
Results may differ from a plain program's by a relative error of at most 0.0003.
Values sent between devices are 32-bit elements; how exact they have to be, the bound alone decides.
No kernel may reach another device: no remote copies, remote signals or barrier semaphores. Data moves between devices by JAX's collectives and lax.ppermute only.
A program may use at most 256 MiB of HBM per device.

v0:
```python
import functools

import jax
import jax.numpy as jnp
from jax import lax
from jax.experimental import pallas as pl
from jax.experimental.pallas import tpu as pltpu
from jax.sharding import PartitionSpec as P

HIGHEST = lax.Precision.HIGHEST
F32 = jnp.float32
BF16 = jnp.bfloat16
VMEM_LIMIT = 56 * 2**20
NN = (((1,), (0,)), ((), ()))
NT = (((1,), (1,)), ((), ()))


def split(x):
    hi = x.astype(BF16)
    return hi, (x - hi.astype(F32)).astype(BF16)


def parted(x):
    hi = lax.reduce_precision(x, 8, 7)
    return hi.astype(BF16), (x - hi).astype(BF16)


def dot3(a, b, dims=NN):
    one = functools.partial(lax.dot_general, dimension_numbers=dims, preferred_element_type=F32)
    return one(a[0], b[0]) + (one(a[0], b[1]) + one(a[1], b[0]))


def call(kernel, grid, prefetch, ins, outs, shapes, name, scratch=(), aliases=None, after=(), through=()):
    n_in, n_out = len(ins), len(outs)
    extra = len(after) + len(through)
    anywhere = pl.BlockSpec(memory_space=pl.ANY)

    def body(*refs):
        start = prefetch + n_in
        stop = start + extra + n_out
        kernel(*refs[:start], *refs[start + extra : stop], *refs[stop + len(through) :])

    aliases = dict(aliases or {})
    for t in range(len(through)):
        aliases[prefetch + n_in + len(after) + t] = n_out + t
    built = pl.pallas_call(
        body,
        grid_spec=pltpu.PrefetchScalarGridSpec(
            num_scalar_prefetch=prefetch,
            grid=grid,
            in_specs=list(ins) + [anywhere] * extra,
            out_specs=list(outs) + [anywhere] * len(through),
            scratch_shapes=scratch,
        ),
        out_shape=[jax.ShapeDtypeStruct(shape, kind) for shape, kind in shapes]
        + [jax.ShapeDtypeStruct(x.shape, x.dtype) for x in through],
        input_output_aliases=aliases,
        compiler_params=pltpu.CompilerParams(vmem_limit_bytes=VMEM_LIMIT),
        cost_estimate=pl.CostEstimate(flops=1, bytes_accessed=1, transcendentals=0),
        name=name,
    )
    return lambda *args: built(*args, *after, *through)


def whole(*shape):
    return pl.BlockSpec(shape, lambda *_: (0,) * len(shape))


def lower(n):
    return [(i, j) for i in range(n) for j in range(i + 1)]


def dense_kernel(blk, step, nnza, nnzb, width, where, acol, bcol, a_ref, b_ref, p_ref, fh, fl, uh, ul, w_ref, buf):
    i = pl.program_id(0)
    rows = p_ref.shape[0]
    buf[...] = jnp.zeros_like(buf)
    diag = lax.broadcasted_iota(jnp.int32, (blk, blk), 0) == lax.broadcasted_iota(jnp.int32, (blk, blk), 1)
    eye = jnp.where(diag, 0.75, 0.0).astype(F32)
    for t in range(step // blk):
        row = i * (step // blk) + t
        for s in range(nnza):
            col = pl.multiple_of(acol[row * nnza + s] * blk, blk)
            block = a_ref[t, s]
            if s == 0:
                block = block + eye
            buf[t * blk : (t + 1) * blk, pl.ds(col, blk)] = block
        for s in range(nnzb):
            col = pl.multiple_of(width + bcol[row * nnzb + s] * blk, blk)
            buf[t * blk : (t + 1) * blk, pl.ds(col, blk)] = b_ref[t, s]
    hi, lo = split(buf[...])
    fh[...] = hi
    fl[...] = lo
    orders = buf.shape[1] - width
    uh[:orders], ul[:orders] = split(buf[:, width:].T)
    uh[orders:], ul[orders:] = split(buf[:, pl.ds(pl.multiple_of(where[0] * rows, rows), rows)].T)
    part = dot3(split(p_ref[...]), (hi[:, width:], lo[:, width:]))

    @pl.when(i == 0)
    def _():
        w_ref[...] = part

    @pl.when(i > 0)
    def _():
        w_ref[...] += part


def dense(where, cost_rows, a_blocks, a_cols, b_blocks, b_cols, orders, after):
    rows, width = cost_rows.shape
    _, nnza, blk, _ = a_blocks.shape
    nnzb = b_blocks.shape[1]
    step = 2 * blk
    total = width + orders
    factor = pl.BlockSpec((step, total), lambda i, *_: (i, 0))
    turned = pl.BlockSpec((rows + orders, step), lambda i, *_: (0, i))
    return call(
        functools.partial(dense_kernel, blk, step, nnza, nnzb, width),
        (width // step,),
        3,
        [
            pl.BlockSpec((2, nnza, blk, blk), lambda i, *_: (i, 0, 0, 0)),
            pl.BlockSpec((2, nnzb, blk, blk), lambda i, *_: (i, 0, 0, 0)),
            pl.BlockSpec((rows, step), lambda i, *_: (0, i)),
        ],
        [factor, factor, turned, turned, whole(rows, orders)],
        [((width, total), BF16)] * 2 + [((rows + orders, width), BF16)] * 2 + [((rows, orders), F32)],
        "dense",
        [pltpu.VMEM((step, total), F32)],
        after=after,
    )(where, a_cols.reshape(-1), b_cols.reshape(-1), a_blocks, b_blocks, cost_rows)


def gram_kernel(blk, pieces, weight, where, bh, bl, ah, al, w_ref, own, *refs):
    keep, give, drift, x = refs[pieces - 1 :]
    rows = own.shape[0]
    z, core = where[0], where[1]
    x[pl.ds(pl.multiple_of(z * rows, rows), rows)] = own[...]
    for d in range(1, pieces):
        base = lax.rem(z - d + pieces, pieces) * rows
        x[pl.ds(pl.multiple_of(base, rows), rows)] = refs[d - 1][...]
    w = w_ref[...]
    h = dot3((bh[...], bl[...]), split(w)) * weight[0]
    y = dot3((ah[...], al[...]), split(x[...]))
    drift[...] = y
    q = dot3(split(w.T), split(y)) * weight[0]
    tiles = [h[i * blk : (i + 1) * blk, j * blk : (j + 1) * blk] for i, j in lower(h.shape[0] // blk)]
    tiles += [q[i * blk : (i + 1) * blk] for i in range(h.shape[0] // blk)]
    count = len(tiles) // 2
    for side in range(2):

        @pl.when(core == side)
        def _():
            for t in range(count):
                keep[t] = tiles[side * count + t]
                give[t] = tiles[(1 - side) * count + t]


def gram(weight, where, fh, fl, uh, ul, w, own, other, blk):
    rows, orders = w.shape
    samples = own.shape[1]
    pieces = len(other) + 1
    width = rows * pieces
    count = orders // blk
    count = (count * (count + 1) // 2 + count) // 2
    turned = pl.BlockSpec((orders, rows), lambda i, weight, where: (0, where[0]))
    factor = pl.BlockSpec((rows, width), lambda i, weight, where: (where[0], 0))
    return call(
        functools.partial(gram_kernel, blk, pieces),
        (1,),
        2,
        [turned, turned, factor, factor, whole(rows, orders)] + [whole(rows, samples)] * pieces,
        [whole(count, blk, samples)] * 2 + [whole(rows, samples)],
        [((count, blk, samples), F32)] * 2 + [((rows, samples), F32)],
        "gram",
        [pltpu.VMEM((width, samples), F32)],
    )(weight, where, uh, ul, fh, fl, w, own, *other)


def inverse_block(m):
    n = m.shape[0]
    sub = lax.broadcasted_iota(jnp.int32, (8, n), 0)
    lane = lax.broadcasted_iota(jnp.int32, (8, n), 1)
    strips = [m[i : i + 8] for i in range(0, n, 8)]

    def along(v, j):
        return jnp.broadcast_to(v[:, j : j + 1], (8, n))

    def down(v, t):
        return jnp.broadcast_to(v[t : t + 1], (8, n))

    for q in range(n // 8):
        panel = strips[q]
        cols = [along(panel, 8 * q + b) for b in range(8)]
        for t in range(8):
            here = sub == t
            inv = 1.0 / down(cols[t], t)

            def reduced(v):
                r = down(v, t) * inv
                return jnp.where(here, r, v - cols[t] * r)

            panel = reduced(jnp.where(lane == 8 * q + t, jnp.where(here, 1.0, 0.0), panel))
            cols[t + 1 :] = [reduced(v) for v in cols[t + 1 :]]
        inside = (lane >= 8 * q) & (lane < 8 * q + 8)
        rows = [down(panel, b) for b in range(8)]
        for i in range(q + 1, q + n // 8):
            old = strips[i % (n // 8)]
            terms = [along(old, 8 * q + b) * rows[b] for b in range(8)]
            while len(terms) > 1:
                terms = [x + y for x, y in zip(terms[::2], terms[1::2])]
            strips[i % (n // 8)] = jnp.where(inside, 0.0, old) - terms[0]
        strips[q] = panel
    return jnp.concatenate(strips, axis=0)


def inverse_kernel(where, mine, other, d_ref, out, u_ref, tiles):
    core = where[0]
    half, blk, _ = mine.shape
    n = out.shape[0]
    tiles[pl.ds(core * half, half)] = mine[...]
    tiles[pl.ds((1 - core) * half, half)] = other[...]
    dot = functools.partial(jnp.dot, precision=HIGHEST, preferred_element_type=F32)
    pairs = lower(n // blk)
    for t, (i, j) in enumerate(pairs):
        out[i * blk : (i + 1) * blk, j * blk : (j + 1) * blk] = tiles[t]
        if i != j:
            out[j * blk : (j + 1) * blk, i * blk : (i + 1) * blk] = tiles[t].T
    diag = lax.broadcasted_iota(jnp.int32, (n, n), 0) == lax.broadcasted_iota(jnp.int32, (n, n), 1)
    out[...] += jnp.where(diag, d_ref[...], 0.0)

    @pl.loop(0, n // blk)
    def _(b):
        here = pl.ds(pl.multiple_of(b * blk, blk), blk)
        inv = inverse_block(out[here, here])
        row = dot(inv, out[here, :])
        col = out[:, here]
        out[...] -= dot(col, row)
        out[:, here] = -dot(col, inv)
        out[here, :] = row
        out[here, here] = inv

    q = jnp.concatenate([tiles[len(pairs) + i] for i in range(n // blk)], axis=0)
    u_ref[...] = -dot(out[...], q)


def inverse(where, mine, other, control_cost, after):
    half, blk, samples = mine.shape
    n = control_cost.shape[0]
    return call(
        inverse_kernel,
        (1,),
        1,
        [whole(half, blk, samples)] * 2 + [whole(1, n)],
        [whole(n, n), whole(n, samples)],
        [((n, n), F32), ((n, samples), F32)],
        "inverse",
        [pltpu.VMEM((2 * half, blk, samples), F32)],
        after=after,
    )(where, mine, other, control_cost[None])


def tiled(block, blk):
    n = block.shape[0] // blk
    return [block[i * blk : (i + 1) * blk, j * blk : (j + 1) * blk] for i in range(n) for j in range(n)]


def pack_kernel(blk, where, own, near, inner, far, diag_out, pair_out, mid_out):
    for t, (i, j) in enumerate(lower(own.shape[0] // blk)):
        tile = own[i * blk : (i + 1) * blk, j * blk : (j + 1) * blk]
        diag_out[t] = tile
        mid_out[t] = tile
    count = diag_out.shape[0]
    for t, tile in enumerate(tiled(near, blk)):
        mid_out[count + t] = tile
    for t, tile in enumerate(tiled(inner, blk) + tiled(far, blk)):
        pair_out[t] = tile


def pack(where, cost_rows, blk):
    rows = cost_rows.shape[0]
    count, full = len(lower(rows // blk)), (rows // blk) ** 2
    specs = [pl.BlockSpec((rows, rows), functools.partial(lambda t, i, where: (0, where[t]), t)) for t in range(4)]
    sizes = [count, 2 * full, count + full]
    return call(
        functools.partial(pack_kernel, blk),
        (1,),
        1,
        specs,
        [whole(size, blk, blk) for size in sizes],
        [((size, blk, blk), F32) for size in sizes],
        "pack",
    )(where, *[cost_rows] * 4)


def unpack(tiles, step, n, xh, xl):
    blk = tiles.shape[1]
    for t, (i, j) in enumerate(lower(n) if step == 0 else [(i, j) for i in range(n) for j in range(n)]):
        tile = tiles[t if step == 0 else len(lower(n)) + (step - 1) * n * n + t]
        places = [(i, j, tile)] + ([(j, i, tile.T)] if step == 0 and i != j else [])
        for r, c, value in places:
            at = slice(r * blk, (r + 1) * blk), slice(c * blk, (c + 1) * blk)
            xh[at], xl[at] = split(value)


def begin_kernel(where, p_ref, uh, ul, vh, vl, mine, rest):
    j = pl.program_id(0)
    p = split(p_ref[...])
    part = dot3((uh[...], ul[...]), p, NT)

    @pl.when(j == 0)
    def _():
        mine[...] = part

    @pl.when(j > 0)
    def _():
        mine[...] += part

    rest[...] = dot3((vh[...], vl[...]), p)


def begin(where, cost_rows, uh, ul, after, through):
    rows, width = cost_rows.shape
    tall = uh.shape[0]
    each = pl.BlockSpec((tall, rows), lambda j, where: (0, j))
    own = pl.BlockSpec((tall, rows), lambda j, where: (0, where[0]))
    return call(
        begin_kernel,
        (width // rows,),
        1,
        [pl.BlockSpec((rows, rows), lambda j, where: (0, j)), each, each, own, own],
        [whole(tall, rows), each],
        [((tall, rows), F32), ((tall, width), F32)],
        "begin",
        after=after,
        through=through,
    )(where, cost_rows, uh, ul, uh, ul)


def spread_kernel(where, weight, n_ref, fh, fl, s_out, g_out, hi, lo):
    @pl.when(pl.program_id(0) == 0)
    def _():
        hi[...], lo[...] = split(n_ref[...] * weight[0])

    part = dot3((hi[...], lo[...]), (fh[...], fl[...]))
    orders = g_out.shape[0]
    s_out[...] = part[orders:]
    g_out[...] = part[:orders]


def spread(where, weight, n, fh, fl, width, after, through):
    tall, rows = n.shape
    orders = tall - rows
    tile = 512
    s_spec = pl.BlockSpec((rows, tile), lambda n, *_: (0, n))
    g_spec = pl.BlockSpec((orders, tile), lambda n, *_: (0, n))
    factor = pl.BlockSpec((rows, tile), lambda n, where, _: (where[0], n))
    return call(
        spread_kernel,
        (width // tile,),
        2,
        [whole(tall, rows), factor, factor],
        [s_spec, g_spec],
        [((rows, width), F32), ((orders, width), F32)],
        "spread",
        [pltpu.VMEM((tall, rows), BF16)] * 2,
        after=after,
        through=through,
    )(where, weight, n, fh, fl)


def stage_kernel(sources, options, size, where, weight, *refs):
    arrived = refs[: sources * options]
    vh, vl, n_in, fh, fl, s_in, g_in, *refs = refs[sources * options :]
    if size > 1:
        uh, ul, s_out, g_out, n_out, done, hi, lo, xh, xl = refs
    else:
        s_out, g_out, done, hi, lo, xh, xl = refs
    g = pl.program_id(0)
    n = xh.shape[0] // arrived[0].shape[1]
    for c in range(options):
        for t in range(size):

            @pl.when((g == t) & (where[0] == c))
            def _():
                if sources == 2 and t > 0:
                    rest = arrived[2 * c + 1]
                    for k in range(n * n):
                        at = slice(k // n * rest.shape[1], (k // n + 1) * rest.shape[1])
                        to = slice(k % n * rest.shape[2], (k % n + 1) * rest.shape[2])
                        xh[at, to], xl[at, to] = split(rest[(t - 1) * n * n + k])
                else:
                    unpack(arrived[sources * c], t, n, xh, xl)

    @pl.when(g == 0)
    def _():
        done[...] = n_in[...] + dot3((vh[...], vl[...]), (xh[...], xl[...]))

    if size > 1:

        @pl.when((g > 0) & (g < size))
        def _():
            x = xh[...], xl[...]
            done[...] += dot3((uh[...], ul[...]), x, NT)
            n_out[...] = n_in[...] + dot3((vh[...], vl[...]), x)

    @pl.when(g == size)
    def _():
        hi[...], lo[...] = split(done[...] * weight[0])

    @pl.when(g >= size)
    def _():
        part = dot3((hi[...], lo[...]), (fh[...], fl[...]))
        orders = g_out.shape[0]
        s_out[...] = s_in[...] + part[orders:]
        g_out[...] = g_in[...] + part[:orders]


def stage(where, weight, options, size, uh, ul, n, fh, fl, sums, after=(), through=()):
    tall, width = n.shape
    rows, orders = sums[0].shape[0], sums[1].shape[0]
    sources = len(options[0])
    tile = 512

    def place(g, where):
        return where[1 + jnp.minimum(g, size - 1)]

    def later(g, where):
        return where[1 + jnp.clip(g, 1, size - 1)]

    def turn(g):
        return jnp.maximum(g - size, 0)

    block = pl.BlockSpec((tall, rows), lambda g, where, _: (0, place(g, where)))
    beyond = pl.BlockSpec((tall, rows), lambda g, where, _: (0, later(g, where)))
    focus = pl.BlockSpec((tall, rows), lambda g, where, _: (0, where[1]))
    factor = pl.BlockSpec((rows, tile), lambda g, where, _: (where[1], turn(g)))
    s_spec = pl.BlockSpec((rows, tile), lambda g, *_: (0, turn(g)))
    g_spec = pl.BlockSpec((orders, tile), lambda g, *_: (0, turn(g)))
    arrived = [x for o in options for x in o]
    first = 2 + len(arrived)
    more = size > 1
    return call(
        functools.partial(stage_kernel, sources, len(options), size),
        (size + width // tile,),
        2,
        [whole(*x.shape) for x in arrived]
        + [focus, focus, block, factor, factor, s_spec, g_spec]
        + [beyond] * (2 * more),
        [s_spec, g_spec] + [beyond] * more,
        [((rows, width), F32), ((orders, width), F32)] + [((tall, width), F32)] * more,
        "stage",
        [pltpu.VMEM((tall, rows), F32)] + [pltpu.VMEM((tall, rows), BF16)] * 2 + [pltpu.VMEM((rows, rows), BF16)] * 2,
        {first + 5: 0, first + 6: 1, **({first + 2: 2} if more else {})},
        after,
        through,
    )(where, weight, *arrived, uh, ul, n, fh, fl, *sums, *([uh, ul] if more else []))


def final_kernel(where, h_ref, g1, g2, s1, s2, q1, q2, d_ref, gain, out, hi, lo):
    n = pl.program_id(0)
    rows = out.shape[0]

    @pl.when(n == 0)
    def _():
        value = -dot3(split(h_ref[...]), split(g1[...] + g2[...]))
        gain[...] = value
        hi[...], lo[...] = split(value.T)

    part = s1[...] + s2[...] + dot3((hi[...], lo[...]), split(q1[...] + q2[...]))
    diag = lax.broadcasted_iota(jnp.int32, (rows, rows), 0) == lax.broadcasted_iota(jnp.int32, (rows, rows), 1)
    out[...] = part + jnp.where(diag & (n == where[0]), d_ref[...], 0.0)


def final(where, hinv, own, other, state_cost):
    rows, width = own[0].shape
    orders = own[1].shape[0]
    s_spec = pl.BlockSpec((rows, rows), lambda n, where: (0, n))
    g_spec = pl.BlockSpec((orders, rows), lambda n, where: (0, n))
    mine = pl.BlockSpec((orders, rows), lambda n, where: (0, where[0]))
    return call(
        final_kernel,
        (width // rows,),
        1,
        [whole(orders, orders), mine, mine, s_spec, s_spec, g_spec, g_spec, whole(1, rows)],
        [whole(orders, rows), s_spec],
        [((orders, rows), F32), ((rows, width), F32)],
        "final",
        [pltpu.VMEM((rows, orders), BF16)] * 2,
    )(where, hinv, own[1], other[1], own[0], other[0], own[1], other[1], state_cost[None])


def image_kernel(where, weight, fh, fl, p_ref, out, acc):
    k = pl.program_id(0)
    part = dot3(split(p_ref[...]), (fh[...], fl[...]))

    @pl.when(k == 0)
    def _():
        acc[...] = part

    @pl.when(k > 0)
    def _():
        acc[...] += part

    @pl.when(k == pl.num_programs(0) - 1)
    def _():
        out[...] = acc[...].T * weight[0]


def image(where, weight, fh, fl, cost_rows):
    rows, width = cost_rows.shape
    chunk = 512
    factor = pl.BlockSpec((chunk, rows), lambda k, where, _: (k, where[0]))
    return call(
        image_kernel,
        (width // chunk,),
        2,
        [factor, factor, pl.BlockSpec((rows, chunk), lambda k, *_: (0, k))],
        [whole(rows, rows)],
        [((rows, rows), F32)],
        "image",
        [pltpu.VMEM((rows, rows), F32)],
    )(where, weight, fh, fl, cost_rows)[0]


def accumulate_kernel(first, where, y_ref, fh, fl, *refs):
    out = refs[-1]
    part = dot3(split(y_ref[...]), (fh[...], fl[...]))
    out[...] = part if first else refs[0][...] + part


def accumulate(where, y, fh, fl, acc):
    rows = y.shape[0]
    total = fh.shape[1]
    tile = 512
    first = acc is None
    spec = pl.BlockSpec((rows, tile), lambda n, where: (0, n))
    factor = pl.BlockSpec((rows, tile), lambda n, where: (where[0], n))
    return call(
        functools.partial(accumulate_kernel, first),
        (total // tile,),
        1,
        [whole(rows, rows), factor, factor] + [spec] * (not first),
        [spec],
        [((rows, total), F32)],
        "accumulate",
        aliases=None if first else {4: 0},
    )(where, y, fh, fl, *(() if first else (acc,)))[0]


def by_images(z, parts, weight, cost_rows, fh, fl):
    rows, width = cost_rows.shape
    acc = None
    for d in range(parts):
        block = image(((z + d) % parts)[None], weight, fh, fl, cost_rows)
        if d:
            block = lax.ppermute(block, "row", [(i, (i + d) % parts) for i in range(parts)])
        acc = accumulate(((z - d) % parts)[None], block, fh, fl, acc)
    cross = lax.all_gather(acc[:, width:], "row")
    return acc[:, :width], jnp.swapaxes(cross.reshape(width, -1), 0, 1)


def by_blocks(z, weight, cost_rows, fh, fl, uh, ul, sent, tiles):
    width = cost_rows.shape[1]
    edge = ((z == 0) | (z == 3)).astype(jnp.int32)
    left = z < 2

    def at(i):
        return jnp.where(left, i, 3 - i)

    def moved(x, pairs):
        return lax.ppermute(x, "row", pairs)

    def to_partner(x):
        return moved(x, [(0, 1), (1, 0), (2, 3), (3, 2)])

    def across(x):
        return moved(x, [(1, 2), (2, 1)])

    def to_end(x):
        return moved(x, [(1, 0), (2, 3)])

    diag, pair, inward = sent
    diag, pair, mid = to_partner(diag), to_partner(pair), across(inward)
    tiles = tiles[0] + swapped(tiles[1])
    mine, n = begin(z[None], cost_rows, uh, ul, [tiles], [])
    tiles = tiles + to_partner(tiles)
    *sums, diag, mid = spread(z[None], weight, mine, fh, fl, width, [tiles], [diag, mid])
    mid_last, end = across(diag), to_end(mid)
    tiles = tiles + moved(tiles, [(0, 3), (1, 2), (2, 1), (3, 0)])
    where = jnp.stack([z * 0, z ^ 1, at(2), at(3)])
    *sums, n, mid_last = stage(
        where, weight, [[diag, pair]], 3, uh, ul, n, fh, fl, sums, [tiles], [mid_last]
    )
    end_last = to_end(mid_last)

    def rest(hinv):
        where = jnp.stack([edge, at(2), at(3)])
        *more, whole_n = stage(where, weight, [[mid], [end]], 2, uh, ul, n, fh, fl, sums, [hinv])
        where = jnp.stack([edge, at(3)])
        return stage(where, weight, [[mid_last], [end_last]], 1, uh, ul, whole_n, fh, fl, more)

    return tiles, sums[0], rest


def swapped(x):
    n = lax.axis_size("leaf")
    return lax.ppermute(x, "leaf", [(i, i ^ 1) for i in range(n)])


def shards(
    leaf_cost,
    a_blocks,
    a_cols,
    b_blocks,
    b_cols,
    branch_prob,
    state_cost,
    control_cost,
    parent_state,
):
    cost_rows = leaf_cost[0]
    rows, width = cost_rows.shape
    blk = a_blocks.shape[3]
    orders = control_cost.shape[0]
    parts = lax.axis_size("row")
    z = lax.axis_index("row")
    leaf = lax.axis_index("leaf")
    core = leaf % 2
    line = parts == 4 and rows == orders

    place = jnp.stack([z, core])
    sent = []
    if line:
        left = z < 2
        near = jnp.where(left, 0, 3)
        sent = pack(jnp.stack([z, near, jnp.where(left, 2, 1), 3 - near]), cost_rows, blk)

    own_state = lax.dynamic_index_in_dim(parent_state, leaf // 2, 0, keepdims=False)
    other = [lax.ppermute(own_state, "row", [(i, (i + d) % parts) for i in range(parts)]) for d in range(1, parts)]

    fh, fl, uh, ul, w = dense(z[None], cost_rows, a_blocks[0], a_cols[0], b_blocks[0], b_cols[0], orders, sent)
    *tiles, drift = gram(branch_prob, place, fh, fl, uh, ul, w, own_state, other, blk)
    if line:
        tiles, ready, rest = by_blocks(z, branch_prob, cost_rows, fh, fl, uh, ul, sent, tiles)
    else:
        tiles = lax.psum(tiles[0] + swapped(tiles[1]), "row")
        own = by_images(z, parts, branch_prob, cost_rows, fh, fl)
        ready, rest = own[0], lambda hinv: own
    hinv, order = inverse(core[None], tiles, swapped(tiles), control_cost, [ready])
    own = rest(hinv)
    other = tuple(swapped(x) for x in own)
    b_mine = [lax.dynamic_slice(f, (z * rows, width), (rows, orders)) for f in (fh, fl)]
    reached = drift + dot3(b_mine, parted(order))
    gain, pcost = final(z[None], hinv, own, other, state_cost)
    return pcost[None], gain[None], reached[None]


def solution(mesh):
    placed = (
        P("leaf", "row", None),
        P("leaf", None, None, None, None),
        P("leaf", None, None),
        P("leaf", None, None, None, None),
        P("leaf", None, None),
        P("leaf"),
        P("row"),
        P(),
        P(None, "row", None),
    )
    return jax.shard_map(
        shards,
        mesh=mesh,
        in_specs=placed,
        out_specs=(P("leaf", "row", None), P("leaf", None, "row"), P("leaf", "row", None)),
        check_vma=False,
    )
```

profile of v0, /device:TPU:21, one launch (start us, length us, event | category | flops | bytes accessed | tf_op | source)
XLA Modules:
  0.0 285.1 jit_solution(14731487041336289737)
XLA Ops:
  1.3 5.3 %pack.1 = (f32[10,128,128]{2,1,0:T(8,128)}, f32[32,128,128]{2,1,0:T(8,128)}, f32[26,128,128]{2,1,0:T(8,128)}) custom-call(s32[4]{0:T(128)} %pad_add_fusion.1.refs_0_, f32[512,2048]{1,0:T(8,128)} %bitcast.19, f32[512,2048]{1,0:T(8,128)} %bitcast.20, f32[512,2048]{1,0:T(8,128)} %bitcast.21, f32[512,2048]{1,0:T(8,128)} %bitcast.22), custom_call_target="tpu_custom_call" | custom-call | flops 1 | bytes 1 | tf_op jit(solution)/shard_map/pack/pallas_call | solution.py:62
  6.5 2.1 collective-permute-start.8
  8.7 2.5 collective-permute-start.1
  14.1 20.7 %dense.1 = (bf16[2048,2560]{1,0:T(8,128)(2,1)}, bf16[2048,2560]{1,0:T(8,128)(2,1)}, bf16[1024,2048]{1,0:T(8,128)(2,1)}, bf16[1024,2048]{1,0:T(8,128)(2,1)}, f32[512,512]{1,0:T(8,128)}) custom-call(s32[1]{0:T(128)} %bitcast.refs_0_, s32[128]{0:T(128)} %reshape_squeeze.6.refs_1_, s32[32]{0:T(128)} %reshape_squeeze.7.refs_2_, f32[16,8,128,128]{3,2,1,0:T(8,128)} %bitcast.25, ...), custom_call_target="tpu_custom_call" | custom-call | flops 1 | bytes 1 | tf_op jit(solution)/shard_map/dense/pallas_call | solution.py:62
  36.1 27.6 %collective-permute-done.refs_8_ = f32[512,128]{1,0:T(8,128)S(1)} collective-permute-done((f32[512,128]{1,0:T(8,128)S(1)}, f32[512,128]{1,0:T(8,128)S(1)}, u32[]{:S(2)}, u32[]{:S(2)}) %collective-permute-start) | collective-permute-done | bytes 262176 | tf_op jit(solution)/shard_map/ppermute | solution.py:638
  63.7 4.3 %collective-permute-done.2.refs_10_ = f32[512,128]{1,0:T(8,128)S(1)} collective-permute-done((f32[512,128]{1,0:T(8,128)S(1)}, f32[512,128]{1,0:T(8,128)S(1)}, u32[]{:S(2)}, u32[]{:S(2)}) %collective-permute-start.2) | collective-permute-done | bytes 262176 | tf_op jit(solution)/shard_map/ppermute | solution.py:638
  68.7 8.9 %gram.1 = (f32[7,128,128]{2,1,0:T(8,128)}, f32[7,128,128]{2,1,0:T(8,128)}, f32[512,128]{1,0:T(8,128)}) custom-call(f32[1]{0:T(128)S(6)} %copy.38.refs_0_.refs_1_, s32[2]{0:T(128)} %pad_add_fusion.refs_1_, bf16[1024,2048]{1,0:T(8,128)(2,1)} %get-tuple-element.36.refs_2_.refs_4_.refs_11_, bf16[1024,2048]{1,0:T(8,128)(2,1)} %get-tuple-element.37.refs_3_.refs_5_.refs_12_, ...), custom_call_target="tpu_custom_call" | custom-call | flops 1 | bytes 1 | tf_op jit(solution)/shard_map/gram/pallas_call | solution.py:62
  78.1 3.7 %collective-permute-start.7 = (f32[10,128,128]{2,1,0:T(8,128)S(1)}, f32[10,128,128]{2,1,0:T(8,128)S(1)}, u32[]{:S(2)}, u32[]{:S(2)}) collective-permute-start(f32[10,128,128]{2,1,0:T(8,128)S(1)} %copy-done.10), channel_id=1, source_target_pairs={{0,1},{1,0},{2,3},{3,2},{4,5},{5,4},{6,7},{7,6},{8,9},{9,8},{10,11... | collective-permute-start | bytes 1966088 | tf_op jit(solution)/shard_map/ppermute | solution.py:570
  82.8 1.7 collective-permute-start.4
  84.5 19.5 %begin.1 = (f32[1024,512]{1,0:T(8,128)}, f32[1024,2048]{1,0:T(8,128)}) custom-call(s32[1]{0:T(128)} %bitcast.refs_0_, f32[512,2048]{1,0:T(8,128)} %bitcast.24, bf16[1024,2048]{1,0:T(8,128)(2,1)} %get-tuple-element.36.refs_2_.refs_4_.refs_11_, bf16[1024,2048]{1,0:T(8,128)(2,1)} %get-tuple-element.37.refs_3_.refs_5_.refs_12_, ...), custom_call_target="tpu_custom_call" | custom-call | flops 1 | bytes 1 | tf_op jit(solution)/shard_map/begin/pallas_call | solution.py:62
  104.0 2.6 collective-permute-done.4
  106.6 1.8 add.34.refs_5_
  109.9 10.9 %spread.1 = (f32[512,2048]{1,0:T(8,128)}, f32[512,2048]{1,0:T(8,128)}, f32[10,128,128]{2,1,0:T(8,128)}, f32[26,128,128]{2,1,0:T(8,128)}) custom-call(s32[1]{0:T(128)} %bitcast.refs_0_, f32[1]{0:T(128)S(6)} %copy.38.refs_0_.refs_1_, f32[1024,512]{1,0:T(8,128)} %get-tuple-element.43.refs_2_, ...), custom_call_target="tpu_custom_call", output_to_operand_aliasing={{2}: (6, {}), {3}: (7, {})} | custom-call | flops 1 | bytes 1 | tf_op jit(solution)/shard_map/spread/pallas_call | solution.py:62
  120.8 4.4 %collective-permute-start.12 = (f32[26,128,128]{2,1,0:T(8,128)}, f32[26,128,128]{2,1,0:T(8,128)}, u32[]{:S(2)}, u32[]{:S(2)}) collective-permute-start(f32[26,128,128]{2,1,0:T(8,128)} %get-tuple-element.51.refs_2_), channel_id=1, source_target_pairs={{1,0},{2,3},{5,4},{6,7},{9,8},{10,11},{13,12},{14,15},{17,16},{18,... | collective-permute-start | bytes 5111816 | tf_op jit(solution)/shard_map/ppermute | solution.py:570
  125.1 2.1 collective-permute-start.10
  127.3 1.5 collective-permute-start.5
  129.4 31.8 %collective-permute-done.5 = f32[7,128,128]{2,1,0:T(8,128)S(1)} collective-permute-done((f32[7,128,128]{2,1,0:T(8,128)S(1)}, f32[7,128,128]{2,1,0:T(8,128)S(1)}, u32[]{:S(2)}, u32[]{:S(2)}) %collective-permute-start.5) | collective-permute-done | bytes 458784 | tf_op jit(solution)/shard_map/ppermute | solution.py:570
  162.9 26.0 %stage.3 = (f32[512,2048]{1,0:T(8,128)}, f32[512,2048]{1,0:T(8,128)}, f32[1024,2048]{1,0:T(8,128)}, f32[10,128,128]{2,1,0:T(8,128)}) custom-call(s32[4]{0:T(128)} %pad_add_fusion.2.refs_0_, f32[1]{0:T(128)S(6)} %copy.38.refs_0_.refs_1_, ...), custom_call_target="tpu_custom_call", output_to_operand_aliasing={{0}: (9, {}), {1}: (10, {}), {2}: (6, {}), {3}: (14, {})} | custom-call | flops 1 | bytes 1 | tf_op jit(solution)/shard_map/stage/pallas_call | solution.py:62
  193.0 26.3 %inverse.1 = (f32[512,512]{1,0:T(8,128)}, f32[512,128]{1,0:T(8,128)}) custom-call(s32[1]{0:T(128)} %bitcast.1.refs_0_, f32[7,128,128]{2,1,0:T(8,128)} %add.35.refs_13_.refs_1_, f32[7,128,128]{2,1,0:T(8,128)} %copy-done.12, f32[1,512]{1,0:T(1,128)} %bitcast.27, f32[512,2048]{1,0:T(8,128)} %get-tuple-element.48.refs_4_.refs_9_), custom_call_target="tpu_custom_call" | custom-call | flops 1 | bytes 1 | tf_op jit(solution)/shard_map/inverse/pallas_call | solution.py:62
  219.3 22.3 %stage.4 = (f32[512,2048]{1,0:T(8,128)}, f32[512,2048]{1,0:T(8,128)}, f32[1024,2048]{1,0:T(8,128)}) custom-call(s32[3]{0:T(128)} %pad_add_fusion.4.refs_0_, f32[1]{0:T(128)S(6)} %copy.38.refs_0_.refs_1_, f32[26,128,128]{2,1,0:T(8,128)} %get-tuple-element.51.refs_2_, ...), custom_call_target="tpu_custom_call", output_to_operand_aliasing={{0}: (9, {}), {1}: (10, {}), {2}: (6, {})} | custom-call | flops 1 | bytes 1 | tf_op jit(solution)/shard_map/stage/pallas_call | solution.py:62
  242.4 16.8 %stage.5 = (f32[512,2048]{1,0:T(8,128)}, f32[512,2048]{1,0:T(8,128)}) custom-call(s32[2]{0:T(128)} %pad_add_fusion.3.refs_0_, f32[1]{0:T(128)S(6)} %copy.38.refs_0_.refs_1_, f32[10,128,128]{2,1,0:T(8,128)} %get-tuple-element.50.refs_2_, f32[10,128,128]{2,1,0:T(8,128)} %copy-done.11, ...), custom_call_target="tpu_custom_call", output_to_operand_aliasing={{0}: (9, {}), {1}: (10, {})} | custom-call | flops 1 | bytes 1 | tf_op jit(solution)/shard_map/stage/pallas_call | solution.py:62
  264.5 2.2 collective-permute-done.13.refs_3_.refs_7_
  266.7 6.0 %collective-permute-done.14.refs_5_ = f32[512,2048]{1,0:T(8,128)} collective-permute-done((f32[512,2048]{1,0:T(8,128)}, f32[512,2048]{1,0:T(8,128)}, u32[]{:S(2)}, u32[]{:S(2)}) %collective-permute-start.14) | collective-permute-done | bytes 4194336 | tf_op jit(solution)/shard_map/ppermute | solution.py:606
  272.7 12.1 %final.1 = (f32[512,512]{1,0:T(8,128)}, f32[512,2048]{1,0:T(8,128)}) custom-call(s32[1]{0:T(128)} %bitcast.refs_0_, f32[512,512]{1,0:T(8,128)} %get-tuple-element.49.refs_13_.refs_1_, f32[512,2048]{1,0:T(8,128)} %get-tuple-element.57.refs_2_.refs_6_, f32[512,2048]{1,0:T(8,128)} %collective-permute-done.13.refs_3_.refs_7_, ...), custom_call_target="tpu_custom_call" | custom-call | flops 1 | bytes 1 | tf_op jit(solution)/shard_map/final/pallas_call | solution.py:62
  (71 shorter events, 20.4 us)
Async XLA Ops:
  1.2 11.4 %copy-start.17 = (s32[1,16,8]{1,2,0:T(8,128)S(1)}, s32[1,16,8]{1,2,0:T(8,128)}, u32[]{:S(2)}) copy-start(s32[1,16,8]{1,2,0:T(8,128)} %param.11) | copy-start | bytes 1540
  1.3 12.2 %copy-start.18 = (s32[1,16,2]{1,2,0:T(2,128)S(1)}, s32[1,16,2]{1,2,0:T(2,128)}, u32[]{:S(2)}) copy-start(s32[1,16,2]{1,2,0:T(2,128)} %param.13) | copy-start | bytes 388
  6.5 101.9 %collective-permute-start.8 = (f32[26,128,128]{2,1,0:T(8,128)}, f32[26,128,128]{2,1,0:T(8,128)S(1)}, u32[]{:S(2)}, u32[]{:S(2)}) collective-permute-start(f32[26,128,128]{2,1,0:T(8,128)} %get-tuple-element.35.refs_8_), channel_id=1, source_target_pairs={{1,2},{2,1},{5,6},{6,5},{9,10},{10,9},{13,14},{14,13},{17,18},{18,... | collective-permute-start | bytes 5111816 | tf_op jit(solution)/shard_map/ppermute | solution.py:570
  8.7 26.1 %copy-start.9 = (f32[512,128]{1,0:T(8,128)}, f32[512,128]{1,0:T(8,128)S(1)}, u32[]{:S(2)}) copy-start(f32[512,128]{1,0:T(8,128)S(1)} %dynamic-slice_bitcast_fusion.refs_7_) | copy-start | bytes 786436
  8.7 55.0 %collective-permute-start = (f32[512,128]{1,0:T(8,128)S(1)}, f32[512,128]{1,0:T(8,128)S(1)}, u32[]{:S(2)}, u32[]{:S(2)}) collective-permute-start(f32[512,128]{1,0:T(8,128)S(1)} %dynamic-slice_bitcast_fusion.refs_7_), channel_id=1, source_target_pairs={{0,1},{1,2},{2,3},{3,0},{4,5},{5,6},{6,7},{7,4},{8,9},{9,10},{10,1... | collective-permute-start | bytes 786440 | tf_op jit(solution)/shard_map/ppermute | solution.py:638
  8.7 54.9 %collective-permute-start.1 = (f32[512,128]{1,0:T(8,128)S(1)}, f32[512,128]{1,0:T(8,128)S(1)}, u32[]{:S(2)}, u32[]{:S(2)}) collective-permute-start(f32[512,128]{1,0:T(8,128)S(1)} %dynamic-slice_bitcast_fusion.refs_7_), channel_id=1, source_target_pairs={{0,2},{1,3},{2,0},{3,1},{4,6},{5,7},{6,4},{7,5},{8,10},{9,11},{10,... | collective-permute-start | bytes 786440 | tf_op jit(solution)/shard_map/ppermute | solution.py:638
  11.2 56.8 %collective-permute-start.2 = (f32[512,128]{1,0:T(8,128)S(1)}, f32[512,128]{1,0:T(8,128)S(1)}, u32[]{:S(2)}, u32[]{:S(2)}) collective-permute-start(f32[512,128]{1,0:T(8,128)S(1)} %dynamic-slice_bitcast_fusion.refs_7_), channel_id=1, source_target_pairs={{0,3},{1,0},{2,1},{3,2},{4,7},{5,4},{6,5},{7,6},{8,11},{9,8},{10,9... | collective-permute-start | bytes 786440 | tf_op jit(solution)/shard_map/ppermute | solution.py:638
  11.2 150.9 %collective-permute-start.9 = (f32[32,128,128]{2,1,0:T(8,128)}, f32[32,128,128]{2,1,0:T(8,128)}, u32[]{:S(2)}, u32[]{:S(2)}) collective-permute-start(f32[32,128,128]{2,1,0:T(8,128)} %get-tuple-element.34.refs_7_), channel_id=1, source_target_pairs={{0,1},{1,0},{2,3},{3,2},{4,5},{5,4},{6,7},{7,6},{8,9},{9,8},{10,11... | collective-permute-start | bytes 6291464 | tf_op jit(solution)/shard_map/ppermute | solution.py:570
  68.7 9.4 %copy-start.10 = (f32[10,128,128]{2,1,0:T(8,128)S(1)}, f32[10,128,128]{2,1,0:T(8,128)}, u32[]{:S(2)}) copy-start(f32[10,128,128]{2,1,0:T(8,128)} %get-tuple-element.33.refs_6_) | copy-start | bytes 1966084
  77.6 4.1 %collective-permute-start.3 = (f32[7,128,128]{2,1,0:T(8,128)}, f32[7,128,128]{2,1,0:T(8,128)S(1)}, u32[]{:S(2)}, u32[]{:S(2)}) collective-permute-start(f32[7,128,128]{2,1,0:T(8,128)} %get-tuple-element.42), channel_id=1, source_target_pairs={{0,4},{4,0},{8,12},{12,8},{16,20},{20,16},{24,28},{28,24},{1,5},{5... | collective-permute-start | bytes 1376264 | tf_op jit(solution)/shard_map/ppermute | solution.py:606
  78.1 30.4 %collective-permute-start.7 = (f32[10,128,128]{2,1,0:T(8,128)S(1)}, f32[10,128,128]{2,1,0:T(8,128)S(1)}, u32[]{:S(2)}, u32[]{:S(2)}) collective-permute-start(f32[10,128,128]{2,1,0:T(8,128)S(1)} %copy-done.10), channel_id=1, source_target_pairs={{0,1},{1,0},{2,3},{3,2},{4,5},{5,4},{6,7},{7,6},{8,9},{9,8},{10,11... | collective-permute-start | bytes 1966088 | tf_op jit(solution)/shard_map/ppermute | solution.py:570
  82.8 23.8 %collective-permute-start.4 = (f32[7,128,128]{2,1,0:T(8,128)S(1)}, f32[7,128,128]{2,1,0:T(8,128)S(1)}, u32[]{:S(2)}, u32[]{:S(2)}) collective-permute-start(f32[7,128,128]{2,1,0:T(8,128)S(1)} %add.33.refs_6_), channel_id=1, source_target_pairs={{0,1},{1,0},{2,3},{3,2},{4,5},{5,4},{6,7},{7,6},{8,9},{9,8},{10,11... | collective-permute-start | bytes 1376264 | tf_op jit(solution)/shard_map/ppermute | solution.py:570
  109.9 17.4 %copy-start.4 = (f32[7,128,128]{2,1,0:T(8,128)S(1)}, f32[7,128,128]{2,1,0:T(8,128)}, u32[]{:S(2)}) copy-start(f32[7,128,128]{2,1,0:T(8,128)} %add.34.refs_5_) | copy-start | bytes 1376260
  120.8 98.6 %collective-permute-start.12 = (f32[26,128,128]{2,1,0:T(8,128)}, f32[26,128,128]{2,1,0:T(8,128)}, u32[]{:S(2)}, u32[]{:S(2)}) collective-permute-start(f32[26,128,128]{2,1,0:T(8,128)} %get-tuple-element.51.refs_2_), channel_id=1, source_target_pairs={{1,0},{2,3},{5,4},{6,7},{9,8},{10,11},{13,12},{14,15},{17,16},{18,... | collective-permute-start | bytes 5111816 | tf_op jit(solution)/shard_map/ppermute | solution.py:570
  125.1 36.9 %collective-permute-start.10 = (f32[10,128,128]{2,1,0:T(8,128)}, f32[10,128,128]{2,1,0:T(8,128)S(1)}, u32[]{:S(2)}, u32[]{:S(2)}) collective-permute-start(f32[10,128,128]{2,1,0:T(8,128)} %get-tuple-element.44.refs_2_), channel_id=1, source_target_pairs={{1,2},{2,1},{5,6},{6,5},{9,10},{10,9},{13,14},{14,13},{17,18},{18,... | collective-permute-start | bytes 1966088 | tf_op jit(solution)/shard_map/ppermute | solution.py:570
  127.3 34.0 %collective-permute-start.5 = (f32[7,128,128]{2,1,0:T(8,128)S(1)}, f32[7,128,128]{2,1,0:T(8,128)S(1)}, u32[]{:S(2)}, u32[]{:S(2)}) collective-permute-start(f32[7,128,128]{2,1,0:T(8,128)S(1)} %copy-done.4), channel_id=1, source_target_pairs={{0,3},{1,2},{2,1},{3,0},{4,7},{5,6},{6,5},{7,4},{8,11},{9,10},{10,... | collective-permute-start | bytes 1376264 | tf_op jit(solution)/shard_map/ppermute | solution.py:570
  162.9 27.4 %copy-start.3 = (f32[7,128,128]{2,1,0:T(8,128)S(1)}, f32[7,128,128]{2,1,0:T(8,128)}, u32[]{:S(2)}) copy-start(f32[7,128,128]{2,1,0:T(8,128)} %add.35.refs_13_.refs_1_) | copy-start | bytes 1376260
  188.9 52.7 %collective-permute-start.11 = (f32[10,128,128]{2,1,0:T(8,128)}, f32[10,128,128]{2,1,0:T(8,128)S(1)}, u32[]{:S(2)}, u32[]{:S(2)}) collective-permute-start(f32[10,128,128]{2,1,0:T(8,128)} %get-tuple-element.50.refs_2_), channel_id=1, source_target_pairs={{1,0},{2,3},{5,4},{6,7},{9,8},{10,11},{13,12},{14,15},{17,16},{18,... | collective-permute-start | bytes 1966088 | tf_op jit(solution)/shard_map/ppermute | solution.py:570
  190.3 2.0 collective-permute-start.6
  242.4 17.3 %copy-start.8 = (f32[512,128]{1,0:T(8,128)S(1)}, f32[512,128]{1,0:T(8,128)}, u32[]{:S(2)}) copy-start(f32[512,128]{1,0:T(8,128)} %get-tuple-element.62) | copy-start | bytes 786436
  242.4 21.4 %copy-start.16 = (f32[512,128]{1,0:T(8,128)S(1)}, f32[512,128]{1,0:T(8,128)}, u32[]{:S(2)}) copy-start(f32[512,128]{1,0:T(8,128)} %get-tuple-element.61) | copy-start | bytes 786436
  259.2 7.5 %collective-permute-start.13 = (f32[512,2048]{1,0:T(8,128)}, f32[512,2048]{1,0:T(8,128)}, u32[]{:S(2)}, u32[]{:S(2)}) collective-permute-start(f32[512,2048]{1,0:T(8,128)} %get-tuple-element.57.refs_2_.refs_6_), channel_id=1, source_target_pairs={{0,4},{4,0},{8,12},{12,8},{16,20},{20,16},{24,28},{28,24},{1,5},{5... | collective-permute-start | bytes 12582920 | tf_op jit(solution)/shard_map/ppermute | solution.py:606
  259.6 13.1 %collective-permute-start.14 = (f32[512,2048]{1,0:T(8,128)}, f32[512,2048]{1,0:T(8,128)}, u32[]{:S(2)}, u32[]{:S(2)}) collective-permute-start(f32[512,2048]{1,0:T(8,128)} %get-tuple-element.58.refs_4_), channel_id=1, source_target_pairs={{0,4},{4,0},{8,12},{12,8},{16,20},{20,16},{24,28},{28,24},{1,5},{5... | collective-permute-start | bytes 12582920 | tf_op jit(solution)/shard_map/ppermute | solution.py:606
  272.7 12.1 %copy-start.1 = (f32[4,512,128]{2,1,0:T(8,128)S(1)}, f32[4,512,128]{2,1,0:T(8,128)}, u32[]{:S(2)}) copy-start(f32[4,512,128]{2,1,0:T(8,128)} %param.17) | copy-start | bytes 3145732
  (10 other events, 23.8 us)
where the time goes:
time: 286 us; the launch traced here: 285 us
  Pallas kernels  169 us (59%)
  waiting for transfers between devices  74.8 us (26%)
  starting transfers between devices  22.3 us (8%)
  other arithmetic  7.53 us (3%)
  local copies, waits for them, and re-layouts  6.03 us (2%)
  matrix products  4.03 us (1%)
    pallas_call x10, Pallas kernels, call(): return lambda *args: built(*args, *after, *through)  169 us
    ppermute x8, waiting for transfers between devices, moved(): return lax.ppermute(x, 'row', pairs)  34.4 us
    ppermute x3, waiting for transfers between devices, shards(): lax.ppermute(own_state, 'row', [(i, (i + d) % parts) for i in range(parts)])  31.9 us
    ppermute x8, starting transfers between devices, moved(): return lax.ppermute(x, 'row', pairs)  18.2 us
    ppermute x4, waiting for transfers between devices, swapped(): return lax.ppermute(x, 'leaf', [(i, i ^ 1) for i in range(n)])  8.45 us
  transfers between devices with their start and end apart: 15, of which 7 were waited for; matrix products, arithmetic and copies ran while one was open for 4% of the time, Pallas kernels for 47%

commit v1 on v0

v1 whole, which is shorter than its diff:
```python
import functools

import jax
import jax.numpy as jnp
from jax import lax
from jax.experimental import pallas as pl
from jax.experimental.pallas import tpu as pltpu
from jax.sharding import PartitionSpec as P

HIGHEST = lax.Precision.HIGHEST
F32 = jnp.float32
BF16 = jnp.bfloat16
VMEM_LIMIT = 56 * 2**20
NN = (((1,), (0,)), ((), ()))
NT = (((1,), (1,)), ((), ()))


def split(x):
    hi = x.astype(BF16)
    return hi, (x - hi.astype(F32)).astype(BF16)


def parted(x):
    hi = lax.reduce_precision(x, 8, 7)
    return hi.astype(BF16), (x - hi).astype(BF16)


def dot3(a, b, dims=NN):
    one = functools.partial(lax.dot_general, dimension_numbers=dims, preferred_element_type=F32)
    return one(a[0], b[0]) + (one(a[0], b[1]) + one(a[1], b[0]))


def call(kernel, grid, prefetch, ins, outs, shapes, name, scratch=(), aliases=None, after=(), through=()):
    n_in, n_out = len(ins), len(outs)
    extra = len(after) + len(through)
    anywhere = pl.BlockSpec(memory_space=pl.ANY)

    def body(*refs):
        start = prefetch + n_in
        stop = start + extra + n_out
        kernel(*refs[:start], *refs[start + extra : stop], *refs[stop + len(through) :])

    aliases = dict(aliases or {})
    for t in range(len(through)):
        aliases[prefetch + n_in + len(after) + t] = n_out + t
    built = pl.pallas_call(
        body,
        grid_spec=pltpu.PrefetchScalarGridSpec(
            num_scalar_prefetch=prefetch,
            grid=grid,
            in_specs=list(ins) + [anywhere] * extra,
            out_specs=list(outs) + [anywhere] * len(through),
            scratch_shapes=scratch,
        ),
        out_shape=[jax.ShapeDtypeStruct(shape, kind) for shape, kind in shapes]
        + [jax.ShapeDtypeStruct(x.shape, x.dtype) for x in through],
        input_output_aliases=aliases,
        compiler_params=pltpu.CompilerParams(vmem_limit_bytes=VMEM_LIMIT),
        cost_estimate=pl.CostEstimate(flops=1, bytes_accessed=1, transcendentals=0),
        name=name,
    )
    return lambda *args: built(*args, *after, *through)


def whole(*shape):
    return pl.BlockSpec(shape, lambda *_: (0,) * len(shape))


def lower(n):
    return [(i, j) for i in range(n) for j in range(i + 1)]


def dense_kernel(blk, step, width, where, acol, bcol, a_ref, b_ref, p_ref, fh, fl, uh, ul, w_ref, buf, turned):
    i = pl.program_id(0)
    rows = p_ref.shape[0]
    orders = buf.shape[1] - width
    buf[...] = jnp.zeros_like(buf)
    turned[...] = jnp.zeros_like(turned)
    diag = lax.broadcasted_iota(jnp.int32, (blk, blk), 0) == lax.broadcasted_iota(jnp.int32, (blk, blk), 1)
    eye = jnp.where(diag, 0.75, 0.0).astype(F32)
    for t in range(step // blk):
        row = i * (step // blk) + t
        at = slice(t * blk, (t + 1) * blk)
        for s in range(a_ref.shape[1]):
            col = acol[0, row, s]
            block = a_ref[t, s] + eye if s == 0 else a_ref[t, s]
            buf[at, pl.ds(pl.multiple_of(col * blk, blk), blk)] = block
            local = col - where[0] * (rows // blk)

            @pl.when((local >= 0) & (local < rows // blk))
            def _():
                turned[pl.ds(pl.multiple_of(orders + local * blk, blk), blk), at] = block.T

        for s in range(b_ref.shape[1]):
            col = bcol[0, row, s]
            buf[at, pl.ds(pl.multiple_of(width + col * blk, blk), blk)] = b_ref[t, s]
            turned[pl.ds(pl.multiple_of(col * blk, blk), blk), at] = b_ref[t, s].T
    hi, lo = split(buf[...])
    fh[...] = hi
    fl[...] = lo
    uh[...], ul[...] = split(turned[...])
    part = dot3(split(p_ref[...]), (hi[:, width:], lo[:, width:]))

    @pl.when(i == 0)
    def _():
        w_ref[...] = part

    @pl.when(i > 0)
    def _():
        w_ref[...] += part


def dense(where, cost_rows, a_blocks, a_cols, b_blocks, b_cols, orders, after):
    rows, width = cost_rows.shape
    _, nnza, blk, _ = a_blocks.shape
    nnzb = b_blocks.shape[1]
    step = 2 * blk
    total = width + orders
    factor = pl.BlockSpec((step, total), lambda i, *_: (i, 0))
    turned = pl.BlockSpec((rows + orders, step), lambda i, *_: (0, i))
    return call(
        functools.partial(dense_kernel, blk, step, width),
        (width // step,),
        3,
        [
            pl.BlockSpec((2, nnza, blk, blk), lambda i, *_: (i, 0, 0, 0)),
            pl.BlockSpec((2, nnzb, blk, blk), lambda i, *_: (i, 0, 0, 0)),
            pl.BlockSpec((rows, step), lambda i, *_: (0, i)),
        ],
        [factor, factor, turned, turned, whole(rows, orders)],
        [((width, total), BF16)] * 2 + [((rows + orders, width), BF16)] * 2 + [((rows, orders), F32)],
        "dense",
        [pltpu.VMEM((step, total), F32), pltpu.VMEM((rows + orders, step), F32)],
        after=after,
    )(where, a_cols, b_cols, a_blocks, b_blocks, cost_rows)


def gram_kernel(blk, weight, where, bh, bl, w_ref, keep, give):
    core = where[1]
    h = dot3((bh[...], bl[...]), split(w_ref[...])) * weight[0]
    tiles = [h[i * blk : (i + 1) * blk, j * blk : (j + 1) * blk] for i, j in lower(h.shape[0] // blk)]
    count = len(tiles) // 2
    for side in range(2):

        @pl.when(core == side)
        def _():
            for t in range(count):
                keep[t] = tiles[side * count + t]
                give[t] = tiles[(1 - side) * count + t]


def gram(weight, where, uh, ul, w, blk, through):
    rows, orders = w.shape
    count = len(lower(orders // blk)) // 2
    turned = pl.BlockSpec((orders, rows), lambda i, weight, where: (0, where[0]))
    return call(
        functools.partial(gram_kernel, blk),
        (1,),
        2,
        [turned, turned, whole(rows, orders)],
        [whole(count, blk, blk)] * 2,
        [((count, blk, blk), F32)] * 2,
        "gram",
        through=through,
    )(weight, where, uh, ul, w)


def inverse_block(m):
    n = m.shape[0]
    sub = lax.broadcasted_iota(jnp.int32, (8, n), 0)
    lane = lax.broadcasted_iota(jnp.int32, (8, n), 1)
    strips = [m[i : i + 8] for i in range(0, n, 8)]

    def along(v, j):
        return jnp.broadcast_to(v[:, j : j + 1], (8, n))

    def down(v, t):
        return jnp.broadcast_to(v[t : t + 1], (8, n))

    for q in range(n // 8):
        panel = strips[q]
        cols = [along(panel, 8 * q + b) for b in range(8)]
        for t in range(8):
            here = sub == t
            inv = 1.0 / down(cols[t], t)

            def reduced(v):
                r = down(v, t) * inv
                return jnp.where(here, r, v - cols[t] * r)

            panel = reduced(jnp.where(lane == 8 * q + t, jnp.where(here, 1.0, 0.0), panel))
            cols[t + 1 :] = [reduced(v) for v in cols[t + 1 :]]
        inside = (lane >= 8 * q) & (lane < 8 * q + 8)
        rows = [down(panel, b) for b in range(8)]
        for i in range(q + 1, q + n // 8):
            old = strips[i % (n // 8)]
            terms = [along(old, 8 * q + b) * rows[b] for b in range(8)]
            while len(terms) > 1:
                terms = [x + y for x, y in zip(terms[::2], terms[1::2])]
            strips[i % (n // 8)] = jnp.where(inside, 0.0, old) - terms[0]
        strips[q] = panel
    return jnp.concatenate(strips, axis=0)


def inverse_kernel(where, mine, other, d_ref, out):
    half, blk, _ = mine.shape
    n = out.shape[0]
    dot = functools.partial(jnp.dot, precision=HIGHEST, preferred_element_type=F32)
    for side in range(2):

        @pl.when(where[0] == side)
        def _():
            for t, (i, j) in enumerate(lower(n // blk)):
                tile = (mine if t // half == side else other)[t % half]
                out[i * blk : (i + 1) * blk, j * blk : (j + 1) * blk] = tile
                if i != j:
                    out[j * blk : (j + 1) * blk, i * blk : (i + 1) * blk] = tile.T

    diag = lax.broadcasted_iota(jnp.int32, (n, n), 0) == lax.broadcasted_iota(jnp.int32, (n, n), 1)
    out[...] += jnp.where(diag, d_ref[...], 0.0)

    @pl.loop(0, n // blk)
    def _(b):
        here = pl.ds(pl.multiple_of(b * blk, blk), blk)
        inv = inverse_block(out[here, here])
        row = dot(inv, out[here, :])
        col = out[:, here]
        out[...] -= dot(col, row)
        out[:, here] = -dot(col, inv)
        out[here, :] = row
        out[here, here] = inv


def inverse(where, mine, other, control_cost, after):
    half, blk, _ = mine.shape
    n = control_cost.shape[0]
    return call(
        inverse_kernel,
        (1,),
        1,
        [whole(half, blk, blk)] * 2 + [whole(1, n)],
        [whole(n, n)],
        [((n, n), F32)],
        "inverse",
        after=after,
    )(where, mine, other, control_cost[None])[0]


def tiled(block, blk):
    n = block.shape[0] // blk
    return [block[i * blk : (i + 1) * blk, j * blk : (j + 1) * blk] for i in range(n) for j in range(n)]


def pack_kernel(blk, where, own, near, inner, far, x_ref, pair_out, mid_out):
    diag = [own[i * blk : (i + 1) * blk, j * blk : (j + 1) * blk] for i, j in lower(own.shape[0] // blk)]
    x = [x_ref[0, :blk], x_ref[0, blk:]]
    for t, tile in enumerate(diag + x + tiled(inner, blk) + tiled(far, blk)):
        pair_out[t] = tile
    for t, tile in enumerate(diag + x + tiled(near, blk)):
        mid_out[t] = tile


def pack(where, cost_rows, parent_state, blk):
    rows = cost_rows.shape[0]
    samples = parent_state.shape[2]
    count, full = len(lower(rows // blk)) + 2, (rows // blk) ** 2
    specs = [pl.BlockSpec((rows, rows), functools.partial(lambda t, i, where: (0, where[t]), t)) for t in range(4)]
    specs.append(pl.BlockSpec((1, rows // 2, samples), lambda i, where: (where[4], where[5], 0)))
    sizes = [count + 2 * full, count + full]
    return call(
        functools.partial(pack_kernel, blk),
        (1,),
        1,
        specs,
        [whole(size, blk, blk) for size in sizes],
        [((size, blk, blk), F32) for size in sizes],
        "pack",
    )(where, *[cost_rows] * 4, parent_state)


def unpack(tiles, step, n, xh, xl):
    blk = tiles.shape[1]
    lead = len(lower(n))
    for t, (i, j) in enumerate(lower(n) if step == 0 else [(i, j) for i in range(n) for j in range(n)]):
        tile = tiles[t if step == 0 else lead + 2 + (step - 1) * n * n + t]
        places = [(i, j, tile)] + ([(j, i, tile.T)] if step == 0 and i != j else [])
        for r, c, value in places:
            at = slice(r * blk, (r + 1) * blk), slice(c * blk, (c + 1) * blk)
            xh[at], xl[at] = split(value)


def collect_kernel(where, pair, mid, end, mid_last, end_last, out):
    out[:2] = pair[...]

    @pl.when(where[0] == 1)
    def _():
        out[2:4] = end[...]
        out[4:6] = end_last[...]

    @pl.when(where[0] == 0)
    def _():
        out[2:4] = mid[...]
        out[4:6] = mid_last[...]


def collect(where, messages):
    blk = messages[0].shape[1]
    lead = messages[3].shape[0] // 2 - 1
    return call(
        collect_kernel,
        (1,),
        1,
        [pl.BlockSpec((2, blk, blk), lambda i, where: (lead, 0, 0))] * 5,
        [whole(6, blk, blk)],
        [((6, blk, blk), F32)],
        "collect",
    )(where, *messages)[0]


def drift_kernel(where, own, mine, other, fh, fl, x_ref, out):
    blk = mine.shape[1]
    rows = own.shape[1]
    core = where[0]
    x_ref[pl.ds(pl.multiple_of(where[1] * rows, rows), rows)] = own[0]
    for d in range(3):
        for t in range(2):
            base = where[2 + d] * rows + t * blk
            half = rows // 2
            x_ref[pl.ds(pl.multiple_of(base + core * half, blk), blk)] = mine[2 * d + t]
            x_ref[pl.ds(pl.multiple_of(base + (1 - core) * half, blk), blk)] = other[2 * d + t]
    out[...] = dot3((fh[...], fl[...]), split(x_ref[...]))


def drift(where, parent_state, mine, other, fh, fl):
    _, rows, samples = parent_state.shape
    count, blk, _ = mine.shape
    width = rows * 4
    factor = pl.BlockSpec((rows, width), lambda i, where: (where[1], 0))
    return call(
        drift_kernel,
        (1,),
        1,
        [pl.BlockSpec((1, rows, samples), lambda i, where: (where[5], 0, 0))]
        + [whole(count, blk, blk)] * 2
        + [factor, factor],
        [whole(width, samples), whole(rows, samples)],
        [((width, samples), F32), ((rows, samples), F32)],
        "drift",
    )(where, parent_state, mine, other, fh, fl)


def passed(arrays, after):
    return call(lambda *_: None, (1,), 0, [], [], [], "passed", after=[after], through=arrays)()


def begin_kernel(steps, where, weight, p_ref, uh, ul, vh, vl, fh, fl, rest, s_out, g_out, mine, hi, lo):
    g = pl.program_id(0)

    @pl.when(g < steps)
    def _():
        p = split(p_ref[...])
        part = dot3((uh[...], ul[...]), p, NT)

        @pl.when(g == 0)
        def _():
            mine[...] = part

        @pl.when(g > 0)
        def _():
            mine[...] += part

        @pl.when(g != where[0])
        def _():
            rest[...] = dot3((vh[...], vl[...]), p)

    @pl.when(g == steps)
    def _():
        hi[...], lo[...] = split(mine[...] * weight[0])

    @pl.when(g >= steps)
    def _():
        part = dot3((hi[...], lo[...]), (fh[...], fl[...]))
        orders = g_out.shape[0]
        s_out[...] = part[orders:]
        g_out[...] = part[:orders]


def begin(where, weight, cost_rows, uh, ul, fh, fl, after):
    rows, width = cost_rows.shape
    tall = uh.shape[0]
    orders = tall - rows
    steps = width // rows
    tile = 512

    def early(g):
        return jnp.minimum(g, steps - 1)

    def late(g):
        return jnp.maximum(g - steps, 0)

    each = pl.BlockSpec((tall, rows), lambda g, *_: (0, early(g)))
    own = pl.BlockSpec((tall, rows), lambda g, where, _: (0, where[0]))
    factor = pl.BlockSpec((rows, tile), lambda g, where, _: (where[0], late(g)))
    return call(
        functools.partial(begin_kernel, steps),
        (steps + width // tile,),
        2,
        [pl.BlockSpec((rows, rows), lambda g, *_: (0, early(g))), each, each, own, own, factor, factor],
        [
            each,
            pl.BlockSpec((rows, tile), lambda g, *_: (0, late(g))),
            pl.BlockSpec((orders, tile), lambda g, *_: (0, late(g))),
        ],
        [((tall, width), F32), ((rows, width), F32), ((orders, width), F32)],
        "begin",
        [pltpu.VMEM((tall, rows), F32)] + [pltpu.VMEM((tall, rows), BF16)] * 2,
        after=after,
    )(where, weight, cost_rows, uh, ul, uh, ul, fh, fl)


def stage_kernel(options, size, where, weight, *refs):
    arrived = refs[:options]
    vh, vl, n_in, fh, fl, s_in, g_in, *refs = refs[options:]
    if size > 1:
        uh, ul, s_out, g_out, n_out, done, hi, lo, xh, xl = refs
    else:
        s_out, g_out, done, hi, lo, xh, xl = refs
    g = pl.program_id(0)
    n = xh.shape[0] // arrived[0].shape[1]
    for c in range(options):
        for t in range(size):

            @pl.when((g == t) & (where[0] == c))
            def _():
                unpack(arrived[c], t, n, xh, xl)

    @pl.when(g == 0)
    def _():
        done[...] = n_in[...] + dot3((vh[...], vl[...]), (xh[...], xl[...]))

    if size > 1:

        @pl.when((g > 0) & (g < size))
        def _():
            x = xh[...], xl[...]
            done[...] += dot3((uh[...], ul[...]), x, NT)
            n_out[...] = n_in[...] + dot3((vh[...], vl[...]), x)

    @pl.when(g == size)
    def _():
        hi[...], lo[...] = split(done[...] * weight[0])

    @pl.when(g >= size)
    def _():
        part = dot3((hi[...], lo[...]), (fh[...], fl[...]))
        orders = g_out.shape[0]
        s_out[...] = s_in[...] + part[orders:]
        g_out[...] = g_in[...] + part[:orders]


def stage(where, weight, arrived, size, uh, ul, n, fh, fl, sums, after=(), through=()):
    tall, width = n.shape
    rows, orders = sums[0].shape[0], sums[1].shape[0]
    tile = 512

    def place(g, where):
        return where[1 + jnp.minimum(g, size - 1)]

    def later(g, where):
        return where[1 + jnp.clip(g, 1, size - 1)]

    def turn(g):
        return jnp.maximum(g - size, 0)

    block = pl.BlockSpec((tall, rows), lambda g, where, _: (0, place(g, where)))
    beyond = pl.BlockSpec((tall, rows), lambda g, where, _: (0, later(g, where)))
    focus = pl.BlockSpec((tall, rows), lambda g, where, _: (0, where[1]))
    factor = pl.BlockSpec((rows, tile), lambda g, where, _: (where[1], turn(g)))
    s_spec = pl.BlockSpec((rows, tile), lambda g, *_: (0, turn(g)))
    g_spec = pl.BlockSpec((orders, tile), lambda g, *_: (0, turn(g)))
    first = 2 + len(arrived)
    more = size > 1
    return call(
        functools.partial(stage_kernel, len(arrived), size),
        (size + width // tile,),
        2,
        [whole(*x.shape) for x in arrived]
        + [focus, focus, block, factor, factor, s_spec, g_spec]
        + [beyond] * (2 * more),
        [s_spec, g_spec] + [beyond] * more,
        [((rows, width), F32), ((orders, width), F32)] + [((tall, width), F32)] * more,
        "stage",
        [pltpu.VMEM((tall, rows), F32)] + [pltpu.VMEM((tall, rows), BF16)] * 2 + [pltpu.VMEM((rows, rows), BF16)] * 2,
        {first + 5: 0, first + 6: 1, **({first + 2: 2} if more else {})},
        after,
        through,
    )(where, weight, *arrived, uh, ul, n, fh, fl, *sums, *([uh, ul] if more else []))


def final_kernel(where, h_ref, g1, g2, s1, s2, q1, q2, d_ref, x_ref, y_ref, bh, bl, gain, out, reached, hi, lo, q):
    n = pl.program_id(0)
    rows = out.shape[0]

    @pl.when(n == 0)
    def _():
        value = -dot3(split(h_ref[...]), split(g1[...] + g2[...]))
        gain[...] = value
        hi[...], lo[...] = split(value.T)
        q[...] = jnp.zeros_like(q)

    cross = split(q1[...] + q2[...])
    part = s1[...] + s2[...] + dot3((hi[...], lo[...]), cross)
    diag = lax.broadcasted_iota(jnp.int32, (rows, rows), 0) == lax.broadcasted_iota(jnp.int32, (rows, rows), 1)
    out[...] = part + jnp.where(diag & (n == where[0]), d_ref[...], 0.0)
    q[...] += dot3(cross, split(x_ref[...]))

    @pl.when(n == pl.num_programs(0) - 1)
    def _():
        u = -dot3(split(h_ref[...]), split(q[...]))
        reached[...] = y_ref[...] + dot3((bh[...], bl[...]), split(u))


def final(where, hinv, own, other, state_cost, x, y, fh, fl):
    rows, width = own[0].shape
    orders = own[1].shape[0]
    samples = x.shape[1]
    s_spec = pl.BlockSpec((rows, rows), lambda n, where: (0, n))
    g_spec = pl.BlockSpec((orders, rows), lambda n, where: (0, n))
    mine = pl.BlockSpec((orders, rows), lambda n, where: (0, where[0]))
    factor = pl.BlockSpec((rows, orders), lambda n, where: (where[0], width // orders))
    return call(
        final_kernel,
        (width // rows,),
        1,
        [whole(orders, orders), mine, mine, s_spec, s_spec, g_spec, g_spec, whole(1, rows)]
        + [pl.BlockSpec((rows, samples), lambda n, where: (n, 0)), whole(rows, samples), factor, factor],
        [whole(orders, rows), s_spec, whole(rows, samples)],
        [((orders, rows), F32), ((rows, width), F32), ((rows, samples), F32)],
        "final",
        [pltpu.VMEM((rows, orders), BF16)] * 2 + [pltpu.VMEM((orders, samples), F32)],
    )(where, hinv, own[1], other[1], own[0], other[0], own[1], other[1], state_cost[None], x, y, fh, fl)


def image_kernel(where, weight, fh, fl, p_ref, out, acc):
    k = pl.program_id(0)
    part = dot3(split(p_ref[...]), (fh[...], fl[...]))

    @pl.when(k == 0)
    def _():
        acc[...] = part

    @pl.when(k > 0)
    def _():
        acc[...] += part

    @pl.when(k == pl.num_programs(0) - 1)
    def _():
        out[...] = acc[...].T * weight[0]


def image(where, weight, fh, fl, cost_rows):
    rows, width = cost_rows.shape
    chunk = 512
    factor = pl.BlockSpec((chunk, rows), lambda k, where, _: (k, where[0]))
    return call(
        image_kernel,
        (width // chunk,),
        2,
        [factor, factor, pl.BlockSpec((rows, chunk), lambda k, *_: (0, k))],
        [whole(rows, rows)],
        [((rows, rows), F32)],
        "image",
        [pltpu.VMEM((rows, rows), F32)],
    )(where, weight, fh, fl, cost_rows)[0]


def accumulate_kernel(first, where, y_ref, fh, fl, *refs):
    out = refs[-1]
    part = dot3(split(y_ref[...]), (fh[...], fl[...]))
    out[...] = part if first else refs[0][...] + part


def accumulate(where, y, fh, fl, acc):
    rows = y.shape[0]
    total = fh.shape[1]
    tile = 512
    first = acc is None
    spec = pl.BlockSpec((rows, tile), lambda n, where: (0, n))
    factor = pl.BlockSpec((rows, tile), lambda n, where: (where[0], n))
    return call(
        functools.partial(accumulate_kernel, first),
        (total // tile,),
        1,
        [whole(rows, rows), factor, factor] + [spec] * (not first),
        [spec],
        [((rows, total), F32)],
        "accumulate",
        aliases=None if first else {4: 0},
    )(where, y, fh, fl, *(() if first else (acc,)))[0]


def by_images(z, parts, weight, cost_rows, fh, fl):
    rows, width = cost_rows.shape
    acc = None
    for d in range(parts):
        block = image(((z + d) % parts)[None], weight, fh, fl, cost_rows)
        if d:
            block = lax.ppermute(block, "row", [(i, (i + d) % parts) for i in range(parts)])
        acc = accumulate(((z - d) % parts)[None], block, fh, fl, acc)
    cross = lax.all_gather(acc[:, width:], "row")
    return acc[:, :width], jnp.swapaxes(cross.reshape(width, -1), 0, 1)


def by_blocks(z, core, parent, weight, cost_rows, parent_state, dense_parts, control_cost, blk, messages):
    fh, fl, uh, ul, w = dense_parts
    edge = ((z == 0) | (z == 3)).astype(jnp.int32)
    left = z < 2
    second, third = jnp.where(left, 2, 1), jnp.where(left, 3, 0)

    def moved(x, *pairs):
        return lax.ppermute(x, "row", pairs)

    def across(x):
        return moved(x, (1, 2), (2, 1))

    def to_end(x):
        return moved(x, (1, 0), (2, 3))

    pair = moved(messages[0], (0, 1), (1, 0), (2, 3), (3, 2))
    mid = across(messages[1])
    keep, give = gram(weight, jnp.stack([z, core]), uh, ul, w, blk, [])
    tiles = keep + swapped(give)
    n, *sums = begin(z[None], weight, cost_rows, uh, ul, fh, fl, [tiles])
    tiles = tiles + moved(tiles, (0, 1), (3, 2))
    mid, tiles = passed([mid, tiles], n)
    end = to_end(mid)
    tiles = tiles + across(tiles)
    pair, tiles = passed([pair, tiles], n)
    mid_last = across(pair[: len(lower(w.shape[0] // blk)) + 2])
    finished = to_end(tiles)
    where = jnp.stack([z * 0, z ^ 1, second, third])
    *sums, n = stage(where, weight, [pair], 3, uh, ul, n, fh, fl, sums)
    mid_last, finished = passed([mid_last, finished], n)
    end_last = to_end(mid_last)
    tiles = jnp.where(edge == 1, finished, tiles)
    hinv = inverse(core[None], tiles, swapped(tiles), control_cost, [n])
    where = jnp.stack([edge, second, third])
    *sums, n = stage(where, weight, [mid, end], 2, uh, ul, n, fh, fl, sums, [hinv])
    where = jnp.stack([edge, third])
    sums = stage(where, weight, [mid_last, end_last], 1, uh, ul, n, fh, fl, sums)
    halves = collect(edge[None], [pair, mid, end, mid_last, end_last])
    where = jnp.stack([core, z, z ^ 1, second, third, parent])
    x, y = drift(where, parent_state, halves, swapped(halves), fh, fl)
    return hinv, sums, x, y


def swapped(x):
    n = lax.axis_size("leaf")
    return lax.ppermute(x, "leaf", [(i, i ^ 1) for i in range(n)])


def shards(
    leaf_cost,
    a_blocks,
    a_cols,
    b_blocks,
    b_cols,
    branch_prob,
    state_cost,
    control_cost,
    parent_state,
):
    cost_rows = leaf_cost[0]
    rows, width = cost_rows.shape
    blk = a_blocks.shape[3]
    orders = control_cost.shape[0]
    parts = lax.axis_size("row")
    z = lax.axis_index("row")
    leaf = lax.axis_index("leaf")
    core = leaf % 2
    line = parts == 4 and rows == orders

    sent = []
    if line:
        left = z < 2
        near = jnp.where(left, 0, 3)
        where = jnp.stack([z, near, jnp.where(left, 2, 1), 3 - near, leaf // 2, core])
        sent = pack(where, cost_rows, parent_state, blk)
    parts_of = dense(z[None], cost_rows, a_blocks[0], a_cols, b_blocks[0], b_cols, orders, sent)
    fh, fl, uh, ul, w = parts_of
    if line:
        hinv, own, x, y = by_blocks(
            z, core, leaf // 2, branch_prob, cost_rows, parent_state, parts_of, control_cost, blk, sent
        )
    else:
        keep, give = gram(branch_prob, jnp.stack([z, core]), uh, ul, w, blk, [])
        tiles = lax.psum(keep + swapped(give), "row")
        hinv = inverse(core[None], tiles, swapped(tiles), control_cost, [])
        own = by_images(z, parts, branch_prob, cost_rows, fh, fl)
        own_state = lax.dynamic_index_in_dim(parent_state, leaf // 2, 0, keepdims=False)
        x = lax.all_gather(own_state, "row", tiled=True)
        y = dot3([lax.dynamic_slice(f, (z * rows, 0), (rows, width)) for f in (fh, fl)], parted(x))
    other = tuple(swapped(x) for x in own)
    gain, pcost, reached = final(z[None], hinv, own, other, state_cost, x, y, fh, fl)
    return pcost[None], gain[None], reached[None]


def solution(mesh):
    placed = (
        P("leaf", "row", None),
        P("leaf", None, None, None, None),
        P("leaf", None, None),
        P("leaf", None, None, None, None),
        P("leaf", None, None),
        P("leaf"),
        P("row"),
        P(),
        P(None, "row", None),
    )
    return jax.shard_map(
        shards,
        mesh=mesh,
        in_specs=placed,
        out_specs=(P("leaf", "row", None), P("leaf", None, "row"), P("leaf", "row", None)),
        check_vma=False,
    )
```

time: 286 us -> 238 us (0.83)
  the two profiles are of different devices: /device:TPU:21 before, /device:TPU:0 now
where the time goes in v1:
time: 238 us; the launch traced here: 237 us
  Pallas kernels  175 us (74%)
  waiting for transfers between devices  26.3 us (11%)
  starting transfers between devices  17.2 us (7%)
  local copies, waits for them, and re-layouts  8.67 us (4%)
  other arithmetic  7.95 us (3%)
    pallas_call x14, Pallas kernels, call(): return lambda *args: built(*args, *after, *through)  175 us
    ppermute x8, waiting for transfers between devices, moved(): return lax.ppermute(x, 'row', pairs)  19.1 us
    ppermute x8, starting transfers between devices, moved(): return lax.ppermute(x, 'row', pairs)  16.2 us
    ppermute x5, waiting for transfers between devices, swapped(): return lax.ppermute(x, 'leaf', [(i, i ^ 1) for i in range(n)])  7.22 us
    unnamed x24, local copies, waits for them, and re-layouts  6.27 us
  transfers between devices with their start and end apart: 13, of which 5 were waited for; matrix products, arithmetic and copies ran while one was open for 5% of the time, Pallas kernels for 58%

profile of v1, /device:TPU:0, one launch (start us, length us, event | category | flops | bytes accessed | tf_op | source)
XLA Modules:
  0.0 236.8 jit_solution(9745062801205322651)
XLA Ops:
  1.3 5.5 %pack.1 = (f32[44,128,128]{2,1,0:T(8,128)}, f32[28,128,128]{2,1,0:T(8,128)}) custom-call(s32[6]{0:T(128)} %stack.61.refs_0_, f32[512,2048]{1,0:T(8,128)} %bitcast.17, f32[512,2048]{1,0:T(8,128)} %bitcast.18, f32[512,2048]{1,0:T(8,128)} %bitcast.19, f32[512,2048]{1,0:T(8,128)} %bitcast.20, f32[4,512,128]{2,1,0:T(8,128)} %refs_1_.6), custom_call_target="tpu_custom_call" | custom-call | flops 1 | bytes 1 | tf_op jit(solution)/shard_map/pack/pallas_call | solution.py:62
  6.8 2.9 %collective-permute-start.1 = (f32[44,128,128]{2,1,0:T(8,128)}, f32[44,128,128]{2,1,0:T(8,128)S(1)}, u32[]{:S(2)}, u32[]{:S(2)}) collective-permute-start(f32[44,128,128]{2,1,0:T(8,128)} %get-tuple-element.34.refs_6_), channel_id=1, source_target_pairs={{0,1},{1,0},{2,3},{3,2},{4,5},{5,4},{6,7},{7,6},{8,9},{9,8},{10,11... | collective-permute-start | bytes 8650760 | tf_op jit(solution)/shard_map/ppermute | solution.py:621
  9.7 1.9 collective-permute-start.2
  13.0 23.9 %dense.1 = (bf16[2048,2560]{1,0:T(8,128)(2,1)}, bf16[2048,2560]{1,0:T(8,128)(2,1)}, bf16[1024,2048]{1,0:T(8,128)(2,1)}, bf16[1024,2048]{1,0:T(8,128)(2,1)}, f32[512,512]{1,0:T(8,128)}) custom-call(s32[1]{0:T(128)} %bitcast.refs_0_, s32[1,16,8]{2,1,0:T(8,128)} %copy.26.refs_1_, s32[1,16,2]{2,1,0:T(8,128)} %copy.27.refs_2_, f32[16,8,128,128]{3,2,1,0:T(8,128)} %bitcast.23, ...), custom_call_target="tpu_custom_call" | custom-call | flops 1 | bytes 1 | tf_op jit(solution)/shard_map/dense/pallas_call | solution.py:62
  38.1 4.1 %gram.1 = (f32[5,128,128]{2,1,0:T(8,128)}, f32[5,128,128]{2,1,0:T(8,128)}) custom-call(f32[1]{0:T(128)S(6)} %copy.42.refs_0_.refs_1_, s32[2]{0:T(128)} %pad_add_fusion.1.refs_1_, bf16[1024,2048]{1,0:T(8,128)(2,1)} %get-tuple-element.36.refs_2_.refs_3_.refs_5_.refs_10_.refs_4_.refs_11_, ...), custom_call_target="tpu_custom_call" | custom-call | flops 1 | bytes 1 | tf_op jit(solution)/shard_map/gram/pallas_call | solution.py:62
  42.4 1.6 collective-permute-done
  45.0 5.8 %collective-permute-start.3 = (f32[5,128,128]{2,1,0:T(8,128)S(1)}, f32[5,128,128]{2,1,0:T(8,128)S(1)}, u32[]{:S(2)}, u32[]{:S(2)}) collective-permute-start(f32[5,128,128]{2,1,0:T(8,128)S(1)} %add.15.refs_9_), channel_id=1, source_target_pairs={{0,1},{3,2},{4,5},{7,6},{8,9},{11,10},{12,13},{15,14},{16,17},{19,... | collective-permute-start | bytes 983048 | tf_op jit(solution)/shard_map/ppermute | solution.py:621
  50.9 26.8 %begin.1 = (f32[1024,2048]{1,0:T(8,128)}, f32[512,2048]{1,0:T(8,128)}, f32[512,2048]{1,0:T(8,128)}) custom-call(s32[1]{0:T(128)} %bitcast.refs_0_, f32[1]{0:T(128)S(6)} %copy.42.refs_0_.refs_1_, f32[512,2048]{1,0:T(8,128)} %bitcast.22, bf16[1024,2048]{1,0:T(8,128)(2,1)} %get-tuple-element.36.refs_2_.refs_3_.refs_5_.refs_10_.refs_4_.refs_11_, ...), custom_call_target="tpu_custom_call" | custom-call | flops 1 | bytes 1 | tf_op jit(solution)/shard_map/begin/pallas_call | solution.py:62
  78.7 1.7 add.16.refs_2_
  81.1 1.3 collective-permute-start.9
  82.4 1.8 add.17.refs_2_
  84.2 1.6 copy-done
  85.7 1.2 slice.3
  87.7 1.5 collective-permute-start.6
  89.7 25.9 %stage.3 = (f32[512,2048]{1,0:T(8,128)}, f32[512,2048]{1,0:T(8,128)}, f32[1024,2048]{1,0:T(8,128)}) custom-call(s32[4]{0:T(128)} %pad_add_fusion.refs_0_, f32[1]{0:T(128)S(6)} %copy.42.refs_0_.refs_1_, f32[44,128,128]{2,1,0:T(8,128)} %get-tuple-element.45.refs_2_.refs_1_, ...), custom_call_target="tpu_custom_call", output_to_operand_aliasing={{0}: (8, {}), {1}: (9, {}), {2}: (5, {})} | custom-call | flops 1 | bytes 1 | tf_op jit(solution)/shard_map/stage/pallas_call | solution.py:62
  115.6 18.1 %collective-permute-done.6.refs_2_ = f32[5,128,128]{2,1,0:T(8,128)S(1)} collective-permute-done((f32[5,128,128]{2,1,0:T(8,128)}, f32[5,128,128]{2,1,0:T(8,128)S(1)}, u32[]{:S(2)}, u32[]{:S(2)}) %collective-permute-start.6) | collective-permute-done | bytes 327712 | tf_op jit(solution)/shard_map/ppermute | solution.py:621
  134.7 1.4 collective-permute-start.8
  139.6 25.7 %inverse.1.refs_13_.refs_1_ = f32[512,512]{1,0:T(8,128)} custom-call(s32[1]{0:T(128)} %bitcast.1.refs_0_, f32[5,128,128]{2,1,0:T(8,128)} %copy-done.6, f32[5,128,128]{2,1,0:T(8,128)} %copy-done.8, f32[1,512]{1,0:T(1,128)} %bitcast.26, f32[1024,2048]{1,0:T(8,128)} %get-tuple-element.48.refs_0_.refs_4_.refs_6_), custom_call_target="tpu_custom_call" | custom-call | flops 1 | bytes 1 | tf_op jit(solution)/shard_map/inverse/pallas_call | solution.py:62
  165.3 22.4 %stage.4 = (f32[512,2048]{1,0:T(8,128)}, f32[512,2048]{1,0:T(8,128)}, f32[1024,2048]{1,0:T(8,128)}) custom-call(s32[3]{0:T(128)} %pad_add_fusion.3.refs_0_, f32[1]{0:T(128)S(6)} %copy.42.refs_0_.refs_1_, f32[28,128,128]{2,1,0:T(8,128)} %get-tuple-element.52.refs_2_, ...), custom_call_target="tpu_custom_call", output_to_operand_aliasing={{0}: (9, {}), {1}: (10, {}), {2}: (6, {})} | custom-call | flops 1 | bytes 1 | tf_op jit(solution)/shard_map/stage/pallas_call | solution.py:62
  188.6 16.8 %stage.5 = (f32[512,2048]{1,0:T(8,128)}, f32[512,2048]{1,0:T(8,128)}) custom-call(s32[2]{0:T(128)} %pad_add_fusion.2.refs_0_, f32[1]{0:T(128)S(6)} %copy.42.refs_0_.refs_1_, f32[12,128,128]{2,1,0:T(8,128)} %get-tuple-element.51.refs_2_.refs_4_, f32[12,128,128]{2,1,0:T(8,128)} %copy-done.2, ...), custom_call_target="tpu_custom_call", output_to_operand_aliasing={{0}: (9, {}), {1}: (10, {})} | custom-call | flops 1 | bytes 1 | tf_op jit(solution)/shard_map/stage/pallas_call | solution.py:62
  205.9 1.9 collect.1.refs_2_
  208.6 5.3 %collective-permute-done.12.refs_3_ = f32[6,128,128]{2,1,0:T(8,128)S(1)} collective-permute-done((f32[6,128,128]{2,1,0:T(8,128)}, f32[6,128,128]{2,1,0:T(8,128)S(1)}, u32[]{:S(2)}, u32[]{:S(2)}) %collective-permute-start.12) | collective-permute-done | bytes 393248 | tf_op jit(solution)/shard_map/ppermute | solution.py:659
  214.6 5.8 %drift.1 = (f32[2048,128]{1,0:T(8,128)}, f32[512,128]{1,0:T(8,128)}) custom-call(s32[6]{0:T(128)} %stack.66.refs_0_, f32[4,512,128]{2,1,0:T(8,128)} %refs_1_.6, f32[6,128,128]{2,1,0:T(8,128)} %collect.1.refs_2_, f32[6,128,128]{2,1,0:T(8,128)} %copy-done.7, bf16[2048,2560]{1,0:T(8,128)(2,1)} %get-tuple-element.38.refs_7_.refs_6_.refs_4_.refs_11_, ...), custom_call_target="tpu_custom_call" | custom-call | flops 1 | bytes 1 | tf_op jit(solution)/shard_map/drift/pallas_call | solution.py:62
  220.4 16.2 %final.1 = (f32[512,512]{1,0:T(8,128)}, f32[512,2048]{1,0:T(8,128)}, f32[512,128]{1,0:T(8,128)}) custom-call(s32[1]{0:T(128)} %bitcast.refs_0_, f32[512,512]{1,0:T(8,128)} %inverse.1.refs_13_.refs_1_, f32[512,2048]{1,0:T(8,128)} %get-tuple-element.58.refs_2_.refs_6_, f32[512,2048]{1,0:T(8,128)} %collective-permute-done.10.refs_3_.refs_7_, ...), custom_call_target="tpu_custom_call" | custom-call | flops 1 | bytes 1 | tf_op jit(solution)/shard_map/final/pallas_call | solution.py:62
  (51 shorter events, 14.1 us)
Async XLA Ops:
  1.3 10.4 %copy-start.9 = (s32[1,16,8]{1,2,0:T(8,128)S(1)}, s32[1,16,8]{1,2,0:T(8,128)}, u32[]{:S(2)}) copy-start(s32[1,16,8]{1,2,0:T(8,128)} %param.11) | copy-start | bytes 1540
  1.3 11.0 %copy-start.10 = (s32[1,16,2]{1,2,0:T(2,128)S(1)}, s32[1,16,2]{1,2,0:T(2,128)}, u32[]{:S(2)}) copy-start(s32[1,16,2]{1,2,0:T(2,128)} %param.13) | copy-start | bytes 388
  6.8 77.4 %collective-permute-start.1 = (f32[44,128,128]{2,1,0:T(8,128)}, f32[44,128,128]{2,1,0:T(8,128)S(1)}, u32[]{:S(2)}, u32[]{:S(2)}) collective-permute-start(f32[44,128,128]{2,1,0:T(8,128)} %get-tuple-element.34.refs_6_), channel_id=1, source_target_pairs={{0,1},{1,0},{2,3},{3,2},{4,5},{5,4},{6,7},{7,6},{8,9},{9,8},{10,11... | collective-permute-start | bytes 8650760 | tf_op jit(solution)/shard_map/ppermute | solution.py:621
  9.7 70.7 %collective-permute-start.2 = (f32[28,128,128]{2,1,0:T(8,128)}, f32[28,128,128]{2,1,0:T(8,128)}, u32[]{:S(2)}, u32[]{:S(2)}) collective-permute-start(f32[28,128,128]{2,1,0:T(8,128)} %get-tuple-element.35.refs_7_), channel_id=1, source_target_pairs={{1,2},{2,1},{5,6},{6,5},{9,10},{10,9},{13,14},{14,13},{17,18},{18,... | collective-permute-start | bytes 5505032 | tf_op jit(solution)/shard_map/ppermute | solution.py:621
  42.2 1.8 collective-permute-start
  45.0 5.8 %copy-start.3 = (f32[5,128,128]{2,1,0:T(8,128)}, f32[5,128,128]{2,1,0:T(8,128)S(1)}, u32[]{:S(2)}) copy-start(f32[5,128,128]{2,1,0:T(8,128)S(1)} %add.15.refs_9_) | copy-start | bytes 983044
  45.0 33.6 %collective-permute-start.3 = (f32[5,128,128]{2,1,0:T(8,128)S(1)}, f32[5,128,128]{2,1,0:T(8,128)S(1)}, u32[]{:S(2)}, u32[]{:S(2)}) collective-permute-start(f32[5,128,128]{2,1,0:T(8,128)S(1)} %add.15.refs_9_), channel_id=1, source_target_pairs={{0,1},{3,2},{4,5},{7,6},{8,9},{11,10},{12,13},{15,14},{16,17},{19,... | collective-permute-start | bytes 983048 | tf_op jit(solution)/shard_map/ppermute | solution.py:621
  80.4 2.0 collective-permute-start.4
  81.1 84.2 %collective-permute-start.9 = (f32[28,128,128]{2,1,0:T(8,128)}, f32[28,128,128]{2,1,0:T(8,128)}, u32[]{:S(2)}, u32[]{:S(2)}) collective-permute-start(f32[28,128,128]{2,1,0:T(8,128)} %get-tuple-element.52.refs_2_), channel_id=1, source_target_pairs={{1,0},{2,3},{5,4},{6,7},{9,8},{10,11},{13,12},{14,15},{17,16},{18,... | collective-permute-start | bytes 5505032 | tf_op jit(solution)/shard_map/ppermute | solution.py:621
  84.2 1.6 copy-start
  86.9 46.8 %collective-permute-start.5 = (f32[12,128,128]{2,1,0:T(8,128)S(1)}, f32[12,128,128]{2,1,0:T(8,128)S(1)}, u32[]{:S(2)}, u32[]{:S(2)}) collective-permute-start(f32[12,128,128]{2,1,0:T(8,128)S(1)} %slice.3), channel_id=1, source_target_pairs={{1,2},{2,1},{5,6},{6,5},{9,10},{10,9},{13,14},{14,13},{17,18},{18,... | collective-permute-start | bytes 2359304 | tf_op jit(solution)/shard_map/ppermute | solution.py:621
  87.7 46.1 %collective-permute-start.6 = (f32[5,128,128]{2,1,0:T(8,128)}, f32[5,128,128]{2,1,0:T(8,128)S(1)}, u32[]{:S(2)}, u32[]{:S(2)}) collective-permute-start(f32[5,128,128]{2,1,0:T(8,128)} %get-tuple-element.49), channel_id=1, source_target_pairs={{1,0},{2,3},{5,4},{6,7},{9,8},{10,11},{13,12},{14,15},{17,16},{18,... | collective-permute-start | bytes 983048 | tf_op jit(solution)/shard_map/ppermute | solution.py:621
  133.7 0.7 copy-start.5
  133.8 1.0 copy-start.1
  134.7 1.4 copy-start.4
  134.7 53.0 %collective-permute-start.8 = (f32[12,128,128]{2,1,0:T(8,128)}, f32[12,128,128]{2,1,0:T(8,128)S(1)}, u32[]{:S(2)}, u32[]{:S(2)}) collective-permute-start(f32[12,128,128]{2,1,0:T(8,128)} %get-tuple-element.51.refs_2_.refs_4_), channel_id=1, source_target_pairs={{1,0},{2,3},{5,4},{6,7},{9,8},{10,11},{13,12},{14,15},{17,16},{18,... | collective-permute-start | bytes 2359304 | tf_op jit(solution)/shard_map/ppermute | solution.py:621
  137.2 1.7 copy-start.6
  137.2 1.7 collective-permute-start.7
  138.9 0.7 copy-start.8
  187.7 0.9 copy-start.2
  205.4 15.0 %collective-permute-start.10 = (f32[512,2048]{1,0:T(8,128)}, f32[512,2048]{1,0:T(8,128)}, u32[]{:S(2)}, u32[]{:S(2)}) collective-permute-start(f32[512,2048]{1,0:T(8,128)} %get-tuple-element.58.refs_2_.refs_6_), channel_id=1, source_target_pairs={{0,4},{4,0},{8,12},{12,8},{16,20},{20,16},{24,28},{28,24},{1,5},{5... | collective-permute-start | bytes 12582920 | tf_op jit(solution)/shard_map/ppermute | solution.py:659
  205.5 14.9 %collective-permute-start.11 = (f32[512,2048]{1,0:T(8,128)}, f32[512,2048]{1,0:T(8,128)}, u32[]{:S(2)}, u32[]{:S(2)}) collective-permute-start(f32[512,2048]{1,0:T(8,128)} %get-tuple-element.59.refs_4_), channel_id=1, source_target_pairs={{0,4},{4,0},{8,12},{12,8},{16,20},{20,16},{24,28},{28,24},{1,5},{5... | collective-permute-start | bytes 12582920 | tf_op jit(solution)/shard_map/ppermute | solution.py:659
  207.8 6.0 %collective-permute-start.12 = (f32[6,128,128]{2,1,0:T(8,128)}, f32[6,128,128]{2,1,0:T(8,128)S(1)}, u32[]{:S(2)}, u32[]{:S(2)}) collective-permute-start(f32[6,128,128]{2,1,0:T(8,128)} %collect.1.refs_2_), channel_id=1, source_target_pairs={{0,4},{4,0},{8,12},{12,8},{16,20},{20,16},{24,28},{28,24},{1,5},{5... | collective-permute-start | bytes 1179656 | tf_op jit(solution)/shard_map/ppermute | solution.py:659
  213.9 0.7 copy-start.7

commit v2 on v1

--- a/solution.py
+++ b/solution.py
@@ -70,12 +70,12 @@
     return [(i, j) for i in range(n) for j in range(i + 1)]
 
 
-def dense_kernel(blk, step, width, where, acol, bcol, a_ref, b_ref, p_ref, fh, fl, uh, ul, w_ref, buf, turned):
+def dense_kernel(blk, step, width, where, acol, bcol, a_ref, b_ref, fh, fl, uh, ul):
     i = pl.program_id(0)
-    rows = p_ref.shape[0]
-    orders = buf.shape[1] - width
-    buf[...] = jnp.zeros_like(buf)
-    turned[...] = jnp.zeros_like(turned)
+    orders = fh.shape[1] - width
+    group = (uh.shape[0] - orders) // blk
+    for ref in (fh, fl, uh, ul):
+        ref[...] = jnp.zeros_like(ref)
     diag = lax.broadcasted_iota(jnp.int32, (blk, blk), 0) == lax.broadcasted_iota(jnp.int32, (blk, blk), 1)
     eye = jnp.where(diag, 0.75, 0.0).astype(F32)
     for t in range(step // blk):
@@ -84,36 +84,28 @@
         for s in range(a_ref.shape[1]):
             col = acol[0, row, s]
             block = a_ref[t, s] + eye if s == 0 else a_ref[t, s]
-            buf[at, pl.ds(pl.multiple_of(col * blk, blk), blk)] = block
-            local = col - where[0] * (rows // blk)
-
-            @pl.when((local >= 0) & (local < rows // blk))
+            to = pl.ds(pl.multiple_of(col * blk, blk), blk)
+            fh[at, to], fl[at, to] = split(block)
+            local = col - where[0] * group
+
+            @pl.when((local >= 0) & (local < group))
             def _():
-                turned[pl.ds(pl.multiple_of(orders + local * blk, blk), blk), at] = block.T
+                to = pl.ds(pl.multiple_of(orders + local * blk, blk), blk)
+                uh[to, at], ul[to, at] = split(block.T)
 
         for s in range(b_ref.shape[1]):
             col = bcol[0, row, s]
-            buf[at, pl.ds(pl.multiple_of(width + col * blk, blk), blk)] = b_ref[t, s]
-            turned[pl.ds(pl.multiple_of(col * blk, blk), blk), at] = b_ref[t, s].T
-    hi, lo = split(buf[...])
-    fh[...] = hi
-    fl[...] = lo
-    uh[...], ul[...] = split(turned[...])
-    part = dot3(split(p_ref[...]), (hi[:, width:], lo[:, width:]))
-
-    @pl.when(i == 0)
-    def _():
-        w_ref[...] = part
-
-    @pl.when(i > 0)
-    def _():
-        w_ref[...] += part
-
-
-def dense(where, cost_rows, a_blocks, a_cols, b_blocks, b_cols, orders, after):
-    rows, width = cost_rows.shape
-    _, nnza, blk, _ = a_blocks.shape
+            block = b_ref[t, s]
+            to = pl.ds(pl.multiple_of(width + col * blk, blk), blk)
+            fh[at, to], fl[at, to] = split(block)
+            to = pl.ds(pl.multiple_of(col * blk, blk), blk)
+            uh[to, at], ul[to, at] = split(block.T)
+
+
+def dense(where, rows, a_blocks, a_cols, b_blocks, b_cols, orders, after):
+    count, nnza, blk, _ = a_blocks.shape
     nnzb = b_blocks.shape[1]
+    width = count * blk
     step = 2 * blk
     total = width + orders
     factor = pl.BlockSpec((step, total), lambda i, *_: (i, 0))
@@ -125,44 +117,12 @@
         [
             pl.BlockSpec((2, nnza, blk, blk), lambda i, *_: (i, 0, 0, 0)),
             pl.BlockSpec((2, nnzb, blk, blk), lambda i, *_: (i, 0, 0, 0)),
-            pl.BlockSpec((rows, step), lambda i, *_: (0, i)),
         ],
-        [factor, factor, turned, turned, whole(rows, orders)],
-        [((width, total), BF16)] * 2 + [((rows + orders, width), BF16)] * 2 + [((rows, orders), F32)],
+        [factor, factor, turned, turned],
+        [((width, total), BF16)] * 2 + [((rows + orders, width), BF16)] * 2,
         "dense",
-        [pltpu.VMEM((step, total), F32), pltpu.VMEM((rows + orders, step), F32)],
         after=after,
-    )(where, a_cols, b_cols, a_blocks, b_blocks, cost_rows)
-
-
-def gram_kernel(blk, weight, where, bh, bl, w_ref, keep, give):
-    core = where[1]
-    h = dot3((bh[...], bl[...]), split(w_ref[...])) * weight[0]
-    tiles = [h[i * blk : (i + 1) * blk, j * blk : (j + 1) * blk] for i, j in lower(h.shape[0] // blk)]
-    count = len(tiles) // 2
-    for side in range(2):
-
-        @pl.when(core == side)
-        def _():
-            for t in range(count):
-                keep[t] = tiles[side * count + t]
-                give[t] = tiles[(1 - side) * count + t]
-
-
-def gram(weight, where, uh, ul, w, blk, through):
-    rows, orders = w.shape
-    count = len(lower(orders // blk)) // 2
-    turned = pl.BlockSpec((orders, rows), lambda i, weight, where: (0, where[0]))
-    return call(
-        functools.partial(gram_kernel, blk),
-        (1,),
-        2,
-        [turned, turned, whole(rows, orders)],
-        [whole(count, blk, blk)] * 2,
-        [((count, blk, blk), F32)] * 2,
-        "gram",
-        through=through,
-    )(weight, where, uh, ul, w)
+    )(where, a_cols, b_cols, a_blocks, b_blocks)
 
 
 def inverse_block(m):
@@ -202,22 +162,11 @@
     return jnp.concatenate(strips, axis=0)
 
 
-def inverse_kernel(where, mine, other, d_ref, out):
-    half, blk, _ = mine.shape
+def inverse_kernel(blk, mine, other, d_ref, out):
     n = out.shape[0]
     dot = functools.partial(jnp.dot, precision=HIGHEST, preferred_element_type=F32)
-    for side in range(2):
-
-        @pl.when(where[0] == side)
-        def _():
-            for t, (i, j) in enumerate(lower(n // blk)):
-                tile = (mine if t // half == side else other)[t % half]
-                out[i * blk : (i + 1) * blk, j * blk : (j + 1) * blk] = tile
-                if i != j:
-                    out[j * blk : (j + 1) * blk, i * blk : (i + 1) * blk] = tile.T
-
     diag = lax.broadcasted_iota(jnp.int32, (n, n), 0) == lax.broadcasted_iota(jnp.int32, (n, n), 1)
-    out[...] += jnp.where(diag, d_ref[...], 0.0)
+    out[...] = mine[...] + other[...] + jnp.where(diag, d_ref[...], 0.0)
 
     @pl.loop(0, n // blk)
     def _(b):
@@ -231,19 +180,17 @@
         out[here, here] = inv
 
 
-def inverse(where, mine, other, control_cost, after):
-    half, blk, _ = mine.shape
+def inverse(mine, other, control_cost, blk):
     n = control_cost.shape[0]
     return call(
-        inverse_kernel,
+        functools.partial(inverse_kernel, blk),
         (1,),
-        1,
-        [whole(half, blk, blk)] * 2 + [whole(1, n)],
+        0,
+        [whole(n, n)] * 2 + [whole(1, n)],
         [whole(n, n)],
         [((n, n), F32)],
         "inverse",
-        after=after,
-    )(where, mine, other, control_cost[None])[0]
+    )(mine, other, control_cost[None])[0]
 
 
 def tiled(block, blk):
@@ -251,31 +198,42 @@
     return [block[i * blk : (i + 1) * blk, j * blk : (j + 1) * blk] for i in range(n) for j in range(n)]
 
 
-def pack_kernel(blk, where, own, near, inner, far, x_ref, pair_out, mid_out):
+def pack_kernel(blk, where, own, x_ref, *refs):
+    *blocks, out = refs
     diag = [own[i * blk : (i + 1) * blk, j * blk : (j + 1) * blk] for i, j in lower(own.shape[0] // blk)]
     x = [x_ref[0, :blk], x_ref[0, blk:]]
-    for t, tile in enumerate(diag + x + tiled(inner, blk) + tiled(far, blk)):
-        pair_out[t] = tile
-    for t, tile in enumerate(diag + x + tiled(near, blk)):
-        mid_out[t] = tile
-
-
-def pack(where, cost_rows, parent_state, blk):
+    for t, tile in enumerate(diag + x + [tile for block in blocks for tile in tiled(block, blk)]):
+        out[t] = tile
+
+
+def pack(where, cost_rows, parent_state, blk, after):
     rows = cost_rows.shape[0]
     samples = parent_state.shape[2]
-    count, full = len(lower(rows // blk)) + 2, (rows // blk) ** 2
-    specs = [pl.BlockSpec((rows, rows), functools.partial(lambda t, i, where: (0, where[t]), t)) for t in range(4)]
-    specs.append(pl.BlockSpec((1, rows // 2, samples), lambda i, where: (where[4], where[5], 0)))
-    sizes = [count + 2 * full, count + full]
+    picks = [0] + list(range(3, where.shape[0]))
+    size = len(lower(rows // blk)) + 2 + (len(picks) - 1) * (rows // blk) ** 2
+    specs = [pl.BlockSpec((rows, rows), functools.partial(lambda t, i, where: (0, where[t]), t)) for t in picks]
+    specs.insert(1, pl.BlockSpec((1, rows // 2, samples), lambda i, where: (where[1], where[2], 0)))
+    args = [cost_rows] * len(picks)
+    args.insert(1, parent_state)
     return call(
         functools.partial(pack_kernel, blk),
         (1,),
         1,
         specs,
-        [whole(size, blk, blk) for size in sizes],
-        [((size, blk, blk), F32) for size in sizes],
+        [whole(size, blk, blk)],
+        [((size, blk, blk), F32)],
         "pack",
-    )(where, *[cost_rows] * 4, parent_state)
+        after=after,
+    )(where, *args)[0]
+
+
+def front(message, size):
+    shape = (size,) + message.shape[1:]
+
+    def kernel(x, out):
+        out[...] = x[...]
+
+    return call(kernel, (1,), 0, [whole(*shape)], [whole(*shape)], [(shape, F32)], "front")(message)[0]
 
 
 def unpack(tiles, step, n, xh, xl):
@@ -303,7 +261,7 @@
         out[4:6] = mid_last[...]
 
 
-def collect(where, messages):
+def collect(where, messages, after):
     blk = messages[0].shape[1]
     lead = messages[3].shape[0] // 2 - 1
     return call(
@@ -314,6 +272,7 @@
         [whole(6, blk, blk)],
         [((6, blk, blk), F32)],
         "collect",
+        after=[after],
     )(where, *messages)[0]
 
 
@@ -331,7 +290,7 @@
     out[...] = dot3((fh[...], fl[...]), split(x_ref[...]))
 
 
-def drift(where, parent_state, mine, other, fh, fl):
+def drift(where, parent_state, mine, other, fh, fl, after):
     _, rows, samples = parent_state.shape
     count, blk, _ = mine.shape
     width = rows * 4
@@ -346,14 +305,15 @@
         [whole(width, samples), whole(rows, samples)],
         [((width, samples), F32), ((rows, samples), F32)],
         "drift",
+        after=[after],
     )(where, parent_state, mine, other, fh, fl)
 
 
-def passed(arrays, after):
-    return call(lambda *_: None, (1,), 0, [], [], [], "passed", after=[after], through=arrays)()
-
-
-def begin_kernel(steps, where, weight, p_ref, uh, ul, vh, vl, fh, fl, rest, s_out, g_out, mine, hi, lo):
+def passed(arrays, *after):
+    return call(lambda *_: None, (1,), 0, [], [], [], "passed", after=after, through=arrays)()
+
+
+def begin_kernel(steps, where, weight, p_ref, uh, ul, vh, vl, fh, fl, bh, bl, rest, s_out, g_out, h_out, mine, hi, lo):
     g = pl.program_id(0)
 
     @pl.when(g < steps)
@@ -376,6 +336,8 @@
     @pl.when(g == steps)
     def _():
         hi[...], lo[...] = split(mine[...] * weight[0])
+        orders = h_out.shape[0]
+        h_out[...] = dot3((hi[:orders], lo[:orders]), (bh[...], bl[...]))
 
     @pl.when(g >= steps)
     def _():
@@ -385,7 +347,7 @@
         g_out[...] = part[:orders]
 
 
-def begin(where, weight, cost_rows, uh, ul, fh, fl, after):
+def begin(where, weight, cost_rows, uh, ul, fh, fl):
     rows, width = cost_rows.shape
     tall = uh.shape[0]
     orders = tall - rows
@@ -401,30 +363,31 @@
     each = pl.BlockSpec((tall, rows), lambda g, *_: (0, early(g)))
     own = pl.BlockSpec((tall, rows), lambda g, where, _: (0, where[0]))
     factor = pl.BlockSpec((rows, tile), lambda g, where, _: (where[0], late(g)))
+    control = pl.BlockSpec((rows, orders), lambda g, where, _: (where[0], width // orders))
     return call(
         functools.partial(begin_kernel, steps),
         (steps + width // tile,),
         2,
-        [pl.BlockSpec((rows, rows), lambda g, *_: (0, early(g))), each, each, own, own, factor, factor],
+        [pl.BlockSpec((rows, rows), lambda g, *_: (0, early(g))), each, each, own, own, factor, factor, control, control],
         [
             each,
             pl.BlockSpec((rows, tile), lambda g, *_: (0, late(g))),
             pl.BlockSpec((orders, tile), lambda g, *_: (0, late(g))),
+            whole(orders, orders),
         ],
-        [((tall, width), F32), ((rows, width), F32), ((orders, width), F32)],
+        [((tall, width), F32), ((rows, width), F32), ((orders, width), F32), ((orders, orders), F32)],
         "begin",
         [pltpu.VMEM((tall, rows), F32)] + [pltpu.VMEM((tall, rows), BF16)] * 2,
-        after=after,
-    )(where, weight, cost_rows, uh, ul, uh, ul, fh, fl)
+    )(where, weight, cost_rows, uh, ul, uh, ul, fh, fl, fh, fl)
 
 
 def stage_kernel(options, size, where, weight, *refs):
     arrived = refs[:options]
-    vh, vl, n_in, fh, fl, s_in, g_in, *refs = refs[options:]
+    vh, vl, n_in, fh, fl, bh, bl, s_in, g_in, h_in, *refs = refs[options:]
     if size > 1:
-        uh, ul, s_out, g_out, n_out, done, hi, lo, xh, xl = refs
+        uh, ul, s_out, g_out, h_out, n_out, done, hi, lo, xh, xl = refs
     else:
-        s_out, g_out, done, hi, lo, xh, xl = refs
+        s_out, g_out, h_out, done, hi, lo, xh, xl = refs
     g = pl.program_id(0)
     n = xh.shape[0] // arrived[0].shape[1]
     for c in range(options):
@@ -449,6 +412,8 @@
     @pl.when(g == size)
     def _():
         hi[...], lo[...] = split(done[...] * weight[0])
+        orders = h_out.shape[0]
+        h_out[...] = h_in[...] + dot3((hi[:orders], lo[:orders]), (bh[...], bl[...]))
 
     @pl.when(g >= size)
     def _():
@@ -478,6 +443,7 @@
     factor = pl.BlockSpec((rows, tile), lambda g, where, _: (where[1], turn(g)))
     s_spec = pl.BlockSpec((rows, tile), lambda g, *_: (0, turn(g)))
     g_spec = pl.BlockSpec((orders, tile), lambda g, *_: (0, turn(g)))
+    control = pl.BlockSpec((rows, orders), lambda g, where, _: (where[1], width // orders))
     first = 2 + len(arrived)
     more = size > 1
     return call(
@@ -485,16 +451,16 @@
         (size + width // tile,),
         2,
         [whole(*x.shape) for x in arrived]
-        + [focus, focus, block, factor, factor, s_spec, g_spec]
+        + [focus, focus, block, factor, factor, control, control, s_spec, g_spec, whole(orders, orders)]
         + [beyond] * (2 * more),
-        [s_spec, g_spec] + [beyond] * more,
-        [((rows, width), F32), ((orders, width), F32)] + [((tall, width), F32)] * more,
+        [s_spec, g_spec, whole(orders, orders)] + [beyond] * more,
+        [((rows, width), F32), ((orders, width), F32), ((orders, orders), F32)] + [((tall, width), F32)] * more,
         "stage",
         [pltpu.VMEM((tall, rows), F32)] + [pltpu.VMEM((tall, rows), BF16)] * 2 + [pltpu.VMEM((rows, rows), BF16)] * 2,
-        {first + 5: 0, first + 6: 1, **({first + 2: 2} if more else {})},
+        {first + 7: 0, first + 8: 1, first + 9: 2, **({first + 2: 3} if more else {})},
         after,
         through,
-    )(where, weight, *arrived, uh, ul, n, fh, fl, *sums, *([uh, ul] if more else []))
+    )(where, weight, *arrived, uh, ul, n, fh, fl, fh, fl, *sums, *([uh, ul] if more else []))
 
 
 def final_kernel(where, h_ref, g1, g2, s1, s2, q1, q2, d_ref, x_ref, y_ref, bh, bl, gain, out, reached, hi, lo, q):
@@ -611,11 +577,13 @@
     return acc[:, :width], jnp.swapaxes(cross.reshape(width, -1), 0, 1)
 
 
-def by_blocks(z, core, parent, weight, cost_rows, parent_state, dense_parts, control_cost, blk, messages):
-    fh, fl, uh, ul, w = dense_parts
+def by_blocks(z, core, parent, weight, cost_rows, parent_state, dense_parts, control_cost, messages):
+    fh, fl, uh, ul = dense_parts
     edge = ((z == 0) | (z == 3)).astype(jnp.int32)
     left = z < 2
     second, third = jnp.where(left, 2, 1), jnp.where(left, 3, 0)
+    pair, mid = messages
+    lead = 2 * mid.shape[0] - pair.shape[0]
 
     def moved(x, *pairs):
         return lax.ppermute(x, "row", pairs)
@@ -626,32 +594,25 @@
     def to_end(x):
         return moved(x, (1, 0), (2, 3))
 
-    pair = moved(messages[0], (0, 1), (1, 0), (2, 3), (3, 2))
-    mid = across(messages[1])
-    keep, give = gram(weight, jnp.stack([z, core]), uh, ul, w, blk, [])
-    tiles = keep + swapped(give)
-    n, *sums = begin(z[None], weight, cost_rows, uh, ul, fh, fl, [tiles])
-    tiles = tiles + moved(tiles, (0, 1), (3, 2))
-    mid, tiles = passed([mid, tiles], n)
+    pair = moved(pair, (0, 1), (1, 0), (2, 3), (3, 2))
+    mid = across(mid)
+    n, *sums = begin(z[None], weight, cost_rows, uh, ul, fh, fl)
+    (mid,) = passed([mid], n)
     end = to_end(mid)
-    tiles = tiles + across(tiles)
-    pair, tiles = passed([pair, tiles], n)
-    mid_last = across(pair[: len(lower(w.shape[0] // blk)) + 2])
-    finished = to_end(tiles)
+    mid_last = across(front(pair, lead))
     where = jnp.stack([z * 0, z ^ 1, second, third])
     *sums, n = stage(where, weight, [pair], 3, uh, ul, n, fh, fl, sums)
-    mid_last, finished = passed([mid_last, finished], n)
+    (mid_last,) = passed([mid_last], n)
     end_last = to_end(mid_last)
-    tiles = jnp.where(edge == 1, finished, tiles)
-    hinv = inverse(core[None], tiles, swapped(tiles), control_cost, [n])
     where = jnp.stack([edge, second, third])
-    *sums, n = stage(where, weight, [mid, end], 2, uh, ul, n, fh, fl, sums, [hinv])
+    *sums, n = stage(where, weight, [mid, end], 2, uh, ul, n, fh, fl, sums)
+    halves = collect(edge[None], [pair, mid, end, mid_last, end_last], n)
     where = jnp.stack([edge, third])
-    sums = stage(where, weight, [mid_last, end_last], 1, uh, ul, n, fh, fl, sums)
-    halves = collect(edge[None], [pair, mid, end, mid_last, end_last])
+    s, g, h = stage(where, weight, [mid_last, end_last], 1, uh, ul, n, fh, fl, sums, [halves])
     where = jnp.stack([core, z, z ^ 1, second, third, parent])
-    x, y = drift(where, parent_state, halves, swapped(halves), fh, fl)
-    return hinv, sums, x, y
+    x, y = drift(where, parent_state, halves, swapped(halves), fh, fl, h)
+    other = swapped(h)
+    return h, other, passed([s, g], other, y), x, y
 
 
 def swapped(x):
@@ -684,22 +645,24 @@
     if line:
         left = z < 2
         near = jnp.where(left, 0, 3)
-        where = jnp.stack([z, near, jnp.where(left, 2, 1), 3 - near, leaf // 2, core])
-        sent = pack(where, cost_rows, parent_state, blk)
-    parts_of = dense(z[None], cost_rows, a_blocks[0], a_cols, b_blocks[0], b_cols, orders, sent)
-    fh, fl, uh, ul, w = parts_of
+        lead = [z, leaf // 2, core]
+        sent.append(pack(jnp.stack(lead + [jnp.where(left, 2, 1), 3 - near]), cost_rows, parent_state, blk, []))
+        sent.append(pack(jnp.stack(lead + [near]), cost_rows, parent_state, blk, sent))
+    fh, fl, uh, ul = parts_of = dense(z[None], rows, a_blocks[0], a_cols, b_blocks[0], b_cols, orders, sent)
     if line:
-        hinv, own, x, y = by_blocks(
-            z, core, leaf // 2, branch_prob, cost_rows, parent_state, parts_of, control_cost, blk, sent
+        h, other_h, own, x, y = by_blocks(
+            z, core, leaf // 2, branch_prob, cost_rows, parent_state, parts_of, control_cost, sent
         )
     else:
-        keep, give = gram(branch_prob, jnp.stack([z, core]), uh, ul, w, blk, [])
-        tiles = lax.psum(keep + swapped(give), "row")
-        hinv = inverse(core[None], tiles, swapped(tiles), control_cost, [])
+        w = dot3(parted(cost_rows), (fh[:, width:], fl[:, width:]))
+        b_rows = [lax.dynamic_slice(f, (0, z * rows), (orders, rows)) for f in (uh, ul)]
+        h = lax.psum(dot3(b_rows, parted(w)) * branch_prob[0], "row")
+        other_h = swapped(h)
         own = by_images(z, parts, branch_prob, cost_rows, fh, fl)
         own_state = lax.dynamic_index_in_dim(parent_state, leaf // 2, 0, keepdims=False)
         x = lax.all_gather(own_state, "row", tiled=True)
         y = dot3([lax.dynamic_slice(f, (z * rows, 0), (rows, width)) for f in (fh, fl)], parted(x))
+    hinv = inverse(h, other_h, control_cost, blk)
     other = tuple(swapped(x) for x in own)
     gain, pcost, reached = final(z[None], hinv, own, other, state_cost, x, y, fh, fl)
     return pcost[None], gain[None], reached[None]

time: 238 us -> 213 us (0.89)
  waiting for transfers between devices: 26.3 us -> 12.4 us
  starting transfers between devices: 17.2 us -> 9.46 us
  other arithmetic: 7.95 us -> 2.5 us
    ppermute x8 -> x5, waiting for transfers between devices: 19.1 us -> 10.3 us  [moved(): return lax.ppermute(x, 'row', pairs)]
    ppermute x8 -> x5, starting transfers between devices: 16.2 us -> 8.39 us  [moved(): return lax.ppermute(x, 'row', pairs)]
    ppermute x5 -> x4, waiting for transfers between devices: 7.22 us -> 2.03 us  [swapped(): return lax.ppermute(x, 'leaf', [(i, i ^ 1) for i in range(n)])]
    add x3 -> x0, other arithmetic: 4.5 us -> none  [the longest x1 1.76 us: by_blocks(): tiles = tiles + across(tiles)]
    unnamed x24 -> x20, local copies, waits for them, and re-layouts: 6.27 us -> 8.41 us
    pallas_call x14 -> x15, Pallas kernels: 175 us -> 176 us  [call(): return lambda *args: built(*args, *after, *through)]
  transfers between devices with their start and end apart: 13 -> 9, of which waited for: 5 -> 3; matrix products, arithmetic and copies ran while one was open for 5% -> 2% of each run, Pallas kernels for 58% -> 64%
where the time goes in v2:
time: 213 us; the launch traced here: 212 us
  Pallas kernels  176 us (83%)
  waiting for transfers between devices  12.4 us (6%)
  local copies, waits for them, and re-layouts  9.64 us (5%)
  starting transfers between devices  9.46 us (4%)
  other arithmetic  2.5 us (1%)
    pallas_call x15, Pallas kernels, call(): return lambda *args: built(*args, *after, *through)  176 us
    ppermute x5, waiting for transfers between devices, moved(): return lax.ppermute(x, 'row', pairs)  10.3 us
    unnamed x20, local copies, waits for them, and re-layouts  8.41 us
    ppermute x5, starting transfers between devices, moved(): return lax.ppermute(x, 'row', pairs)  8.39 us
  transfers between devices with their start and end apart: 9, of which 3 were waited for; matrix products, arithmetic and copies ran while one was open for 2% of the time, Pallas kernels for 64%

profile of v2, /device:TPU:0, one launch (start us, length us, event | category | flops | bytes accessed | tf_op | source)
XLA Modules:
  0.0 211.8 jit_solution(1544823705607642241)
XLA Ops:
  1.3 4.4 %pack.2.refs_4_.refs_5_ = f32[44,128,128]{2,1,0:T(8,128)} custom-call(s32[5]{0:T(128)} %stack.69.refs_0_, f32[512,2048]{1,0:T(8,128)} %bitcast.17, f32[4,512,128]{2,1,0:T(8,128)} %refs_1_.6, f32[512,2048]{1,0:T(8,128)} %bitcast.18, f32[512,2048]{1,0:T(8,128)} %bitcast.19), custom_call_target="tpu_custom_call" | custom-call | flops 1 | bytes 1 | tf_op jit(solution)/shard_map/pack/pallas_call | solution.py:62
  5.6 3.0 %collective-permute-start = (f32[44,128,128]{2,1,0:T(8,128)}, f32[44,128,128]{2,1,0:T(8,128)S(1)}, u32[]{:S(2)}, u32[]{:S(2)}) collective-permute-start(f32[44,128,128]{2,1,0:T(8,128)} %pack.2.refs_4_.refs_5_), channel_id=1, source_target_pairs={{0,1},{1,0},{2,3},{3,2},{4,5},{5,4},{6,7},{7,6},{8,9},{9,8},{10,11... | collective-permute-start | bytes 8650760 | tf_op jit(solution)/shard_map/ppermute | solution.py:589
  9.2 3.8 %pack.3.refs_6_ = f32[28,128,128]{2,1,0:T(8,128)} custom-call(s32[4]{0:T(128)} %pad_add_fusion.2.refs_0_, f32[512,2048]{1,0:T(8,128)} %bitcast.20, f32[4,512,128]{2,1,0:T(8,128)} %refs_1_.6, f32[512,2048]{1,0:T(8,128)} %bitcast.21, f32[44,128,128]{2,1,0:T(8,128)} %pack.2.refs_4_.refs_5_), custom_call_target="tpu_custom_call" | custom-call | flops 1 | bytes 1 | tf_op jit(solution)/shard_map/pack/pallas_call | solution.py:62
  13.1 1.9 collective-permute-start.3
  16.3 17.1 %dense.1 = (bf16[2048,2560]{1,0:T(8,128)(2,1)}, bf16[2048,2560]{1,0:T(8,128)(2,1)}, bf16[1024,2048]{1,0:T(8,128)(2,1)}, bf16[1024,2048]{1,0:T(8,128)(2,1)}) custom-call(s32[1]{0:T(128)} %bitcast.refs_0_, s32[1,16,8]{2,1,0:T(8,128)} %copy.27.refs_1_, s32[1,16,2]{2,1,0:T(8,128)} %copy.28.refs_2_, f32[16,8,128,128]{3,2,1,0:T(8,128)} %bitcast.23, ...), custom_call_target="tpu_custom_call" | custom-call | flops 1 | bytes 1 | tf_op jit(solution)/shard_map/dense/pallas_call | solution.py:62
  34.1 28.5 %begin.1 = (f32[1024,2048]{1,0:T(8,128)}, f32[512,2048]{1,0:T(8,128)}, f32[512,2048]{1,0:T(8,128)}, f32[512,512]{1,0:T(8,128)}) custom-call(s32[1]{0:T(128)} %bitcast.refs_0_, f32[1]{0:T(128)S(6)} %copy.44.refs_1_, f32[512,2048]{1,0:T(8,128)} %bitcast.22, bf16[1024,2048]{1,0:T(8,128)(2,1)} %get-tuple-element.29.refs_3_.refs_5_.refs_13_.refs_4_.refs_14_, ...), custom_call_target="tpu_custom_call" | custom-call | flops 1 | bytes 1 | tf_op jit(solution)/shard_map/begin/pallas_call | solution.py:62
  62.6 1.3 collective-permute-start.4
  63.9 8.3 %collective-permute-done.refs_2_.refs_0_.refs_1_ = f32[44,128,128]{2,1,0:T(8,128)S(1)} collective-permute-done((f32[44,128,128]{2,1,0:T(8,128)}, f32[44,128,128]{2,1,0:T(8,128)S(1)}, u32[]{:S(2)}, u32[]{:S(2)}) %collective-permute-start) | collective-permute-done | bytes 2883616 | tf_op jit(solution)/shard_map/ppermute | solution.py:589
  72.2 1.6 copy-done
  73.7 2.1 front.1
  77.3 27.9 %stage.3 = (f32[512,2048]{1,0:T(8,128)}, f32[512,2048]{1,0:T(8,128)}, f32[512,512]{1,0:T(8,128)}, f32[1024,2048]{1,0:T(8,128)}) custom-call(s32[4]{0:T(128)} %pad_add_fusion.1.refs_0_, f32[1]{0:T(128)S(6)} %copy.44.refs_1_, f32[44,128,128]{2,1,0:T(8,128)} %copy-done, ...), custom_call_target="tpu_custom_call", output_to_operand_aliasing={{0}: (10, {}), {1}: (11, {}), {2}: (12, {}), {3}: (5, {})} | custom-call | flops 1 | bytes 1 | tf_op jit(solution)/shard_map/stage/pallas_call | solution.py:62
  105.2 0.9 copy-done.2
  106.1 1.3 collective-permute-start.2
  108.7 2.1 collective-permute-done.4.refs_3_
  110.8 24.2 %stage.4 = (f32[512,2048]{1,0:T(8,128)}, f32[512,2048]{1,0:T(8,128)}, f32[512,512]{1,0:T(8,128)}, f32[1024,2048]{1,0:T(8,128)}) custom-call(s32[3]{0:T(128)} %pad_add_fusion.3.refs_0_, f32[1]{0:T(128)S(6)} %copy.44.refs_1_, f32[28,128,128]{2,1,0:T(8,128)} %passed.4.refs_2_, ...), custom_call_target="tpu_custom_call", output_to_operand_aliasing={{0}: (11, {}), {1}: (12, {}), {2}: (13, {}), {3}: (6, {})} | custom-call | flops 1 | bytes 1 | tf_op jit(solution)/shard_map/stage/pallas_call | solution.py:62
  135.0 0.9 copy-done.5
  135.9 2.2 %collect.1.refs_14_.refs_2_ = f32[6,128,128]{2,1,0:T(8,128)} custom-call(s32[1]{0:T(128)} %bitcast.1.refs_0_, f32[44,128,128]{2,1,0:T(8,128)} %copy-done, f32[28,128,128]{2,1,0:T(8,128)} %passed.4.refs_2_, f32[28,128,128]{2,1,0:T(8,128)} %collective-permute-done.4.refs_3_, f32[12,128,128]{2,1,0:T(8,128)} %passed.3.refs_4_.refs_2_, ...), custom_call_target="tpu_custom_call" | custom-call | flops 1 | bytes 1 | tf_op jit(solution)/shard_map/collect/pallas_call | solution.py:62
  138.1 18.5 %stage.5 = (f32[512,2048]{1,0:T(8,128)}, f32[512,2048]{1,0:T(8,128)}, f32[512,512]{1,0:T(8,128)}) custom-call(s32[2]{0:T(128)} %pad_add_fusion.refs_0_, f32[1]{0:T(128)S(6)} %copy.44.refs_1_, f32[12,128,128]{2,1,0:T(8,128)} %passed.3.refs_4_.refs_2_, f32[12,128,128]{2,1,0:T(8,128)} %copy-done.5, ...), custom_call_target="tpu_custom_call", output_to_operand_aliasing={{0}: (11, {}), {1}: (12, {}), {2}: (13, {})} | custom-call | flops 1 | bytes 1 | tf_op jit(solution)/shard_map/stage/pallas_call | solution.py:62
  157.7 2.0 collective-permute-done.6.refs_3_
  160.5 5.8 %drift.1 = (f32[2048,128]{1,0:T(8,128)}, f32[512,128]{1,0:T(8,128)}) custom-call(s32[6]{0:T(128)} %stack.73.refs_0_, f32[4,512,128]{2,1,0:T(8,128)} %refs_1_.6, f32[6,128,128]{2,1,0:T(8,128)} %collect.1.refs_14_.refs_2_, f32[6,128,128]{2,1,0:T(8,128)} %copy-done.6, bf16[2048,2560]{1,0:T(8,128)(2,1)} %get-tuple-element.31.refs_7_.refs_9_.refs_6_.refs_8_.refs_4_.refs_11_, ...), custom_call_target="tpu_custom_call" | custom-call | flops 1 | bytes 1 | tf_op jit(solution)/shard_map/drift/pallas_call | solution.py:62
  166.3 1.0 copy-done.3
  167.8 25.7 %inverse.1.refs_1_ = f32[512,512]{1,0:T(8,128)} custom-call(f32[512,512]{1,0:T(8,128)} %get-tuple-element.45.refs_0_.refs_6_, f32[512,512]{1,0:T(8,128)} %copy-done.3, f32[1,512]{1,0:T(1,128)} %bitcast.26), custom_call_target="tpu_custom_call" | custom-call | flops 1 | bytes 1 | tf_op jit(solution)/shard_map/inverse/pallas_call | solution.py:62
  193.5 2.0 copy-done.1
  195.6 16.1 %final.1 = (f32[512,512]{1,0:T(8,128)}, f32[512,2048]{1,0:T(8,128)}, f32[512,128]{1,0:T(8,128)}) custom-call(s32[1]{0:T(128)} %bitcast.refs_0_, f32[512,512]{1,0:T(8,128)} %inverse.1.refs_1_, f32[512,2048]{1,0:T(8,128)} %get-tuple-element.49.refs_2_.refs_6_, f32[512,2048]{1,0:T(8,128)} %copy-done.1, f32[512,2048]{1,0:T(8,128)} %get-tuple-element.50.refs_4_, ...), custom_call_target="tpu_custom_call" | custom-call | flops 1 | bytes 1 | tf_op jit(solution)/shard_map/final/pallas_call | solution.py:62
  (35 shorter events, 7.8 us)
Async XLA Ops:
  5.6 66.5 %collective-permute-start = (f32[44,128,128]{2,1,0:T(8,128)}, f32[44,128,128]{2,1,0:T(8,128)S(1)}, u32[]{:S(2)}, u32[]{:S(2)}) collective-permute-start(f32[44,128,128]{2,1,0:T(8,128)} %pack.2.refs_4_.refs_5_), channel_id=1, source_target_pairs={{0,1},{1,0},{2,3},{3,2},{4,5},{5,4},{6,7},{7,6},{8,9},{9,8},{10,11... | collective-permute-start | bytes 8650760 | tf_op jit(solution)/shard_map/ppermute | solution.py:589
  9.2 5.8 %copy-start.7 = (s32[1,16,8]{1,2,0:T(8,128)S(1)}, s32[1,16,8]{1,2,0:T(8,128)}, u32[]{:S(2)}) copy-start(s32[1,16,8]{1,2,0:T(8,128)} %param.11) | copy-start | bytes 1540
  9.2 6.4 %copy-start.8 = (s32[1,16,2]{1,2,0:T(2,128)S(1)}, s32[1,16,2]{1,2,0:T(2,128)}, u32[]{:S(2)}) copy-start(s32[1,16,2]{1,2,0:T(2,128)} %param.13) | copy-start | bytes 388
  13.1 49.5 %collective-permute-start.3 = (f32[28,128,128]{2,1,0:T(8,128)}, f32[28,128,128]{2,1,0:T(8,128)}, u32[]{:S(2)}, u32[]{:S(2)}) collective-permute-start(f32[28,128,128]{2,1,0:T(8,128)} %pack.3.refs_6_), channel_id=1, source_target_pairs={{1,2},{2,1},{5,6},{6,5},{9,10},{10,9},{13,14},{14,13},{17,18},{18,... | collective-permute-start | bytes 5505032 | tf_op jit(solution)/shard_map/ppermute | solution.py:589
  62.6 48.2 %collective-permute-start.4 = (f32[28,128,128]{2,1,0:T(8,128)}, f32[28,128,128]{2,1,0:T(8,128)}, u32[]{:S(2)}, u32[]{:S(2)}) collective-permute-start(f32[28,128,128]{2,1,0:T(8,128)} %passed.4.refs_2_), channel_id=1, source_target_pairs={{1,0},{2,3},{5,4},{6,7},{9,8},{10,11},{13,12},{14,15},{17,16},{18,... | collective-permute-start | bytes 5505032 | tf_op jit(solution)/shard_map/ppermute | solution.py:589
  72.2 1.6 copy-start
  75.8 29.4 %collective-permute-start.1 = (f32[12,128,128]{2,1,0:T(8,128)}, f32[12,128,128]{2,1,0:T(8,128)S(1)}, u32[]{:S(2)}, u32[]{:S(2)}) collective-permute-start(f32[12,128,128]{2,1,0:T(8,128)} %front.1), channel_id=1, source_target_pairs={{1,2},{2,1},{5,6},{6,5},{9,10},{10,9},{13,14},{14,13},{17,18},{18,... | collective-permute-start | bytes 2359304 | tf_op jit(solution)/shard_map/ppermute | solution.py:589
  105.2 0.9 copy-start.2
  106.1 28.9 %collective-permute-start.2 = (f32[12,128,128]{2,1,0:T(8,128)}, f32[12,128,128]{2,1,0:T(8,128)S(1)}, u32[]{:S(2)}, u32[]{:S(2)}) collective-permute-start(f32[12,128,128]{2,1,0:T(8,128)} %passed.3.refs_4_.refs_2_), channel_id=1, source_target_pairs={{1,0},{2,3},{5,4},{6,7},{9,8},{10,11},{13,12},{14,15},{17,16},{18,... | collective-permute-start | bytes 2359304 | tf_op jit(solution)/shard_map/ppermute | solution.py:589
  135.0 0.9 copy-start.5
  138.1 18.5 %copy-start.4 = (f32[6,128,128]{2,1,0:T(8,128)S(1)}, f32[6,128,128]{2,1,0:T(8,128)}, u32[]{:S(2)}) copy-start(f32[6,128,128]{2,1,0:T(8,128)} %collect.1.refs_14_.refs_2_) | copy-start | bytes 1179652
  156.5 9.8 %collective-permute-start.5 = (f32[512,512]{1,0:T(8,128)}, f32[512,512]{1,0:T(8,128)S(1)}, u32[]{:S(2)}, u32[]{:S(2)}) collective-permute-start(f32[512,512]{1,0:T(8,128)} %get-tuple-element.45.refs_0_.refs_6_), channel_id=1, source_target_pairs={{0,4},{4,0},{8,12},{12,8},{16,20},{20,16},{24,28},{28,24},{1,5},{5... | collective-permute-start | bytes 3145736 | tf_op jit(solution)/shard_map/ppermute | solution.py:620
  156.6 3.1 %collective-permute-start.6 = (f32[6,128,128]{2,1,0:T(8,128)S(1)}, f32[6,128,128]{2,1,0:T(8,128)S(1)}, u32[]{:S(2)}, u32[]{:S(2)}) collective-permute-start(f32[6,128,128]{2,1,0:T(8,128)S(1)} %copy-done.4), channel_id=1, source_target_pairs={{0,4},{4,0},{8,12},{12,8},{16,20},{20,16},{24,28},{28,24},{1,5},{5... | collective-permute-start | bytes 1179656 | tf_op jit(solution)/shard_map/ppermute | solution.py:620
  159.8 0.7 copy-start.6
  166.3 1.0 copy-start.3
  167.3 26.3 %collective-permute-start.7 = (f32[512,2048]{1,0:T(8,128)}, f32[512,2048]{1,0:T(8,128)S(1)}, u32[]{:S(2)}, u32[]{:S(2)}) collective-permute-start(f32[512,2048]{1,0:T(8,128)} %get-tuple-element.49.refs_2_.refs_6_), channel_id=1, source_target_pairs={{0,4},{4,0},{8,12},{12,8},{16,20},{20,16},{24,28},{28,24},{1,5},{5... | collective-permute-start | bytes 12582920 | tf_op jit(solution)/shard_map/ppermute | solution.py:620
  167.4 26.1 %collective-permute-start.8 = (f32[512,2048]{1,0:T(8,128)}, f32[512,2048]{1,0:T(8,128)}, u32[]{:S(2)}, u32[]{:S(2)}) collective-permute-start(f32[512,2048]{1,0:T(8,128)} %get-tuple-element.50.refs_4_), channel_id=1, source_target_pairs={{0,4},{4,0},{8,12},{12,8},{16,20},{20,16},{24,28},{28,24},{1,5},{5... | collective-permute-start | bytes 12582920 | tf_op jit(solution)/shard_map/ppermute | solution.py:620
  193.5 2.0 copy-start.1

commit v3 on v2

--- a/solution.py
+++ b/solution.py
@@ -10,7 +10,7 @@
 HIGHEST = lax.Precision.HIGHEST
 F32 = jnp.float32
 BF16 = jnp.bfloat16
-VMEM_LIMIT = 56 * 2**20
+VMEM_LIMIT = 62 * 2**20
 NN = (((1,), (0,)), ((), ()))
 NT = (((1,), (1,)), ((), ()))
 
@@ -27,7 +27,10 @@
 
 def dot3(a, b, dims=NN):
     one = functools.partial(lax.dot_general, dimension_numbers=dims, preferred_element_type=F32)
-    return one(a[0], b[0]) + (one(a[0], b[1]) + one(a[1], b[0]))
+    rows = a[0].shape[0]
+    both = jnp.concatenate(a, axis=0) if isinstance(a, (tuple, list)) else a.reshape(2 * rows, a.shape[2])
+    part = one(both, b[0])
+    return part[:rows] + (part[rows:] + one(a[0], b[1]))
 
 
 def call(kernel, grid, prefetch, ins, outs, shapes, name, scratch=(), aliases=None, after=(), through=()):
@@ -70,11 +73,11 @@
     return [(i, j) for i in range(n) for j in range(i + 1)]
 
 
-def dense_kernel(blk, step, width, where, acol, bcol, a_ref, b_ref, fh, fl, uh, ul):
+def dense_kernel(blk, step, width, where, acol, bcol, a_ref, b_ref, fh, fl, u):
     i = pl.program_id(0)
     orders = fh.shape[1] - width
-    group = (uh.shape[0] - orders) // blk
-    for ref in (fh, fl, uh, ul):
+    group = (u.shape[1] - orders) // blk
+    for ref in (fh, fl, u):
         ref[...] = jnp.zeros_like(ref)
     diag = lax.broadcasted_iota(jnp.int32, (blk, blk), 0) == lax.broadcasted_iota(jnp.int32, (blk, blk), 1)
     eye = jnp.where(diag, 0.75, 0.0).astype(F32)
@@ -91,7 +94,7 @@
             @pl.when((local >= 0) & (local < group))
             def _():
                 to = pl.ds(pl.multiple_of(orders + local * blk, blk), blk)
-                uh[to, at], ul[to, at] = split(block.T)
+                u[0, to, at], u[1, to, at] = split(block.T)
 
         for s in range(b_ref.shape[1]):
             col = bcol[0, row, s]
@@ -99,7 +102,7 @@
             to = pl.ds(pl.multiple_of(width + col * blk, blk), blk)
             fh[at, to], fl[at, to] = split(block)
             to = pl.ds(pl.multiple_of(col * blk, blk), blk)
-            uh[to, at], ul[to, at] = split(block.T)
+            u[0, to, at], u[1, to, at] = split(block.T)
 
 
 def dense(where, rows, a_blocks, a_cols, b_blocks, b_cols, orders, after):
@@ -109,7 +112,7 @@
     step = 2 * blk
     total = width + orders
     factor = pl.BlockSpec((step, total), lambda i, *_: (i, 0))
-    turned = pl.BlockSpec((rows + orders, step), lambda i, *_: (0, i))
+    turned = pl.BlockSpec((2, rows + orders, step), lambda i, *_: (0, 0, i))
     return call(
         functools.partial(dense_kernel, blk, step, width),
         (width // step,),
@@ -118,8 +121,8 @@
             pl.BlockSpec((2, nnza, blk, blk), lambda i, *_: (i, 0, 0, 0)),
             pl.BlockSpec((2, nnzb, blk, blk), lambda i, *_: (i, 0, 0, 0)),
         ],
-        [factor, factor, turned, turned],
-        [((width, total), BF16)] * 2 + [((rows + orders, width), BF16)] * 2,
+        [factor, factor, turned],
+        [((width, total), BF16)] * 2 + [((2, rows + orders, width), BF16)],
         "dense",
         after=after,
     )(where, a_cols, b_cols, a_blocks, b_blocks)
@@ -168,14 +171,16 @@
     diag = lax.broadcasted_iota(jnp.int32, (n, n), 0) == lax.broadcasted_iota(jnp.int32, (n, n), 1)
     out[...] = mine[...] + other[...] + jnp.where(diag, d_ref[...], 0.0)
 
+    place = lax.broadcasted_iota(jnp.int32, (n, blk), 0) // blk
+
     @pl.loop(0, n // blk)
     def _(b):
         here = pl.ds(pl.multiple_of(b * blk, blk), blk)
         inv = inverse_block(out[here, here])
         row = dot(inv, out[here, :])
-        col = out[:, here]
-        out[...] -= dot(col, row)
-        out[:, here] = -dot(col, inv)
+        out[...] -= dot(out[:, here], row)
+        col = row.T
+        out[:, here] = jnp.where(place < b, col, -col)
         out[here, :] = row
         out[here, here] = inv
 
@@ -277,33 +282,47 @@
 
 
 def drift_kernel(where, own, mine, other, fh, fl, x_ref, out):
+    g = pl.program_id(0)
+    core = where[0]
     blk = mine.shape[1]
     rows = own.shape[1]
-    core = where[0]
-    x_ref[pl.ds(pl.multiple_of(where[1] * rows, rows), rows)] = own[0]
+
+    @pl.when(g == 0)
+    def _():
+        x_ref[...] = own[0]
+
     for d in range(3):
-        for t in range(2):
-            base = where[2 + d] * rows + t * blk
-            half = rows // 2
-            x_ref[pl.ds(pl.multiple_of(base + core * half, blk), blk)] = mine[2 * d + t]
-            x_ref[pl.ds(pl.multiple_of(base + (1 - core) * half, blk), blk)] = other[2 * d + t]
-    out[...] = dot3((fh[...], fl[...]), split(x_ref[...]))
+
+        @pl.when(g == d + 1)
+        def _():
+            for t in range(2):
+                x_ref[pl.ds(pl.multiple_of(core * (rows // 2) + t * blk, blk), blk)] = mine[2 * d + t]
+                x_ref[pl.ds(pl.multiple_of((1 - core) * (rows // 2) + t * blk, blk), blk)] = other[2 * d + t]
+
+    part = dot3((fh[...], fl[...]), split(x_ref[...]))
+
+    @pl.when(g == 0)
+    def _():
+        out[...] = part
+
+    @pl.when(g > 0)
+    def _():
+        out[...] += part
 
 
 def drift(where, parent_state, mine, other, fh, fl, after):
     _, rows, samples = parent_state.shape
     count, blk, _ = mine.shape
-    width = rows * 4
-    factor = pl.BlockSpec((rows, width), lambda i, where: (where[1], 0))
+    factor = pl.BlockSpec((rows, rows), lambda g, where: (where[1], where[1 + g]))
     return call(
         drift_kernel,
-        (1,),
+        (4,),
         1,
-        [pl.BlockSpec((1, rows, samples), lambda i, where: (where[5], 0, 0))]
+        [pl.BlockSpec((1, rows, samples), lambda g, where: (where[5], 0, 0))]
         + [whole(count, blk, blk)] * 2
         + [factor, factor],
-        [whole(width, samples), whole(rows, samples)],
-        [((width, samples), F32), ((rows, samples), F32)],
+        [pl.BlockSpec((rows, samples), lambda g, where: (where[1 + g], 0)), whole(rows, samples)],
+        [((4 * rows, samples), F32), ((rows, samples), F32)],
         "drift",
         after=[after],
     )(where, parent_state, mine, other, fh, fl)
@@ -313,13 +332,13 @@
     return call(lambda *_: None, (1,), 0, [], [], [], "passed", after=after, through=arrays)()
 
 
-def begin_kernel(steps, where, weight, p_ref, uh, ul, vh, vl, fh, fl, bh, bl, rest, s_out, g_out, h_out, mine, hi, lo):
+def begin_kernel(steps, where, weight, p_ref, u, v, fh, fl, bh, bl, rest, s_out, g_out, h_out, mine, pair):
     g = pl.program_id(0)
 
     @pl.when(g < steps)
     def _():
         p = split(p_ref[...])
-        part = dot3((uh[...], ul[...]), p, NT)
+        part = dot3(u[...], p, NT)
 
         @pl.when(g == 0)
         def _():
@@ -331,25 +350,25 @@
 
         @pl.when(g != where[0])
         def _():
-            rest[...] = dot3((vh[...], vl[...]), p)
+            rest[...] = dot3(v[...], p)
 
     @pl.when(g == steps)
     def _():
-        hi[...], lo[...] = split(mine[...] * weight[0])
+        pair[0], pair[1] = split(mine[...] * weight[0])
         orders = h_out.shape[0]
-        h_out[...] = dot3((hi[:orders], lo[:orders]), (bh[...], bl[...]))
+        h_out[...] = dot3(pair[:, :orders], (bh[...], bl[...]))
 
     @pl.when(g >= steps)
     def _():
-        part = dot3((hi[...], lo[...]), (fh[...], fl[...]))
+        part = dot3(pair[...], (fh[...], fl[...]))
         orders = g_out.shape[0]
         s_out[...] = part[orders:]
         g_out[...] = part[:orders]
 
 
-def begin(where, weight, cost_rows, uh, ul, fh, fl):
+def begin(where, weight, cost_rows, u, fh, fl):
     rows, width = cost_rows.shape
-    tall = uh.shape[0]
+    tall = u.shape[1]
     orders = tall - rows
     steps = width // rows
     tile = 512
@@ -360,34 +379,34 @@
     def late(g):
         return jnp.maximum(g - steps, 0)
 
-    each = pl.BlockSpec((tall, rows), lambda g, *_: (0, early(g)))
-    own = pl.BlockSpec((tall, rows), lambda g, where, _: (0, where[0]))
+    each = pl.BlockSpec((2, tall, rows), lambda g, *_: (0, 0, early(g)))
+    own = pl.BlockSpec((2, tall, rows), lambda g, where, _: (0, 0, where[0]))
     factor = pl.BlockSpec((rows, tile), lambda g, where, _: (where[0], late(g)))
     control = pl.BlockSpec((rows, orders), lambda g, where, _: (where[0], width // orders))
     return call(
         functools.partial(begin_kernel, steps),
         (steps + width // tile,),
         2,
-        [pl.BlockSpec((rows, rows), lambda g, *_: (0, early(g))), each, each, own, own, factor, factor, control, control],
+        [pl.BlockSpec((rows, rows), lambda g, *_: (0, early(g))), each, own, factor, factor, control, control],
         [
-            each,
+            pl.BlockSpec((tall, rows), lambda g, *_: (0, early(g))),
             pl.BlockSpec((rows, tile), lambda g, *_: (0, late(g))),
             pl.BlockSpec((orders, tile), lambda g, *_: (0, late(g))),
             whole(orders, orders),
         ],
         [((tall, width), F32), ((rows, width), F32), ((orders, width), F32), ((orders, orders), F32)],
         "begin",
-        [pltpu.VMEM((tall, rows), F32)] + [pltpu.VMEM((tall, rows), BF16)] * 2,
-    )(where, weight, cost_rows, uh, ul, uh, ul, fh, fl, fh, fl)
+        [pltpu.VMEM((tall, rows), F32), pltpu.VMEM((2, tall, rows), BF16)],
+    )(where, weight, cost_rows, u, u, fh, fl, fh, fl)
 
 
 def stage_kernel(options, size, where, weight, *refs):
     arrived = refs[:options]
-    vh, vl, n_in, fh, fl, bh, bl, s_in, g_in, h_in, *refs = refs[options:]
+    v, n_in, fh, fl, bh, bl, s_in, g_in, h_in, *refs = refs[options:]
     if size > 1:
-        uh, ul, s_out, g_out, h_out, n_out, done, hi, lo, xh, xl = refs
+        u, s_out, g_out, h_out, n_out, done, pair, xh, xl = refs
     else:
-        s_out, g_out, h_out, done, hi, lo, xh, xl = refs
+        s_out, g_out, h_out, done, pair, xh, xl = refs
     g = pl.program_id(0)
     n = xh.shape[0] // arrived[0].shape[1]
     for c in range(options):
@@ -399,31 +418,31 @@
 
     @pl.when(g == 0)
     def _():
-        done[...] = n_in[...] + dot3((vh[...], vl[...]), (xh[...], xl[...]))
+        done[...] = n_in[...] + dot3(v[...], (xh[...], xl[...]))
 
     if size > 1:
 
         @pl.when((g > 0) & (g < size))
         def _():
             x = xh[...], xl[...]
-            done[...] += dot3((uh[...], ul[...]), x, NT)
-            n_out[...] = n_in[...] + dot3((vh[...], vl[...]), x)
+            done[...] += dot3(u[...], x, NT)
+            n_out[...] = n_in[...] + dot3(v[...], x)
 
     @pl.when(g == size)
     def _():
-        hi[...], lo[...] = split(done[...] * weight[0])
+        pair[0], pair[1] = split(done[...] * weight[0])
         orders = h_out.shape[0]
-        h_out[...] = h_in[...] + dot3((hi[:orders], lo[:orders]), (bh[...], bl[...]))
+        h_out[...] = h_in[...] + dot3(pair[:, :orders], (bh[...], bl[...]))
 
     @pl.when(g >= size)
     def _():
-        part = dot3((hi[...], lo[...]), (fh[...], fl[...]))
+        part = dot3(pair[...], (fh[...], fl[...]))
         orders = g_out.shape[0]
         s_out[...] = s_in[...] + part[orders:]
         g_out[...] = g_in[...] + part[:orders]
 
 
-def stage(where, weight, arrived, size, uh, ul, n, fh, fl, sums, after=(), through=()):
+def stage(where, weight, arrived, size, u, n, fh, fl, sums, after=(), through=()):
     tall, width = n.shape
     rows, orders = sums[0].shape[0], sums[1].shape[0]
     tile = 512
@@ -439,7 +458,8 @@
 
     block = pl.BlockSpec((tall, rows), lambda g, where, _: (0, place(g, where)))
     beyond = pl.BlockSpec((tall, rows), lambda g, where, _: (0, later(g, where)))
-    focus = pl.BlockSpec((tall, rows), lambda g, where, _: (0, where[1]))
+    u_beyond = pl.BlockSpec((2, tall, rows), lambda g, where, _: (0, 0, later(g, where)))
+    u_focus = pl.BlockSpec((2, tall, rows), lambda g, where, _: (0, 0, where[1]))
     factor = pl.BlockSpec((rows, tile), lambda g, where, _: (where[1], turn(g)))
     s_spec = pl.BlockSpec((rows, tile), lambda g, *_: (0, turn(g)))
     g_spec = pl.BlockSpec((orders, tile), lambda g, *_: (0, turn(g)))
@@ -451,19 +471,19 @@
         (size + width // tile,),
         2,
         [whole(*x.shape) for x in arrived]
-        + [focus, focus, block, factor, factor, control, control, s_spec, g_spec, whole(orders, orders)]
-        + [beyond] * (2 * more),
+        + [u_focus, block, factor, factor, control, control, s_spec, g_spec, whole(orders, orders)]
+        + [u_beyond] * more,
         [s_spec, g_spec, whole(orders, orders)] + [beyond] * more,
         [((rows, width), F32), ((orders, width), F32), ((orders, orders), F32)] + [((tall, width), F32)] * more,
         "stage",
-        [pltpu.VMEM((tall, rows), F32)] + [pltpu.VMEM((tall, rows), BF16)] * 2 + [pltpu.VMEM((rows, rows), BF16)] * 2,
-        {first + 7: 0, first + 8: 1, first + 9: 2, **({first + 2: 3} if more else {})},
+        [pltpu.VMEM((tall, rows), F32), pltpu.VMEM((2, tall, rows), BF16)] + [pltpu.VMEM((rows, rows), BF16)] * 2,
+        {first + 6: 0, first + 7: 1, first + 8: 2, **({first + 1: 3} if more else {})},
         after,
         through,
-    )(where, weight, *arrived, uh, ul, n, fh, fl, fh, fl, *sums, *([uh, ul] if more else []))
-
-
-def final_kernel(where, h_ref, g1, g2, s1, s2, q1, q2, d_ref, x_ref, y_ref, bh, bl, gain, out, reached, hi, lo, q):
+    )(where, weight, *arrived, u, n, fh, fl, fh, fl, *sums, *([u] if more else []))
+
+
+def final_kernel(where, h_ref, g1, g2, s1, s2, q1, q2, d_ref, x_ref, y_ref, bh, bl, gain, out, reached, pair, q):
     n = pl.program_id(0)
     rows = out.shape[0]
 
@@ -471,11 +491,11 @@
     def _():
         value = -dot3(split(h_ref[...]), split(g1[...] + g2[...]))
         gain[...] = value
-        hi[...], lo[...] = split(value.T)
+        pair[0], pair[1] = split(value.T)
         q[...] = jnp.zeros_like(q)
 
     cross = split(q1[...] + q2[...])
-    part = s1[...] + s2[...] + dot3((hi[...], lo[...]), cross)
+    part = s1[...] + s2[...] + dot3(pair[...], cross)
     diag = lax.broadcasted_iota(jnp.int32, (rows, rows), 0) == lax.broadcasted_iota(jnp.int32, (rows, rows), 1)
     out[...] = part + jnp.where(diag & (n == where[0]), d_ref[...], 0.0)
     q[...] += dot3(cross, split(x_ref[...]))
@@ -503,7 +523,7 @@
         [whole(orders, rows), s_spec, whole(rows, samples)],
         [((orders, rows), F32), ((rows, width), F32), ((rows, samples), F32)],
         "final",
-        [pltpu.VMEM((rows, orders), BF16)] * 2 + [pltpu.VMEM((orders, samples), F32)],
+        [pltpu.VMEM((2, rows, orders), BF16), pltpu.VMEM((orders, samples), F32)],
     )(where, hinv, own[1], other[1], own[0], other[0], own[1], other[1], state_cost[None], x, y, fh, fl)
 
 
@@ -578,7 +598,7 @@
 
 
 def by_blocks(z, core, parent, weight, cost_rows, parent_state, dense_parts, control_cost, messages):
-    fh, fl, uh, ul = dense_parts
+    fh, fl, u = dense_parts
     edge = ((z == 0) | (z == 3)).astype(jnp.int32)
     left = z < 2
     second, third = jnp.where(left, 2, 1), jnp.where(left, 3, 0)
@@ -596,19 +616,19 @@
 
     pair = moved(pair, (0, 1), (1, 0), (2, 3), (3, 2))
     mid = across(mid)
-    n, *sums = begin(z[None], weight, cost_rows, uh, ul, fh, fl)
+    n, *sums = begin(z[None], weight, cost_rows, u, fh, fl)
     (mid,) = passed([mid], n)
     end = to_end(mid)
     mid_last = across(front(pair, lead))
     where = jnp.stack([z * 0, z ^ 1, second, third])
-    *sums, n = stage(where, weight, [pair], 3, uh, ul, n, fh, fl, sums)
+    *sums, n = stage(where, weight, [pair], 3, u, n, fh, fl, sums)
     (mid_last,) = passed([mid_last], n)
     end_last = to_end(mid_last)
     where = jnp.stack([edge, second, third])
-    *sums, n = stage(where, weight, [mid, end], 2, uh, ul, n, fh, fl, sums)
+    *sums, n = stage(where, weight, [mid, end], 2, u, n, fh, fl, sums)
     halves = collect(edge[None], [pair, mid, end, mid_last, end_last], n)
     where = jnp.stack([edge, third])
-    s, g, h = stage(where, weight, [mid_last, end_last], 1, uh, ul, n, fh, fl, sums, [halves])
+    s, g, h = stage(where, weight, [mid_last, end_last], 1, u, n, fh, fl, sums, [halves])
     where = jnp.stack([core, z, z ^ 1, second, third, parent])
     x, y = drift(where, parent_state, halves, swapped(halves), fh, fl, h)
     other = swapped(h)
@@ -648,14 +668,14 @@
         lead = [z, leaf // 2, core]
         sent.append(pack(jnp.stack(lead + [jnp.where(left, 2, 1), 3 - near]), cost_rows, parent_state, blk, []))
         sent.append(pack(jnp.stack(lead + [near]), cost_rows, parent_state, blk, sent))
-    fh, fl, uh, ul = parts_of = dense(z[None], rows, a_blocks[0], a_cols, b_blocks[0], b_cols, orders, sent)
+    fh, fl, u = parts_of = dense(z[None], rows, a_blocks[0], a_cols, b_blocks[0], b_cols, orders, sent)
     if line:
         h, other_h, own, x, y = by_blocks(
             z, core, leaf // 2, branch_prob, cost_rows, parent_state, parts_of, control_cost, sent
         )
     else:
         w = dot3(parted(cost_rows), (fh[:, width:], fl[:, width:]))
-        b_rows = [lax.dynamic_slice(f, (0, z * rows), (orders, rows)) for f in (uh, ul)]
+        b_rows = [lax.dynamic_slice(f, (0, z * rows), (orders, rows)) for f in u]
         h = lax.psum(dot3(b_rows, parted(w)) * branch_prob[0], "row")
         other_h = swapped(h)
         own = by_images(z, parts, branch_prob, cost_rows, fh, fl)

time: 213 us -> 212 us (level)
  local copies, waits for them, and re-layouts: 9.64 us -> 6.88 us
  waiting for transfers between devices: 12.4 us -> 14.6 us
    unnamed x20 -> x16, local copies, waits for them, and re-layouts: 8.41 us -> 5.54 us
    ppermute x5, waiting for transfers between devices: 10.3 us -> 12.6 us  [moved(): return lax.ppermute(x, 'row', pairs)]
where the time goes in v3:
time: 212 us; the launch traced here: 211 us
  Pallas kernels  176 us (83%)
  waiting for transfers between devices  14.6 us (7%)
  starting transfers between devices  9.15 us (4%)
  local copies, waits for them, and re-layouts  6.88 us (3%)
  other arithmetic  2.46 us (1%)
    pallas_call x15, Pallas kernels, call(): return lambda *args: built(*args, *after, *through)  176 us
    ppermute x5, waiting for transfers between devices, moved(): return lax.ppermute(x, 'row', pairs)  12.6 us
    ppermute x5, starting transfers between devices, moved(): return lax.ppermute(x, 'row', pairs)  8.08 us
    unnamed x16, local copies, waits for them, and re-layouts  5.54 us
  transfers between devices with their start and end apart: 9, of which 3 were waited for; matrix products, arithmetic and copies ran while one was open for 2% of the time, Pallas kernels for 64%

profile of v3, /device:TPU:0, one launch (start us, length us, event | category | flops | bytes accessed | tf_op | source)
XLA Modules:
  0.0 210.9 jit_solution(12761858764460508411)
XLA Ops:
  1.3 4.4 %pack.2.refs_4_.refs_5_ = f32[44,128,128]{2,1,0:T(8,128)} custom-call(s32[5]{0:T(128)} %stack.69.refs_0_, f32[512,2048]{1,0:T(8,128)} %bitcast.17, f32[4,512,128]{2,1,0:T(8,128)} %refs_1_.6, f32[512,2048]{1,0:T(8,128)} %bitcast.18, f32[512,2048]{1,0:T(8,128)} %bitcast.19), custom_call_target="tpu_custom_call" | custom-call | flops 1 | bytes 1 | tf_op jit(solution)/shard_map/pack/pallas_call | solution.py:65
  5.7 3.0 %collective-permute-start = (f32[44,128,128]{2,1,0:T(8,128)}, f32[44,128,128]{2,1,0:T(8,128)}, u32[]{:S(2)}, u32[]{:S(2)}) collective-permute-start(f32[44,128,128]{2,1,0:T(8,128)} %pack.2.refs_4_.refs_5_), channel_id=1, source_target_pairs={{0,1},{1,0},{2,3},{3,2},{4,5},{5,4},{6,7},{7,6},{8,9},{9,8},{10,11... | collective-permute-start | bytes 8650760 | tf_op jit(solution)/shard_map/ppermute | solution.py:609
  9.3 3.8 %pack.3.refs_6_ = f32[28,128,128]{2,1,0:T(8,128)} custom-call(s32[4]{0:T(128)} %pad_add_fusion.2.refs_0_, f32[512,2048]{1,0:T(8,128)} %bitcast.20, f32[4,512,128]{2,1,0:T(8,128)} %refs_1_.6, f32[512,2048]{1,0:T(8,128)} %bitcast.21, f32[44,128,128]{2,1,0:T(8,128)} %pack.2.refs_4_.refs_5_), custom_call_target="tpu_custom_call" | custom-call | flops 1 | bytes 1 | tf_op jit(solution)/shard_map/pack/pallas_call | solution.py:65
  13.2 0.8 collective-permute-start.3
  15.3 17.0 %dense.1 = (bf16[2048,2560]{1,0:T(8,128)(2,1)}, bf16[2048,2560]{1,0:T(8,128)(2,1)}, bf16[2,1024,2048]{2,1,0:T(8,128)(2,1)}) custom-call(s32[1]{0:T(128)} %bitcast.refs_0_, s32[1,16,8]{2,1,0:T(8,128)} %copy.27.refs_1_, s32[1,16,2]{2,1,0:T(8,128)} %copy.28.refs_2_, f32[16,8,128,128]{3,2,1,0:T(8,128)} %bitcast.23, f32[16,2,128,128]{3,2,1,0:T(8,128)} %bitcast.24, ...), custom_call_target="tpu_custom_call" | custom-call | flops 1 | bytes 1 | tf_op jit(solution)/shard_map/dense/pallas_call | solution.py:65
  32.9 28.7 %begin.1 = (f32[1024,2048]{1,0:T(8,128)}, f32[512,2048]{1,0:T(8,128)}, f32[512,2048]{1,0:T(8,128)}, f32[512,512]{1,0:T(8,128)}) custom-call(s32[1]{0:T(128)} %bitcast.refs_0_, f32[1]{0:T(128)S(6)} %copy.44.refs_1_, f32[512,2048]{1,0:T(8,128)} %bitcast.22, bf16[2,1024,2048]{2,1,0:T(8,128)(2,1)} %get-tuple-element.28.refs_3_.refs_4_.refs_12_.refs_13_, ...), custom_call_target="tpu_custom_call" | custom-call | flops 1 | bytes 1 | tf_op jit(solution)/shard_map/begin/pallas_call | solution.py:65
  61.6 1.2 copy-done
  62.8 1.3 collective-permute-start.4
  64.1 8.2 %collective-permute-done.refs_2_.refs_0_.refs_1_ = f32[44,128,128]{2,1,0:T(8,128)} collective-permute-done((f32[44,128,128]{2,1,0:T(8,128)}, f32[44,128,128]{2,1,0:T(8,128)}, u32[]{:S(2)}, u32[]{:S(2)}) %collective-permute-start) | collective-permute-done | bytes 2883616 | tf_op jit(solution)/shard_map/ppermute | solution.py:609
  72.3 2.1 front.1
  74.4 1.5 collective-permute-start.1
  76.6 27.9 %stage.3 = (f32[512,2048]{1,0:T(8,128)}, f32[512,2048]{1,0:T(8,128)}, f32[512,512]{1,0:T(8,128)}, f32[1024,2048]{1,0:T(8,128)}) custom-call(s32[4]{0:T(128)} %pad_add_fusion.1.refs_0_, f32[1]{0:T(128)S(6)} %copy.44.refs_1_, ...), custom_call_target="tpu_custom_call", output_to_operand_aliasing={{0}: (9, {}), {1}: (10, {}), {2}: (11, {}), {3}: (4, {})} | custom-call | flops 1 | bytes 1 | tf_op jit(solution)/shard_map/stage/pallas_call | solution.py:65
  104.5 1.5 collective-permute-start.2
  107.2 4.4 %collective-permute-done.4.refs_3_ = f32[28,128,128]{2,1,0:T(8,128)S(1)} collective-permute-done((f32[28,128,128]{2,1,0:T(8,128)}, f32[28,128,128]{2,1,0:T(8,128)S(1)}, u32[]{:S(2)}, u32[]{:S(2)}) %collective-permute-start.4) | collective-permute-done | bytes 1835040 | tf_op jit(solution)/shard_map/ppermute | solution.py:609
  111.6 1.2 copy-done.1
  112.8 24.2 %stage.4 = (f32[512,2048]{1,0:T(8,128)}, f32[512,2048]{1,0:T(8,128)}, f32[512,512]{1,0:T(8,128)}, f32[1024,2048]{1,0:T(8,128)}) custom-call(s32[3]{0:T(128)} %pad_add_fusion.3.refs_0_, f32[1]{0:T(128)S(6)} %copy.44.refs_1_, f32[28,128,128]{2,1,0:T(8,128)} %passed.4.refs_2_, ...), custom_call_target="tpu_custom_call", output_to_operand_aliasing={{0}: (10, {}), {1}: (11, {}), {2}: (12, {}), {3}: (5, {})} | custom-call | flops 1 | bytes 1 | tf_op jit(solution)/shard_map/stage/pallas_call | solution.py:65
  137.1 2.0 collect.1.refs_13_.refs_2_
  139.0 18.5 %stage.5 = (f32[512,2048]{1,0:T(8,128)}, f32[512,2048]{1,0:T(8,128)}, f32[512,512]{1,0:T(8,128)}) custom-call(s32[2]{0:T(128)} %pad_add_fusion.refs_0_, f32[1]{0:T(128)S(6)} %copy.44.refs_1_, f32[12,128,128]{2,1,0:T(8,128)} %passed.3.refs_4_.refs_2_, ...), custom_call_target="tpu_custom_call", output_to_operand_aliasing={{0}: (10, {}), {1}: (11, {}), {2}: (12, {})} | custom-call | flops 1 | bytes 1 | tf_op jit(solution)/shard_map/stage/pallas_call | solution.py:65
  158.8 2.0 collective-permute-done.6.refs_3_
  160.8 0.7 copy-done.4
  161.5 6.3 %drift.1 = (f32[2048,128]{1,0:T(8,128)}, f32[512,128]{1,0:T(8,128)}) custom-call(s32[6]{0:T(128)} %stack.73.refs_0_, f32[4,512,128]{2,1,0:T(8,128)} %refs_1_.6, f32[6,128,128]{2,1,0:T(8,128)} %collect.1.refs_13_.refs_2_, f32[6,128,128]{2,1,0:T(8,128)} %copy-done.4, bf16[2048,2560]{1,0:T(8,128)(2,1)} %get-tuple-element.29.refs_5_.refs_7_.refs_6_.refs_8_.refs_4_.refs_11_, ...), custom_call_target="tpu_custom_call" | custom-call | flops 1 | bytes 1 | tf_op jit(solution)/shard_map/drift/pallas_call | solution.py:65
  167.9 1.0 copy-done.2
  169.4 25.0 %inverse.1.refs_1_ = f32[512,512]{1,0:T(8,128)} custom-call(f32[512,512]{1,0:T(8,128)} %get-tuple-element.43.refs_0_.refs_6_, f32[512,512]{1,0:T(8,128)} %copy-done.2, f32[1,512]{1,0:T(1,128)} %bitcast.26), custom_call_target="tpu_custom_call" | custom-call | flops 1 | bytes 1 | tf_op jit(solution)/shard_map/inverse/pallas_call | solution.py:65
  194.4 16.3 %final.1 = (f32[512,512]{1,0:T(8,128)}, f32[512,2048]{1,0:T(8,128)}, f32[512,128]{1,0:T(8,128)}) custom-call(s32[1]{0:T(128)} %bitcast.refs_0_, f32[512,512]{1,0:T(8,128)} %inverse.1.refs_1_, f32[512,2048]{1,0:T(8,128)} %get-tuple-element.47.refs_2_.refs_6_, f32[512,2048]{1,0:T(8,128)} %collective-permute-done.7.refs_3_.refs_7_, ...), custom_call_target="tpu_custom_call" | custom-call | flops 1 | bytes 1 | tf_op jit(solution)/shard_map/final/pallas_call | solution.py:65
  (31 shorter events, 6.3 us)
Async XLA Ops:
  5.7 66.6 %collective-permute-start = (f32[44,128,128]{2,1,0:T(8,128)}, f32[44,128,128]{2,1,0:T(8,128)}, u32[]{:S(2)}, u32[]{:S(2)}) collective-permute-start(f32[44,128,128]{2,1,0:T(8,128)} %pack.2.refs_4_.refs_5_), channel_id=1, source_target_pairs={{0,1},{1,0},{2,3},{3,2},{4,5},{5,4},{6,7},{7,6},{8,9},{9,8},{10,11... | collective-permute-start | bytes 8650760 | tf_op jit(solution)/shard_map/ppermute | solution.py:609
  9.3 4.6 %copy-start.5 = (s32[1,16,8]{1,2,0:T(8,128)S(1)}, s32[1,16,8]{1,2,0:T(8,128)}, u32[]{:S(2)}) copy-start(s32[1,16,8]{1,2,0:T(8,128)} %param.11) | copy-start | bytes 1540
  9.3 5.3 %copy-start.6 = (s32[1,16,2]{1,2,0:T(2,128)S(1)}, s32[1,16,2]{1,2,0:T(2,128)}, u32[]{:S(2)}) copy-start(s32[1,16,2]{1,2,0:T(2,128)} %param.13) | copy-start | bytes 388
  13.2 48.4 %collective-permute-start.3 = (f32[28,128,128]{2,1,0:T(8,128)}, f32[28,128,128]{2,1,0:T(8,128)S(1)}, u32[]{:S(2)}, u32[]{:S(2)}) collective-permute-start(f32[28,128,128]{2,1,0:T(8,128)} %pack.3.refs_6_), channel_id=1, source_target_pairs={{1,2},{2,1},{5,6},{6,5},{9,10},{10,9},{13,14},{14,13},{17,18},{18,... | collective-permute-start | bytes 5505032 | tf_op jit(solution)/shard_map/ppermute | solution.py:609
  61.6 1.3 copy-start
  62.8 48.7 %collective-permute-start.4 = (f32[28,128,128]{2,1,0:T(8,128)}, f32[28,128,128]{2,1,0:T(8,128)S(1)}, u32[]{:S(2)}, u32[]{:S(2)}) collective-permute-start(f32[28,128,128]{2,1,0:T(8,128)} %passed.4.refs_2_), channel_id=1, source_target_pairs={{1,0},{2,3},{5,4},{6,7},{9,8},{10,11},{13,12},{14,15},{17,16},{18,... | collective-permute-start | bytes 5505032 | tf_op jit(solution)/shard_map/ppermute | solution.py:609
  74.4 30.0 %collective-permute-start.1 = (f32[12,128,128]{2,1,0:T(8,128)}, f32[12,128,128]{2,1,0:T(8,128)}, u32[]{:S(2)}, u32[]{:S(2)}) collective-permute-start(f32[12,128,128]{2,1,0:T(8,128)} %front.1), channel_id=1, source_target_pairs={{1,2},{2,1},{5,6},{6,5},{9,10},{10,9},{13,14},{14,13},{17,18},{18,... | collective-permute-start | bytes 2359304 | tf_op jit(solution)/shard_map/ppermute | solution.py:609
  104.5 32.6 %collective-permute-start.2 = (f32[12,128,128]{2,1,0:T(8,128)}, f32[12,128,128]{2,1,0:T(8,128)}, u32[]{:S(2)}, u32[]{:S(2)}) collective-permute-start(f32[12,128,128]{2,1,0:T(8,128)} %passed.3.refs_4_.refs_2_), channel_id=1, source_target_pairs={{1,0},{2,3},{5,4},{6,7},{9,8},{10,11},{13,12},{14,15},{17,16},{18,... | collective-permute-start | bytes 2359304 | tf_op jit(solution)/shard_map/ppermute | solution.py:609
  111.6 1.2 copy-start.1
  139.0 18.6 %copy-start.3 = (f32[6,128,128]{2,1,0:T(8,128)S(1)}, f32[6,128,128]{2,1,0:T(8,128)}, u32[]{:S(2)}) copy-start(f32[6,128,128]{2,1,0:T(8,128)} %collect.1.refs_13_.refs_2_) | copy-start | bytes 1179652
  157.5 10.3 %collective-permute-start.5 = (f32[512,512]{1,0:T(8,128)}, f32[512,512]{1,0:T(8,128)S(1)}, u32[]{:S(2)}, u32[]{:S(2)}) collective-permute-start(f32[512,512]{1,0:T(8,128)} %get-tuple-element.43.refs_0_.refs_6_), channel_id=1, source_target_pairs={{0,4},{4,0},{8,12},{12,8},{16,20},{20,16},{24,28},{28,24},{1,5},{5... | collective-permute-start | bytes 3145736 | tf_op jit(solution)/shard_map/ppermute | solution.py:640
  157.6 3.1 %collective-permute-start.6 = (f32[6,128,128]{2,1,0:T(8,128)S(1)}, f32[6,128,128]{2,1,0:T(8,128)S(1)}, u32[]{:S(2)}, u32[]{:S(2)}) collective-permute-start(f32[6,128,128]{2,1,0:T(8,128)S(1)} %copy-done.3), channel_id=1, source_target_pairs={{0,4},{4,0},{8,12},{12,8},{16,20},{20,16},{24,28},{28,24},{1,5},{5... | collective-permute-start | bytes 1179656 | tf_op jit(solution)/shard_map/ppermute | solution.py:640
  160.8 0.7 copy-start.4
  167.9 1.0 copy-start.2
  168.8 25.5 %collective-permute-start.7 = (f32[512,2048]{1,0:T(8,128)}, f32[512,2048]{1,0:T(8,128)}, u32[]{:S(2)}, u32[]{:S(2)}) collective-permute-start(f32[512,2048]{1,0:T(8,128)} %get-tuple-element.47.refs_2_.refs_6_), channel_id=1, source_target_pairs={{0,4},{4,0},{8,12},{12,8},{16,20},{20,16},{24,28},{28,24},{1,5},{5... | collective-permute-start | bytes 12582920 | tf_op jit(solution)/shard_map/ppermute | solution.py:640
  169.0 25.4 %collective-permute-start.8 = (f32[512,2048]{1,0:T(8,128)}, f32[512,2048]{1,0:T(8,128)}, u32[]{:S(2)}, u32[]{:S(2)}) collective-permute-start(f32[512,2048]{1,0:T(8,128)} %get-tuple-element.48.refs_4_), channel_id=1, source_target_pairs={{0,4},{4,0},{8,12},{12,8},{16,20},{20,16},{24,28},{28,24},{1,5},{5... | collective-permute-start | bytes 12582920 | tf_op jit(solution)/shard_map/ppermute | solution.py:640

commit v4 on v3

--- a/solution.py
+++ b/solution.py
@@ -7,7 +7,6 @@
 from jax.experimental.pallas import tpu as pltpu
 from jax.sharding import PartitionSpec as P
 
-HIGHEST = lax.Precision.HIGHEST
 F32 = jnp.float32
 BF16 = jnp.bfloat16
 VMEM_LIMIT = 62 * 2**20
@@ -31,6 +30,21 @@
     both = jnp.concatenate(a, axis=0) if isinstance(a, (tuple, list)) else a.reshape(2 * rows, a.shape[2])
     part = one(both, b[0])
     return part[:rows] + (part[rows:] + one(a[0], b[1]))
+
+
+BEGIN_TILE = (256, 512)
+STAGE_TILE = (256, 256)
+
+
+def multiply(out, a, b, dims, tile, add=None):
+    right = dims[0][1][0]
+    for m in range(0, out.shape[0], tile[0]):
+        rows = slice(m, m + tile[0])
+        for n in range(0, out.shape[1], tile[1]):
+            cols = slice(n, n + tile[1])
+            b_part = [x[:, cols] if right == 0 else x[cols] for x in b]
+            value = dot3((a[0, rows], a[1, rows]), b_part, dims)
+            out[rows, cols] = value if add is None else add[rows, cols] + value
 
 
 def call(kernel, grid, prefetch, ins, outs, shapes, name, scratch=(), aliases=None, after=(), through=()):
@@ -76,8 +90,8 @@
 def dense_kernel(blk, step, width, where, acol, bcol, a_ref, b_ref, fh, fl, u):
     i = pl.program_id(0)
     orders = fh.shape[1] - width
-    group = (u.shape[1] - orders) // blk
-    for ref in (fh, fl, u):
+    rows = u.shape[1] - orders
+    for ref in (fh, fl):
         ref[...] = jnp.zeros_like(ref)
     diag = lax.broadcasted_iota(jnp.int32, (blk, blk), 0) == lax.broadcasted_iota(jnp.int32, (blk, blk), 1)
     eye = jnp.where(diag, 0.75, 0.0).astype(F32)
@@ -89,20 +103,18 @@
             block = a_ref[t, s] + eye if s == 0 else a_ref[t, s]
             to = pl.ds(pl.multiple_of(col * blk, blk), blk)
             fh[at, to], fl[at, to] = split(block)
-            local = col - where[0] * group
-
-            @pl.when((local >= 0) & (local < group))
-            def _():
-                to = pl.ds(pl.multiple_of(orders + local * blk, blk), blk)
-                u[0, to, at], u[1, to, at] = split(block.T)
-
         for s in range(b_ref.shape[1]):
-            col = bcol[0, row, s]
-            block = b_ref[t, s]
-            to = pl.ds(pl.multiple_of(width + col * blk, blk), blk)
-            fh[at, to], fl[at, to] = split(block)
-            to = pl.ds(pl.multiple_of(col * blk, blk), blk)
-            u[0, to, at], u[1, to, at] = split(block.T)
+            to = pl.ds(pl.multiple_of(width + bcol[0, row, s] * blk, blk), blk)
+            fh[at, to], fl[at, to] = split(b_ref[t, s])
+
+    own = pl.ds(pl.multiple_of(where[0] * rows, rows), rows)
+    for p, f in enumerate((fh, fl)):
+        for to, cols in ((slice(0, orders), slice(width, None)), (slice(orders, None), own)):
+            part = f[:, cols]
+            n = part.shape[1]
+            diag = lax.broadcasted_iota(jnp.int32, (n, n), 0) == lax.broadcasted_iota(jnp.int32, (n, n), 1)
+            one = jnp.where(diag, 1.0, 0.0).astype(BF16)
+            u[p, to] = lax.dot_general(one, part, NT, preferred_element_type=F32).astype(BF16)
 
 
 def dense(where, rows, a_blocks, a_cols, b_blocks, b_cols, orders, after):
@@ -167,7 +179,9 @@
 
 def inverse_kernel(blk, mine, other, d_ref, out):
     n = out.shape[0]
-    dot = functools.partial(jnp.dot, precision=HIGHEST, preferred_element_type=F32)
+    def dot(a, b):
+        return dot3(split(a), split(b))
+
     diag = lax.broadcasted_iota(jnp.int32, (n, n), 0) == lax.broadcasted_iota(jnp.int32, (n, n), 1)
     out[...] = mine[...] + other[...] + jnp.where(diag, d_ref[...], 0.0)
 
@@ -332,25 +346,24 @@
     return call(lambda *_: None, (1,), 0, [], [], [], "passed", after=after, through=arrays)()
 
 
-def begin_kernel(steps, where, weight, p_ref, u, v, fh, fl, bh, bl, rest, s_out, g_out, h_out, mine, pair):
+def begin_kernel(steps, where, weight, p_ref, u, v, fh, fl, bh, bl, rest, s_out, g_out, h_out, mine, pair, ph, pl_):
     g = pl.program_id(0)
 
     @pl.when(g < steps)
     def _():
-        p = split(p_ref[...])
-        part = dot3(u[...], p, NT)
+        ph[...], pl_[...] = split(p_ref[...])
 
         @pl.when(g == 0)
         def _():
-            mine[...] = part
+            multiply(mine, u, (ph, pl_), NT, BEGIN_TILE)
 
         @pl.when(g > 0)
         def _():
-            mine[...] += part
+            multiply(mine, u, (ph, pl_), NT, BEGIN_TILE, mine)
 
         @pl.when(g != where[0])
         def _():
-            rest[...] = dot3(v[...], p)
+            multiply(rest, v, (ph, pl_), NN, BEGIN_TILE)
 
     @pl.when(g == steps)
     def _():
@@ -360,10 +373,9 @@
 
     @pl.when(g >= steps)
     def _():
-        part = dot3(pair[...], (fh[...], fl[...]))
         orders = g_out.shape[0]
-        s_out[...] = part[orders:]
-        g_out[...] = part[:orders]
+        multiply(g_out, pair.at[:, :orders], (fh, fl), NN, BEGIN_TILE)
+        multiply(s_out, pair.at[:, orders:], (fh, fl), NN, BEGIN_TILE)
 
 
 def begin(where, weight, cost_rows, u, fh, fl):
@@ -396,7 +408,7 @@
         ],
         [((tall, width), F32), ((rows, width), F32), ((orders, width), F32), ((orders, orders), F32)],
         "begin",
-        [pltpu.VMEM((tall, rows), F32), pltpu.VMEM((2, tall, rows), BF16)],
+        [pltpu.VMEM((tall, rows), F32), pltpu.VMEM((2, tall, rows), BF16)] + [pltpu.VMEM((rows, rows), BF16)] * 2,
     )(where, weight, cost_rows, u, u, fh, fl, fh, fl)
 
 
@@ -418,15 +430,14 @@
 
     @pl.when(g == 0)
     def _():
-        done[...] = n_in[...] + dot3(v[...], (xh[...], xl[...]))
+        multiply(done, v, (xh, xl), NN, STAGE_TILE, n_in)
 
     if size > 1:
 
         @pl.when((g > 0) & (g < size))
         def _():
-            x = xh[...], xl[...]
-            done[...] += dot3(u[...], x, NT)
-            n_out[...] = n_in[...] + dot3(v[...], x)
+            multiply(done, u, (xh, xl), NT, STAGE_TILE, done)
+            multiply(n_out, v, (xh, xl), NN, STAGE_TILE, n_in)
 
     @pl.when(g == size)
     def _():
@@ -436,10 +447,9 @@
 
     @pl.when(g >= size)
     def _():
-        part = dot3(pair[...], (fh[...], fl[...]))
         orders = g_out.shape[0]
-        s_out[...] = s_in[...] + part[orders:]
-        g_out[...] = g_in[...] + part[:orders]
+        multiply(g_out, pair.at[:, :orders], (fh, fl), NN, STAGE_TILE, g_in)
+        multiply(s_out, pair.at[:, orders:], (fh, fl), NN, STAGE_TILE, s_in)
 
 
 def stage(where, weight, arrived, size, u, n, fh, fl, sums, after=(), through=()):

time: 212 us -> 210 us (level)
  Pallas kernels: 176 us -> 173 us
    pallas_call x15, Pallas kernels: 176 us -> 173 us  [call(): return lambda *args: built(*args, *after, *through)]
  transfers between devices with their start and end apart: 9 -> 9, of which waited for: 3 -> 3; matrix products, arithmetic and copies ran while one was open for 2% -> 2% of each run, Pallas kernels for 64% -> 63%
where the time goes in v4:
time: 210 us; the launch traced here: 209 us
  Pallas kernels  173 us (82%)
  waiting for transfers between devices  15.2 us (7%)
  starting transfers between devices  9.19 us (4%)
  local copies, waits for them, and re-layouts  6.88 us (3%)
  other arithmetic  2.46 us (1%)
    pallas_call x15, Pallas kernels, call(): return lambda *args: built(*args, *after, *through)  173 us
    ppermute x5, waiting for transfers between devices, moved(): return lax.ppermute(x, 'row', pairs)  13.2 us
    ppermute x5, starting transfers between devices, moved(): return lax.ppermute(x, 'row', pairs)  8.12 us
    unnamed x16, local copies, waits for them, and re-layouts  5.54 us
  transfers between devices with their start and end apart: 9, of which 3 were waited for; matrix products, arithmetic and copies ran while one was open for 2% of the time, Pallas kernels for 63%

profile of v4, /device:TPU:0, one launch (start us, length us, event | category | flops | bytes accessed | tf_op | source)
XLA Modules:
  0.0 208.6 jit_solution(9265551026251864977)
XLA Ops:
  1.3 4.4 %pack.2.refs_4_.refs_5_ = f32[44,128,128]{2,1,0:T(8,128)} custom-call(s32[5]{0:T(128)} %stack.69.refs_0_, f32[512,2048]{1,0:T(8,128)} %bitcast.17, f32[4,512,128]{2,1,0:T(8,128)} %refs_1_.6, f32[512,2048]{1,0:T(8,128)} %bitcast.18, f32[512,2048]{1,0:T(8,128)} %bitcast.19), custom_call_target="tpu_custom_call" | custom-call | flops 1 | bytes 1 | tf_op jit(solution)/shard_map/pack/pallas_call | solution.py:79
  5.7 3.0 %collective-permute-start = (f32[44,128,128]{2,1,0:T(8,128)}, f32[44,128,128]{2,1,0:T(8,128)}, u32[]{:S(2)}, u32[]{:S(2)}) collective-permute-start(f32[44,128,128]{2,1,0:T(8,128)} %pack.2.refs_4_.refs_5_), channel_id=1, source_target_pairs={{0,1},{1,0},{2,3},{3,2},{4,5},{5,4},{6,7},{7,6},{8,9},{9,8},{10,11... | collective-permute-start | bytes 8650760 | tf_op jit(solution)/shard_map/ppermute | solution.py:619
  9.3 3.8 %pack.3.refs_6_ = f32[28,128,128]{2,1,0:T(8,128)} custom-call(s32[4]{0:T(128)} %pad_add_fusion.2.refs_0_, f32[512,2048]{1,0:T(8,128)} %bitcast.20, f32[4,512,128]{2,1,0:T(8,128)} %refs_1_.6, f32[512,2048]{1,0:T(8,128)} %bitcast.21, f32[44,128,128]{2,1,0:T(8,128)} %pack.2.refs_4_.refs_5_), custom_call_target="tpu_custom_call" | custom-call | flops 1 | bytes 1 | tf_op jit(solution)/shard_map/pack/pallas_call | solution.py:79
  13.2 0.8 collective-permute-start.3
  15.3 16.5 %dense.1 = (bf16[2048,2560]{1,0:T(8,128)(2,1)}, bf16[2048,2560]{1,0:T(8,128)(2,1)}, bf16[2,1024,2048]{2,1,0:T(8,128)(2,1)}) custom-call(s32[1]{0:T(128)} %bitcast.refs_0_, s32[1,16,8]{2,1,0:T(8,128)} %copy.27.refs_1_, s32[1,16,2]{2,1,0:T(8,128)} %copy.28.refs_2_, f32[16,8,128,128]{3,2,1,0:T(8,128)} %bitcast.23, f32[16,2,128,128]{3,2,1,0:T(8,128)} %bitcast.24, ...), custom_call_target="tpu_custom_call" | custom-call | flops 1 | bytes 1 | tf_op jit(solution)/shard_map/dense/pallas_call | solution.py:79
  32.4 28.5 %begin.1 = (f32[1024,2048]{1,0:T(8,128)}, f32[512,2048]{1,0:T(8,128)}, f32[512,2048]{1,0:T(8,128)}, f32[512,512]{1,0:T(8,128)}) custom-call(s32[1]{0:T(128)} %bitcast.refs_0_, f32[1]{0:T(128)S(6)} %copy.44.refs_1_, f32[512,2048]{1,0:T(8,128)} %bitcast.22, bf16[2,1024,2048]{2,1,0:T(8,128)(2,1)} %get-tuple-element.28.refs_3_.refs_4_.refs_12_.refs_13_, ...), custom_call_target="tpu_custom_call" | custom-call | flops 1 | bytes 1 | tf_op jit(solution)/shard_map/begin/pallas_call | solution.py:79
  61.0 1.2 copy-done
  62.2 1.3 collective-permute-start.4
  63.5 8.9 %collective-permute-done.refs_2_.refs_0_.refs_1_ = f32[44,128,128]{2,1,0:T(8,128)} collective-permute-done((f32[44,128,128]{2,1,0:T(8,128)}, f32[44,128,128]{2,1,0:T(8,128)}, u32[]{:S(2)}, u32[]{:S(2)}) %collective-permute-start) | collective-permute-done | bytes 2883616 | tf_op jit(solution)/shard_map/ppermute | solution.py:619
  72.3 2.1 front.1
  74.4 1.5 collective-permute-start.1
  76.6 27.9 %stage.3 = (f32[512,2048]{1,0:T(8,128)}, f32[512,2048]{1,0:T(8,128)}, f32[512,512]{1,0:T(8,128)}, f32[1024,2048]{1,0:T(8,128)}) custom-call(s32[4]{0:T(128)} %pad_add_fusion.1.refs_0_, f32[1]{0:T(128)S(6)} %copy.44.refs_1_, ...), custom_call_target="tpu_custom_call", output_to_operand_aliasing={{0}: (9, {}), {1}: (10, {}), {2}: (11, {}), {3}: (4, {})} | custom-call | flops 1 | bytes 1 | tf_op jit(solution)/shard_map/stage/pallas_call | solution.py:79
  104.5 1.5 collective-permute-start.2
  107.3 4.3 %collective-permute-done.4.refs_3_ = f32[28,128,128]{2,1,0:T(8,128)S(1)} collective-permute-done((f32[28,128,128]{2,1,0:T(8,128)}, f32[28,128,128]{2,1,0:T(8,128)S(1)}, u32[]{:S(2)}, u32[]{:S(2)}) %collective-permute-start.4) | collective-permute-done | bytes 1835040 | tf_op jit(solution)/shard_map/ppermute | solution.py:619
  111.6 1.2 copy-done.1
  112.8 24.3 %stage.4 = (f32[512,2048]{1,0:T(8,128)}, f32[512,2048]{1,0:T(8,128)}, f32[512,512]{1,0:T(8,128)}, f32[1024,2048]{1,0:T(8,128)}) custom-call(s32[3]{0:T(128)} %pad_add_fusion.3.refs_0_, f32[1]{0:T(128)S(6)} %copy.44.refs_1_, f32[28,128,128]{2,1,0:T(8,128)} %passed.4.refs_2_, ...), custom_call_target="tpu_custom_call", output_to_operand_aliasing={{0}: (10, {}), {1}: (11, {}), {2}: (12, {}), {3}: (5, {})} | custom-call | flops 1 | bytes 1 | tf_op jit(solution)/shard_map/stage/pallas_call | solution.py:79
  137.1 2.2 %collect.1.refs_13_.refs_2_ = f32[6,128,128]{2,1,0:T(8,128)} custom-call(s32[1]{0:T(128)} %bitcast.1.refs_0_, f32[44,128,128]{2,1,0:T(8,128)} %collective-permute-done.refs_2_.refs_0_.refs_1_, f32[28,128,128]{2,1,0:T(8,128)} %passed.4.refs_2_, f32[28,128,128]{2,1,0:T(8,128)} %copy-done.1, f32[12,128,128]{2,1,0:T(8,128)} %passed.3.refs_4_.refs_2_, ...), custom_call_target="tpu_custom_call" | custom-call | flops 1 | bytes 1 | tf_op jit(solution)/shard_map/collect/pallas_call | solution.py:79
  139.3 18.5 %stage.5 = (f32[512,2048]{1,0:T(8,128)}, f32[512,2048]{1,0:T(8,128)}, f32[512,512]{1,0:T(8,128)}) custom-call(s32[2]{0:T(128)} %pad_add_fusion.refs_0_, f32[1]{0:T(128)S(6)} %copy.44.refs_1_, f32[12,128,128]{2,1,0:T(8,128)} %passed.3.refs_4_.refs_2_, ...), custom_call_target="tpu_custom_call", output_to_operand_aliasing={{0}: (10, {}), {1}: (11, {}), {2}: (12, {})} | custom-call | flops 1 | bytes 1 | tf_op jit(solution)/shard_map/stage/pallas_call | solution.py:79
  159.1 2.0 collective-permute-done.6.refs_3_
  161.1 0.7 copy-done.4
  161.8 6.3 %drift.1 = (f32[2048,128]{1,0:T(8,128)}, f32[512,128]{1,0:T(8,128)}) custom-call(s32[6]{0:T(128)} %stack.73.refs_0_, f32[4,512,128]{2,1,0:T(8,128)} %refs_1_.6, f32[6,128,128]{2,1,0:T(8,128)} %collect.1.refs_13_.refs_2_, f32[6,128,128]{2,1,0:T(8,128)} %copy-done.4, bf16[2048,2560]{1,0:T(8,128)(2,1)} %get-tuple-element.29.refs_5_.refs_7_.refs_6_.refs_8_.refs_4_.refs_11_, ...), custom_call_target="tpu_custom_call" | custom-call | flops 1 | bytes 1 | tf_op jit(solution)/shard_map/drift/pallas_call | solution.py:79
  168.2 1.0 copy-done.2
  169.7 22.3 %inverse.1.refs_1_ = f32[512,512]{1,0:T(8,128)} custom-call(f32[512,512]{1,0:T(8,128)} %get-tuple-element.43.refs_0_.refs_6_, f32[512,512]{1,0:T(8,128)} %copy-done.2, f32[1,512]{1,0:T(1,128)} %bitcast.26), custom_call_target="tpu_custom_call" | custom-call | flops 1 | bytes 1 | tf_op jit(solution)/shard_map/inverse/pallas_call | solution.py:79
  191.9 16.4 %final.1 = (f32[512,512]{1,0:T(8,128)}, f32[512,2048]{1,0:T(8,128)}, f32[512,128]{1,0:T(8,128)}) custom-call(s32[1]{0:T(128)} %bitcast.refs_0_, f32[512,512]{1,0:T(8,128)} %inverse.1.refs_1_, f32[512,2048]{1,0:T(8,128)} %get-tuple-element.47.refs_2_.refs_6_, f32[512,2048]{1,0:T(8,128)} %collective-permute-done.7.refs_3_.refs_7_, ...), custom_call_target="tpu_custom_call" | custom-call | flops 1 | bytes 1 | tf_op jit(solution)/shard_map/final/pallas_call | solution.py:79
  (31 shorter events, 6.3 us)
Async XLA Ops:
  5.7 66.6 %collective-permute-start = (f32[44,128,128]{2,1,0:T(8,128)}, f32[44,128,128]{2,1,0:T(8,128)}, u32[]{:S(2)}, u32[]{:S(2)}) collective-permute-start(f32[44,128,128]{2,1,0:T(8,128)} %pack.2.refs_4_.refs_5_), channel_id=1, source_target_pairs={{0,1},{1,0},{2,3},{3,2},{4,5},{5,4},{6,7},{7,6},{8,9},{9,8},{10,11... | collective-permute-start | bytes 8650760 | tf_op jit(solution)/shard_map/ppermute | solution.py:619
  9.3 4.6 %copy-start.5 = (s32[1,16,8]{1,2,0:T(8,128)S(1)}, s32[1,16,8]{1,2,0:T(8,128)}, u32[]{:S(2)}) copy-start(s32[1,16,8]{1,2,0:T(8,128)} %param.11) | copy-start | bytes 1540
  9.3 5.3 %copy-start.6 = (s32[1,16,2]{1,2,0:T(2,128)S(1)}, s32[1,16,2]{1,2,0:T(2,128)}, u32[]{:S(2)}) copy-start(s32[1,16,2]{1,2,0:T(2,128)} %param.13) | copy-start | bytes 388
  13.2 47.8 %collective-permute-start.3 = (f32[28,128,128]{2,1,0:T(8,128)}, f32[28,128,128]{2,1,0:T(8,128)S(1)}, u32[]{:S(2)}, u32[]{:S(2)}) collective-permute-start(f32[28,128,128]{2,1,0:T(8,128)} %pack.3.refs_6_), channel_id=1, source_target_pairs={{1,2},{2,1},{5,6},{6,5},{9,10},{10,9},{13,14},{14,13},{17,18},{18,... | collective-permute-start | bytes 5505032 | tf_op jit(solution)/shard_map/ppermute | solution.py:619
  60.9 1.3 copy-start
  62.2 49.4 %collective-permute-start.4 = (f32[28,128,128]{2,1,0:T(8,128)}, f32[28,128,128]{2,1,0:T(8,128)S(1)}, u32[]{:S(2)}, u32[]{:S(2)}) collective-permute-start(f32[28,128,128]{2,1,0:T(8,128)} %passed.4.refs_2_), channel_id=1, source_target_pairs={{1,0},{2,3},{5,4},{6,7},{9,8},{10,11},{13,12},{14,15},{17,16},{18,... | collective-permute-start | bytes 5505032 | tf_op jit(solution)/shard_map/ppermute | solution.py:619
  74.4 30.1 %collective-permute-start.1 = (f32[12,128,128]{2,1,0:T(8,128)}, f32[12,128,128]{2,1,0:T(8,128)}, u32[]{:S(2)}, u32[]{:S(2)}) collective-permute-start(f32[12,128,128]{2,1,0:T(8,128)} %front.1), channel_id=1, source_target_pairs={{1,2},{2,1},{5,6},{6,5},{9,10},{10,9},{13,14},{14,13},{17,18},{18,... | collective-permute-start | bytes 2359304 | tf_op jit(solution)/shard_map/ppermute | solution.py:619
  104.5 32.6 %collective-permute-start.2 = (f32[12,128,128]{2,1,0:T(8,128)}, f32[12,128,128]{2,1,0:T(8,128)}, u32[]{:S(2)}, u32[]{:S(2)}) collective-permute-start(f32[12,128,128]{2,1,0:T(8,128)} %passed.3.refs_4_.refs_2_), channel_id=1, source_target_pairs={{1,0},{2,3},{5,4},{6,7},{9,8},{10,11},{13,12},{14,15},{17,16},{18,... | collective-permute-start | bytes 2359304 | tf_op jit(solution)/shard_map/ppermute | solution.py:619
  111.6 1.2 copy-start.1
  139.3 18.6 %copy-start.3 = (f32[6,128,128]{2,1,0:T(8,128)S(1)}, f32[6,128,128]{2,1,0:T(8,128)}, u32[]{:S(2)}) copy-start(f32[6,128,128]{2,1,0:T(8,128)} %collect.1.refs_13_.refs_2_) | copy-start | bytes 1179652
  157.9 10.3 %collective-permute-start.5 = (f32[512,512]{1,0:T(8,128)}, f32[512,512]{1,0:T(8,128)S(1)}, u32[]{:S(2)}, u32[]{:S(2)}) collective-permute-start(f32[512,512]{1,0:T(8,128)} %get-tuple-element.43.refs_0_.refs_6_), channel_id=1, source_target_pairs={{0,4},{4,0},{8,12},{12,8},{16,20},{20,16},{24,28},{28,24},{1,5},{5... | collective-permute-start | bytes 3145736 | tf_op jit(solution)/shard_map/ppermute | solution.py:650
  157.9 3.1 %collective-permute-start.6 = (f32[6,128,128]{2,1,0:T(8,128)S(1)}, f32[6,128,128]{2,1,0:T(8,128)S(1)}, u32[]{:S(2)}, u32[]{:S(2)}) collective-permute-start(f32[6,128,128]{2,1,0:T(8,128)S(1)} %copy-done.3), channel_id=1, source_target_pairs={{0,4},{4,0},{8,12},{12,8},{16,20},{20,16},{24,28},{28,24},{1,5},{5... | collective-permute-start | bytes 1179656 | tf_op jit(solution)/shard_map/ppermute | solution.py:650
  161.1 0.7 copy-start.4
  168.2 1.0 copy-start.2
  169.2 22.8 %collective-permute-start.7 = (f32[512,2048]{1,0:T(8,128)}, f32[512,2048]{1,0:T(8,128)}, u32[]{:S(2)}, u32[]{:S(2)}) collective-permute-start(f32[512,2048]{1,0:T(8,128)} %get-tuple-element.47.refs_2_.refs_6_), channel_id=1, source_target_pairs={{0,4},{4,0},{8,12},{12,8},{16,20},{20,16},{24,28},{28,24},{1,5},{5... | collective-permute-start | bytes 12582920 | tf_op jit(solution)/shard_map/ppermute | solution.py:650
  169.3 22.6 %collective-permute-start.8 = (f32[512,2048]{1,0:T(8,128)}, f32[512,2048]{1,0:T(8,128)}, u32[]{:S(2)}, u32[]{:S(2)}) collective-permute-start(f32[512,2048]{1,0:T(8,128)} %get-tuple-element.48.refs_4_), channel_id=1, source_target_pairs={{0,4},{4,0},{8,12},{12,8},{16,20},{20,16},{24,28},{28,24},{1,5},{5... | collective-permute-start | bytes 12582920 | tf_op jit(solution)/shard_map/ppermute | solution.py:650

commit v5 on v4

--- a/solution.py
+++ b/solution.py
@@ -9,7 +9,7 @@
 
 F32 = jnp.float32
 BF16 = jnp.bfloat16
-VMEM_LIMIT = 62 * 2**20
+VMEM_LIMIT = 24 * 2**20
 NN = (((1,), (0,)), ((), ()))
 NT = (((1,), (1,)), ((), ()))
 
@@ -32,22 +32,35 @@
     return part[:rows] + (part[rows:] + one(a[0], b[1]))
 
 
-BEGIN_TILE = (256, 512)
-STAGE_TILE = (256, 256)
-
-
-def multiply(out, a, b, dims, tile, add=None):
+TILE = (256, 512)
+VMEM = pltpu.VMEM
+STAYS = pl.BlockSpec(memory_space=VMEM)
+
+
+def resident(x):
+    return pltpu.with_memory_space_constraint(x, VMEM)
+
+
+def outside(x):
+    return pltpu.with_memory_space_constraint(x, pltpu.HBM)
+
+
+def column(ref, i, size):
+    return ref.at[..., pl.ds(pl.multiple_of(i * size, size), size)]
+
+
+def multiply(out, a, b, dims, add=None):
     right = dims[0][1][0]
-    for m in range(0, out.shape[0], tile[0]):
-        rows = slice(m, m + tile[0])
-        for n in range(0, out.shape[1], tile[1]):
-            cols = slice(n, n + tile[1])
+    for m in range(0, out.shape[0], TILE[0]):
+        rows = slice(m, m + TILE[0])
+        for n in range(0, out.shape[1], TILE[1]):
+            cols = slice(n, n + TILE[1])
             b_part = [x[:, cols] if right == 0 else x[cols] for x in b]
             value = dot3((a[0, rows], a[1, rows]), b_part, dims)
             out[rows, cols] = value if add is None else add[rows, cols] + value
 
 
-def call(kernel, grid, prefetch, ins, outs, shapes, name, scratch=(), aliases=None, after=(), through=()):
+def call(kernel, grid, prefetch, ins, outs, shapes, name, scratch=(), aliases=None, after=(), through=(), keep=False):
     n_in, n_out = len(ins), len(outs)
     extra = len(after) + len(through)
     anywhere = pl.BlockSpec(memory_space=pl.ANY)
@@ -69,14 +82,19 @@
             out_specs=list(outs) + [anywhere] * len(through),
             scratch_shapes=scratch,
         ),
-        out_shape=[jax.ShapeDtypeStruct(shape, kind) for shape, kind in shapes]
-        + [jax.ShapeDtypeStruct(x.shape, x.dtype) for x in through],
+        out_shape=[x if isinstance(x, pl.MemoryRef) else jax.ShapeDtypeStruct(*x) for x in shapes]
+        + [(VMEM if keep else jax.ShapeDtypeStruct)(x.shape, x.dtype) for x in through],
         input_output_aliases=aliases,
         compiler_params=pltpu.CompilerParams(vmem_limit_bytes=VMEM_LIMIT),
         cost_estimate=pl.CostEstimate(flops=1, bytes_accessed=1, transcendentals=0),
         name=name,
     )
-    return lambda *args: built(*args, *after, *through)
+
+    def run(*args):
+        placed = [resident(x) if spec is STAYS else x for spec, x in zip(ins, args[prefetch:])]
+        return built(*args[:prefetch], *placed, *after, *[resident(x) if keep else x for x in through])
+
+    return run
 
 
 def whole(*shape):
@@ -114,7 +132,7 @@
             n = part.shape[1]
             diag = lax.broadcasted_iota(jnp.int32, (n, n), 0) == lax.broadcasted_iota(jnp.int32, (n, n), 1)
             one = jnp.where(diag, 1.0, 0.0).astype(BF16)
-            u[p, to] = lax.dot_general(one, part, NT, preferred_element_type=F32).astype(BF16)
+            u[p, to, pl.ds(pl.multiple_of(i * step, step), step)] = lax.dot_general(one, part, NT, preferred_element_type=F32).astype(BF16)
 
 
 def dense(where, rows, a_blocks, a_cols, b_blocks, b_cols, orders, after):
@@ -124,7 +142,6 @@
     step = 2 * blk
     total = width + orders
     factor = pl.BlockSpec((step, total), lambda i, *_: (i, 0))
-    turned = pl.BlockSpec((2, rows + orders, step), lambda i, *_: (0, 0, i))
     return call(
         functools.partial(dense_kernel, blk, step, width),
         (width // step,),
@@ -133,11 +150,11 @@
             pl.BlockSpec((2, nnza, blk, blk), lambda i, *_: (i, 0, 0, 0)),
             pl.BlockSpec((2, nnzb, blk, blk), lambda i, *_: (i, 0, 0, 0)),
         ],
-        [factor, factor, turned],
-        [((width, total), BF16)] * 2 + [((2, rows + orders, width), BF16)],
+        [factor, factor, STAYS],
+        [pltpu.HBM((width, total), BF16)] * 2 + [VMEM((2, rows + orders, width), BF16)],
         "dense",
         after=after,
-    )(where, a_cols, b_cols, a_blocks, b_blocks)
+    )(where, a_cols, b_cols, outside(a_blocks), outside(b_blocks))
 
 
 def inverse_block(m):
@@ -232,8 +249,8 @@
     size = len(lower(rows // blk)) + 2 + (len(picks) - 1) * (rows // blk) ** 2
     specs = [pl.BlockSpec((rows, rows), functools.partial(lambda t, i, where: (0, where[t]), t)) for t in picks]
     specs.insert(1, pl.BlockSpec((1, rows // 2, samples), lambda i, where: (where[1], where[2], 0)))
-    args = [cost_rows] * len(picks)
-    args.insert(1, parent_state)
+    args = [outside(cost_rows)] * len(picks)
+    args.insert(1, outside(parent_state))
     return call(
         functools.partial(pack_kernel, blk),
         (1,),
@@ -339,15 +356,19 @@
         [((4 * rows, samples), F32), ((rows, samples), F32)],
         "drift",
         after=[after],
-    )(where, parent_state, mine, other, fh, fl)
-
-
-def passed(arrays, *after):
-    return call(lambda *_: None, (1,), 0, [], [], [], "passed", after=after, through=arrays)()
-
-
-def begin_kernel(steps, where, weight, p_ref, u, v, fh, fl, bh, bl, rest, s_out, g_out, h_out, mine, pair, ph, pl_):
+    )(where, outside(parent_state), mine, other, outside(fh), outside(fl))
+
+
+def passed(arrays, *after, keep=False):
+    return call(lambda *_: None, (1,), 0, [], [], [], "passed", after=after, through=arrays, keep=keep)()
+
+
+def begin_kernel(steps, where, weight, p_ref, u, fh, fl, bh, bl, n_out, s_out, g_out, h_out, token, mine, pair, ph, pl_):
     g = pl.program_id(0)
+    token[...] = jnp.zeros_like(token)
+    rows = ph.shape[0]
+    orders = g_out.shape[0]
+    tile = fh.shape[1]
 
     @pl.when(g < steps)
     def _():
@@ -355,27 +376,23 @@
 
         @pl.when(g == 0)
         def _():
-            multiply(mine, u, (ph, pl_), NT, BEGIN_TILE)
-
-        @pl.when(g > 0)
-        def _():
-            multiply(mine, u, (ph, pl_), NT, BEGIN_TILE, mine)
+            mine[...] = jnp.zeros_like(mine)
+
+        multiply(mine, column(u, g, rows), (ph, pl_), NT, mine)
 
         @pl.when(g != where[0])
         def _():
-            multiply(rest, v, (ph, pl_), NN, BEGIN_TILE)
+            multiply(column(n_out, g, rows), column(u, where[0], rows), (ph, pl_), NN)
 
     @pl.when(g == steps)
     def _():
         pair[0], pair[1] = split(mine[...] * weight[0])
-        orders = h_out.shape[0]
         h_out[...] = dot3(pair[:, :orders], (bh[...], bl[...]))
 
     @pl.when(g >= steps)
     def _():
-        orders = g_out.shape[0]
-        multiply(g_out, pair.at[:, :orders], (fh, fl), NN, BEGIN_TILE)
-        multiply(s_out, pair.at[:, orders:], (fh, fl), NN, BEGIN_TILE)
+        multiply(column(g_out, g - steps, tile), pair.at[:, :orders], (fh, fl), NN)
+        multiply(column(s_out, g - steps, tile), pair.at[:, orders:], (fh, fl), NN)
 
 
 def begin(where, weight, cost_rows, u, fh, fl):
@@ -384,128 +401,110 @@
     orders = tall - rows
     steps = width // rows
     tile = 512
-
-    def early(g):
-        return jnp.minimum(g, steps - 1)
-
-    def late(g):
-        return jnp.maximum(g - steps, 0)
-
-    each = pl.BlockSpec((2, tall, rows), lambda g, *_: (0, 0, early(g)))
-    own = pl.BlockSpec((2, tall, rows), lambda g, where, _: (0, 0, where[0]))
-    factor = pl.BlockSpec((rows, tile), lambda g, where, _: (where[0], late(g)))
+    factor = pl.BlockSpec((rows, tile), lambda g, where, _: (where[0], jnp.maximum(g - steps, 0)))
     control = pl.BlockSpec((rows, orders), lambda g, where, _: (where[0], width // orders))
     return call(
         functools.partial(begin_kernel, steps),
         (steps + width // tile,),
         2,
-        [pl.BlockSpec((rows, rows), lambda g, *_: (0, early(g))), each, own, factor, factor, control, control],
         [
-            pl.BlockSpec((tall, rows), lambda g, *_: (0, early(g))),
-            pl.BlockSpec((rows, tile), lambda g, *_: (0, late(g))),
-            pl.BlockSpec((orders, tile), lambda g, *_: (0, late(g))),
-            whole(orders, orders),
+            pl.BlockSpec((rows, rows), lambda g, *_: (0, jnp.minimum(g, steps - 1))),
+            STAYS,
+            factor,
+            factor,
+            control,
+            control,
         ],
-        [((tall, width), F32), ((rows, width), F32), ((orders, width), F32), ((orders, orders), F32)],
+        [STAYS] * 4 + [whole(8, 128)],
+        [VMEM((tall, width), F32), VMEM((rows, width), F32), VMEM((orders, width), F32), VMEM((orders, orders), F32)]
+        + [((8, 128), F32)],
         "begin",
-        [pltpu.VMEM((tall, rows), F32), pltpu.VMEM((2, tall, rows), BF16)] + [pltpu.VMEM((rows, rows), BF16)] * 2,
-    )(where, weight, cost_rows, u, u, fh, fl, fh, fl)
+        [VMEM((tall, rows), F32), VMEM((2, tall, rows), BF16)] + [VMEM((rows, rows), BF16)] * 2,
+    )(where, weight, outside(cost_rows), u, *[outside(f) for f in (fh, fl, fh, fl)])
 
 
 def stage_kernel(options, size, where, weight, *refs):
     arrived = refs[:options]
-    v, n_in, fh, fl, bh, bl, s_in, g_in, h_in, *refs = refs[options:]
+    u, n_in, fh, fl, bh, bl, s_in, g_in, h_in, *refs = refs[options:]
     if size > 1:
-        u, s_out, g_out, h_out, n_out, done, pair, xh, xl = refs
+        s_out, g_out, h_out, n_out, token, done, pair, xh, xl = refs
     else:
-        s_out, g_out, h_out, done, pair, xh, xl = refs
+        s_out, g_out, h_out, token, done, pair, xh, xl = refs
     g = pl.program_id(0)
-    n = xh.shape[0] // arrived[0].shape[1]
+    token[...] = jnp.zeros_like(token)
+    rows = xh.shape[0]
+    orders = g_out.shape[0]
+    tile = fh.shape[1]
+    f = where[1]
+    v = column(u, f, rows)
     for c in range(options):
         for t in range(size):
 
             @pl.when((g == t) & (where[0] == c))
             def _():
-                unpack(arrived[c], t, n, xh, xl)
+                unpack(arrived[c], t, rows // arrived[c].shape[1], xh, xl)
 
     @pl.when(g == 0)
     def _():
-        multiply(done, v, (xh, xl), NN, STAGE_TILE, n_in)
+        multiply(done, v, (xh, xl), NN, column(n_in, f, rows))
 
     if size > 1:
 
         @pl.when((g > 0) & (g < size))
         def _():
-            multiply(done, u, (xh, xl), NT, STAGE_TILE, done)
-            multiply(n_out, v, (xh, xl), NN, STAGE_TILE, n_in)
+            c = where[1 + g]
+            multiply(done, column(u, c, rows), (xh, xl), NT, done)
+            multiply(column(n_out, c, rows), v, (xh, xl), NN, column(n_in, c, rows))
 
     @pl.when(g == size)
     def _():
         pair[0], pair[1] = split(done[...] * weight[0])
-        orders = h_out.shape[0]
         h_out[...] = h_in[...] + dot3(pair[:, :orders], (bh[...], bl[...]))
 
     @pl.when(g >= size)
     def _():
-        orders = g_out.shape[0]
-        multiply(g_out, pair.at[:, :orders], (fh, fl), NN, STAGE_TILE, g_in)
-        multiply(s_out, pair.at[:, orders:], (fh, fl), NN, STAGE_TILE, s_in)
+        at = g - size
+        multiply(column(g_out, at, tile), pair.at[:, :orders], (fh, fl), NN, column(g_in, at, tile))
+        multiply(column(s_out, at, tile), pair.at[:, orders:], (fh, fl), NN, column(s_in, at, tile))
 
 
 def stage(where, weight, arrived, size, u, n, fh, fl, sums, after=(), through=()):
     tall, width = n.shape
     rows, orders = sums[0].shape[0], sums[1].shape[0]
     tile = 512
-
-    def place(g, where):
-        return where[1 + jnp.minimum(g, size - 1)]
-
-    def later(g, where):
-        return where[1 + jnp.clip(g, 1, size - 1)]
-
-    def turn(g):
-        return jnp.maximum(g - size, 0)
-
-    block = pl.BlockSpec((tall, rows), lambda g, where, _: (0, place(g, where)))
-    beyond = pl.BlockSpec((tall, rows), lambda g, where, _: (0, later(g, where)))
-    u_beyond = pl.BlockSpec((2, tall, rows), lambda g, where, _: (0, 0, later(g, where)))
-    u_focus = pl.BlockSpec((2, tall, rows), lambda g, where, _: (0, 0, where[1]))
-    factor = pl.BlockSpec((rows, tile), lambda g, where, _: (where[1], turn(g)))
-    s_spec = pl.BlockSpec((rows, tile), lambda g, *_: (0, turn(g)))
-    g_spec = pl.BlockSpec((orders, tile), lambda g, *_: (0, turn(g)))
+    factor = pl.BlockSpec((rows, tile), lambda g, where, _: (where[1], jnp.maximum(g - size, 0)))
     control = pl.BlockSpec((rows, orders), lambda g, where, _: (where[1], width // orders))
     first = 2 + len(arrived)
     more = size > 1
+    shapes = [VMEM((rows, width), F32), VMEM((orders, width), F32), VMEM((orders, orders), F32)]
     return call(
         functools.partial(stage_kernel, len(arrived), size),
         (size + width // tile,),
         2,
-        [whole(*x.shape) for x in arrived]
-        + [u_focus, block, factor, factor, control, control, s_spec, g_spec, whole(orders, orders)]
-        + [u_beyond] * more,
-        [s_spec, g_spec, whole(orders, orders)] + [beyond] * more,
-        [((rows, width), F32), ((orders, width), F32), ((orders, orders), F32)] + [((tall, width), F32)] * more,
+        [whole(*x.shape) for x in arrived] + [STAYS, STAYS, factor, factor, control, control] + [STAYS] * 3,
+        [STAYS] * (3 + more) + [whole(8, 128)],
+        shapes + [VMEM((tall, width), F32)] * more + [((8, 128), F32)],
         "stage",
-        [pltpu.VMEM((tall, rows), F32), pltpu.VMEM((2, tall, rows), BF16)] + [pltpu.VMEM((rows, rows), BF16)] * 2,
+        [VMEM((tall, rows), F32), VMEM((2, tall, rows), BF16)] + [VMEM((rows, rows), BF16)] * 2,
         {first + 6: 0, first + 7: 1, first + 8: 2, **({first + 1: 3} if more else {})},
         after,
         through,
-    )(where, weight, *arrived, u, n, fh, fl, fh, fl, *sums, *([u] if more else []))
-
-
-def final_kernel(where, h_ref, g1, g2, s1, s2, q1, q2, d_ref, x_ref, y_ref, bh, bl, gain, out, reached, pair, q):
+    )(where, weight, *arrived, u, n, *[outside(f) for f in (fh, fl, fh, fl)], *sums)
+
+
+def final_kernel(where, h_ref, s_own, g_own, g2, s2, q2, d_ref, x_ref, y_ref, bh, bl, gain, out, reached, pair, q):
     n = pl.program_id(0)
     rows = out.shape[0]
 
     @pl.when(n == 0)
     def _():
-        value = -dot3(split(h_ref[...]), split(g1[...] + g2[...]))
+        value = -dot3(split(h_ref[...]), split(column(g_own, where[0], rows)[...] + g2[...]))
         gain[...] = value
         pair[0], pair[1] = split(value.T)
         q[...] = jnp.zeros_like(q)
 
-    cross = split(q1[...] + q2[...])
-    part = s1[...] + s2[...] + dot3(pair[...], cross)
+    cross = split(column(g_own, n, rows)[...] + q2[...])
+    part = column(s_own, n, rows)[...] + s2[...] + dot3(pair[...], cross)
     diag = lax.broadcasted_iota(jnp.int32, (rows, rows), 0) == lax.broadcasted_iota(jnp.int32, (rows, rows), 1)
     out[...] = part + jnp.where(diag & (n == where[0]), d_ref[...], 0.0)
     q[...] += dot3(cross, split(x_ref[...]))
@@ -528,13 +527,13 @@
         final_kernel,
         (width // rows,),
         1,
-        [whole(orders, orders), mine, mine, s_spec, s_spec, g_spec, g_spec, whole(1, rows)]
+        [whole(orders, orders), STAYS, STAYS, mine, s_spec, g_spec, whole(1, rows)]
         + [pl.BlockSpec((rows, samples), lambda n, where: (n, 0)), whole(rows, samples), factor, factor],
         [whole(orders, rows), s_spec, whole(rows, samples)],
         [((orders, rows), F32), ((rows, width), F32), ((rows, samples), F32)],
         "final",
         [pltpu.VMEM((2, rows, orders), BF16), pltpu.VMEM((orders, samples), F32)],
-    )(where, hinv, own[1], other[1], own[0], other[0], own[1], other[1], state_cost[None], x, y, fh, fl)
+    )(where, hinv, *own, other[1], *other, state_cost[None], x, y, outside(fh), outside(fl))
 
 
 def image_kernel(where, weight, fh, fl, p_ref, out, acc):
@@ -626,23 +625,23 @@
 
     pair = moved(pair, (0, 1), (1, 0), (2, 3), (3, 2))
     mid = across(mid)
-    n, *sums = begin(z[None], weight, cost_rows, u, fh, fl)
-    (mid,) = passed([mid], n)
+    n, *sums, token = begin(z[None], weight, cost_rows, u, fh, fl)
+    (mid,) = passed([mid], token)
     end = to_end(mid)
     mid_last = across(front(pair, lead))
     where = jnp.stack([z * 0, z ^ 1, second, third])
-    *sums, n = stage(where, weight, [pair], 3, u, n, fh, fl, sums)
-    (mid_last,) = passed([mid_last], n)
+    *sums, n, token = stage(where, weight, [pair], 3, u, n, fh, fl, sums)
+    (mid_last,) = passed([mid_last], token)
     end_last = to_end(mid_last)
     where = jnp.stack([edge, second, third])
-    *sums, n = stage(where, weight, [mid, end], 2, u, n, fh, fl, sums)
-    halves = collect(edge[None], [pair, mid, end, mid_last, end_last], n)
+    *sums, n, token = stage(where, weight, [mid, end], 2, u, n, fh, fl, sums)
+    halves = collect(edge[None], [pair, mid, end, mid_last, end_last], token)
     where = jnp.stack([edge, third])
-    s, g, h = stage(where, weight, [mid_last, end_last], 1, u, n, fh, fl, sums, [halves])
+    s, g, h, token = stage(where, weight, [mid_last, end_last], 1, u, n, fh, fl, sums, [halves])
     where = jnp.stack([core, z, z ^ 1, second, third, parent])
-    x, y = drift(where, parent_state, halves, swapped(halves), fh, fl, h)
+    x, y = drift(where, parent_state, halves, swapped(halves), fh, fl, token)
     other = swapped(h)
-    return h, other, passed([s, g], other, y), x, y
+    return h, other, passed([s, g], other, y, keep=True), x, y
 
 
 def swapped(x):

time: 210 us -> 222 us (1.057); the launches traced: 209 us -> 218 us
  local copies, waits for them, and re-layouts: 6.88 us -> 50.3 us
  Pallas kernels: 173 us -> 148 us
  waiting for transfers between devices: 15.2 us -> 8.33 us
    unnamed x16 -> x54, local copies, waits for them, and re-layouts: 5.54 us -> 50.1 us
    pallas_call x15, Pallas kernels: 173 us -> 148 us  [run(): built(*args[:prefetch], *placed, *after, *[resident(x) if keep else x for...]
    ppermute x5, waiting for transfers between devices: 13.2 us -> 6.06 us  [moved(): return lax.ppermute(x, 'row', pairs)]
  transfers between devices with their start and end apart: 9 -> 9, of which waited for: 3 -> 2; matrix products, arithmetic and copies ran while one was open for 2% -> 0% of each run, Pallas kernels for 63% -> 52%
where the time goes in v5:
time: 222 us; the launch traced here: 218 us
  Pallas kernels  148 us (67%)
  local copies, waits for them, and re-layouts  50.3 us (23%)
  starting transfers between devices  10.4 us (5%)
  waiting for transfers between devices  8.33 us (4%)
    pallas_call x15, Pallas kernels, run(): built(*args[:prefetch], *placed, *after, *[resident(x) if keep else x for...  148 us
    unnamed x54, local copies, waits for them, and re-layouts  50.1 us
    ppermute x5, starting transfers between devices, moved(): return lax.ppermute(x, 'row', pairs)  9.27 us
    ppermute x5, waiting for transfers between devices, moved(): return lax.ppermute(x, 'row', pairs)  6.06 us
  transfers between devices with their start and end apart: 9, of which 2 were waited for; matrix products, arithmetic and copies ran while one was open for 0% of the time, Pallas kernels for 52%

profile of v5, /device:TPU:0, one launch (start us, length us, event | category | flops | bytes accessed | tf_op | source)
XLA Modules:
  0.0 218.3 jit_solution(4849574011991689969)
XLA Ops:
  0.7 4.2 %pack.2.refs_4_.refs_5_ = f32[44,128,128]{2,1,0:T(8,128)} custom-call(s32[5]{0:T(128)S(1)} %stack.69.refs_0_, f32[512,2048]{1,0:T(8,128)} %bitcast.19, f32[4,512,128]{2,1,0:T(8,128)} %refs_1_.6, f32[512,2048]{1,0:T(8,128)} %bitcast.20, f32[512,2048]{1,0:T(8,128)} %bitcast.21), custom_call_target="tpu_custom_call" | custom-call | flops 1 | bytes 1 | tf_op jit(solution)/shard_map/pack/pallas_call | solution.py:95
  5.0 3.0 %collective-permute-start = (f32[44,128,128]{2,1,0:T(8,128)}, f32[44,128,128]{2,1,0:T(8,128)S(1)}, u32[]{:S(2)}, u32[]{:S(2)}) collective-permute-start(f32[44,128,128]{2,1,0:T(8,128)} %pack.2.refs_4_.refs_5_), channel_id=1, source_target_pairs={{0,1},{1,0},{2,3},{3,2},{4,5},{5,4},{6,7},{7,6},{8,9},{9,8},{10,11... | collective-permute-start | bytes 8650760 | tf_op jit(solution)/shard_map/ppermute | solution.py:618
  8.1 3.6 %pack.3.refs_6_ = f32[28,128,128]{2,1,0:T(8,128)} custom-call(s32[4]{0:T(128)S(1)} %pad_add_fusion.2.refs_0_, f32[512,2048]{1,0:T(8,128)} %bitcast.22, f32[4,512,128]{2,1,0:T(8,128)} %refs_1_.6, f32[512,2048]{1,0:T(8,128)} %bitcast.23, f32[44,128,128]{2,1,0:T(8,128)} %pack.2.refs_4_.refs_5_), custom_call_target="tpu_custom_call" | custom-call | flops 1 | bytes 1 | tf_op jit(solution)/shard_map/pack/pallas_call | solution.py:95
  13.8 15.0 %dense.1 = (bf16[2048,2560]{1,0:T(8,128)(2,1)}, bf16[2048,2560]{1,0:T(8,128)(2,1)}, bf16[2,1024,2048]{2,1,0:T(8,128)(2,1)S(1)}) custom-call(s32[1]{0:T(128)} %bitcast.refs_0_, s32[1,16,8]{2,1,0:T(8,128)S(1)} %copy.27.refs_1_, s32[1,16,2]{2,1,0:T(8,128)S(1)} %copy.28.refs_2_, f32[16,8,128,128]{3,2,1,0:T(8,128)} %bitcast.25, f32[16,2,128,128]{3,2,1,0:T(8,128)} %bitcast.26, ...), custom_call_target="tpu_custom_call" | custom-call | flops 1 | bytes 1 | tf_op jit(solution)/shard_map/dense/pallas_call | solution.py:95
  29.4 27.4 %begin.1 = (f32[1024,2048]{1,0:T(8,128)S(1)}, f32[512,2048]{1,0:T(8,128)S(1)}, f32[512,2048]{1,0:T(8,128)S(1)}, f32[512,512]{1,0:T(8,128)}, f32[8,128]{1,0:T(8,128)S(1)}) custom-call(s32[1]{0:T(128)} %bitcast.refs_0_, f32[1]{0:T(128)S(6)} %copy.44.refs_1_, f32[512,2048]{1,0:T(8,128)} %bitcast.24, ...), custom_call_target="tpu_custom_call" | custom-call | flops 1 | bytes 1 | tf_op jit(solution)/shard_map/begin/pallas_call | solution.py:95
  60.9 3.3 %copy-done.16 = f32[1024,2048]{1,0:T(8,128)} copy-done((f32[1024,2048]{1,0:T(8,128)}, f32[1024,2048]{1,0:T(8,128)S(1)}, u32[]{:S(2)}) %copy-start.16) | copy-done | bytes 8388632
  65.5 6.0 %collective-permute-done.refs_2_.refs_0_.refs_1_ = f32[44,128,128]{2,1,0:T(8,128)S(1)} collective-permute-done((f32[44,128,128]{2,1,0:T(8,128)}, f32[44,128,128]{2,1,0:T(8,128)S(1)}, u32[]{:S(2)}, u32[]{:S(2)}) %collective-permute-start) | collective-permute-done | bytes 2883616 | tf_op jit(solution)/shard_map/ppermute | solution.py:618
  74.1 3.4 %copy-done.1 = bf16[2,1024,2048]{2,1,0:T(8,128)(2,1)S(1)} copy-done((bf16[2,1024,2048]{2,1,0:T(8,128)(2,1)S(1)}, bf16[2,1024,2048]{2,1,0:T(8,128)(2,1)}, u32[]{:S(2)}) %copy-start.1) | copy-done | bytes 8388632
  77.5 2.2 %copy-done.5 = f32[512,2048]{1,0:T(8,128)S(1)} copy-done((f32[512,2048]{1,0:T(8,128)S(1)}, f32[512,2048]{1,0:T(8,128)}, u32[]{:S(2)}) %copy-start.5) | copy-done | bytes 4194328
  79.7 2.2 %copy-done.11 = f32[512,2048]{1,0:T(8,128)S(1)} copy-done((f32[512,2048]{1,0:T(8,128)S(1)}, f32[512,2048]{1,0:T(8,128)}, u32[]{:S(2)}) %copy-start.11) | copy-done | bytes 4194328
  81.9 3.4 %copy-done.17 = f32[1024,2048]{1,0:T(8,128)S(1)} copy-done((f32[1024,2048]{1,0:T(8,128)S(1)}, f32[1024,2048]{1,0:T(8,128)}, u32[]{:S(2)}) %copy-start.17) | copy-done | bytes 8388632
  85.3 21.7 %stage.3 = (f32[512,2048]{1,0:T(8,128)S(1)}, f32[512,2048]{1,0:T(8,128)S(1)}, f32[512,512]{1,0:T(8,128)}, f32[1024,2048]{1,0:T(8,128)S(1)}, f32[8,128]{1,0:T(8,128)S(1)}) custom-call(s32[4]{0:T(128)S(1)} %pad_add_fusion.1.refs_0_, f32[1]{0:T(128)S(6)} %copy.44.refs_1_, ...), custom_call_target="tpu_custom_call", output_to_operand_aliasing={{0}: (9, {}), {1}: (10, {}), {2}: (11, {}), {3}: (4, {})} | custom-call | flops 1 | bytes 1 | tf_op jit(solution)/shard_map/stage/pallas_call | solution.py:95
  111.0 3.3 %copy-done.18 = f32[1024,2048]{1,0:T(8,128)} copy-done((f32[1024,2048]{1,0:T(8,128)}, f32[1024,2048]{1,0:T(8,128)S(1)}, u32[]{:S(2)}) %copy-start.18) | copy-done | bytes 8388632
  116.0 3.4 %copy-done.2 = bf16[2,1024,2048]{2,1,0:T(8,128)(2,1)S(1)} copy-done((bf16[2,1024,2048]{2,1,0:T(8,128)(2,1)S(1)}, bf16[2,1024,2048]{2,1,0:T(8,128)(2,1)}, u32[]{:S(2)}) %copy-start.2) | copy-done | bytes 8388632
  119.4 2.2 %copy-done.7 = f32[512,2048]{1,0:T(8,128)S(1)} copy-done((f32[512,2048]{1,0:T(8,128)S(1)}, f32[512,2048]{1,0:T(8,128)}, u32[]{:S(2)}) %copy-start.7) | copy-done | bytes 4194328
  123.8 3.4 %copy-done.19 = f32[1024,2048]{1,0:T(8,128)S(1)} copy-done((f32[1024,2048]{1,0:T(8,128)S(1)}, f32[1024,2048]{1,0:T(8,128)}, u32[]{:S(2)}) %copy-start.19) | copy-done | bytes 8388632
  127.1 19.1 %stage.4 = (f32[512,2048]{1,0:T(8,128)S(1)}, f32[512,2048]{1,0:T(8,128)S(1)}, f32[512,512]{1,0:T(8,128)}, f32[1024,2048]{1,0:T(8,128)S(1)}, f32[8,128]{1,0:T(8,128)S(1)}) custom-call(s32[3]{0:T(128)S(1)} %pad_add_fusion.3.refs_0_, f32[1]{0:T(128)S(6)} %copy.44.refs_1_, ...), custom_call_target="tpu_custom_call", output_to_operand_aliasing={{0}: (10, {}), {1}: (11, {}), {2}: (12, {}), {3}: (5, {})} | custom-call | flops 1 | bytes 1 | tf_op jit(solution)/shard_map/stage/pallas_call | solution.py:95
  146.2 3.3 %copy-done.20 = f32[1024,2048]{1,0:T(8,128)} copy-done((f32[1024,2048]{1,0:T(8,128)}, f32[1024,2048]{1,0:T(8,128)S(1)}, u32[]{:S(2)}) %copy-start.20) | copy-done | bytes 8388632
  153.2 3.4 %copy-done.3 = bf16[2,1024,2048]{2,1,0:T(8,128)(2,1)S(1)} copy-done((bf16[2,1024,2048]{2,1,0:T(8,128)(2,1)S(1)}, bf16[2,1024,2048]{2,1,0:T(8,128)(2,1)}, u32[]{:S(2)}) %copy-start.3) | copy-done | bytes 8388632
  156.6 14.7 %stage.5 = (f32[512,2048]{1,0:T(8,128)S(1)}, f32[512,2048]{1,0:T(8,128)S(1)}, f32[512,512]{1,0:T(8,128)}, f32[8,128]{1,0:T(8,128)S(1)}) custom-call(s32[2]{0:T(128)S(1)} %pad_add_fusion.refs_0_, f32[1]{0:T(128)S(6)} %copy.44.refs_1_, f32[12,128,128]{2,1,0:T(8,128)} %passed.3.refs_4_.refs_2_, ...), custom_call_target="tpu_custom_call", output_to_operand_aliasing={{0}: (10, {}), {1}: (11, {}), {2}: (12, {})} | custom-call | flops 1 | bytes 1 | tf_op jit(solution)/shard_map/stage/pallas_call | solution.py:95
  175.9 2.3 %collective-permute-done.6.refs_3_ = f32[6,128,128]{2,1,0:T(8,128)S(1)} collective-permute-done((f32[6,128,128]{2,1,0:T(8,128)S(1)}, f32[6,128,128]{2,1,0:T(8,128)S(1)}, u32[]{:S(2)}, u32[]{:S(2)}) %collective-permute-start.6) | collective-permute-done | bytes 393248 | tf_op jit(solution)/shard_map/ppermute | solution.py:649
  178.2 5.7 %drift.1 = (f32[2048,128]{1,0:T(8,128)S(1)}, f32[512,128]{1,0:T(8,128)S(1)}) custom-call(s32[6]{0:T(128)S(1)} %stack.73.refs_0_, f32[4,512,128]{2,1,0:T(8,128)} %refs_1_.6, f32[6,128,128]{2,1,0:T(8,128)S(1)} %collect.1.refs_13_.refs_2_, f32[6,128,128]{2,1,0:T(8,128)S(1)} %collective-permute-done.6.refs_3_, ...), custom_call_target="tpu_custom_call" | custom-call | flops 1 | bytes 1 | tf_op jit(solution)/shard_map/drift/pallas_call | solution.py:95
  184.6 20.9 %inverse.1.refs_1_ = f32[512,512]{1,0:T(8,128)S(1)} custom-call(f32[512,512]{1,0:T(8,128)} %get-tuple-element.50.refs_0_, f32[512,512]{1,0:T(8,128)S(1)} %collective-permute-done.5.refs_1_.refs_0_, f32[1,512]{1,0:T(1,128)S(1)} %bitcast.18), custom_call_target="tpu_custom_call" | custom-call | flops 1 | bytes 1 | tf_op jit(solution)/shard_map/inverse/pallas_call | solution.py:95
  205.6 12.7 %final.1 = (f32[512,512]{1,0:T(8,128)}, f32[512,2048]{1,0:T(8,128)}, f32[512,128]{1,0:T(8,128)}) custom-call(s32[1]{0:T(128)} %bitcast.refs_0_, f32[512,512]{1,0:T(8,128)S(1)} %inverse.1.refs_1_, f32[512,2048]{1,0:T(8,128)S(1)} %get-tuple-element.55.refs_2_, f32[512,2048]{1,0:T(8,128)S(1)} %get-tuple-element.56.refs_3_, ...), custom_call_target="tpu_custom_call" | custom-call | flops 1 | bytes 1 | tf_op jit(solution)/shard_map/final/pallas_call | solution.py:95
  (69 shorter events, 26.9 us)
Async XLA Ops:
  5.0 66.5 %collective-permute-start = (f32[44,128,128]{2,1,0:T(8,128)}, f32[44,128,128]{2,1,0:T(8,128)S(1)}, u32[]{:S(2)}, u32[]{:S(2)}) collective-permute-start(f32[44,128,128]{2,1,0:T(8,128)} %pack.2.refs_4_.refs_5_), channel_id=1, source_target_pairs={{0,1},{1,0},{2,3},{3,2},{4,5},{5,4},{6,7},{7,6},{8,9},{9,8},{10,11... | collective-permute-start | bytes 8650760 | tf_op jit(solution)/shard_map/ppermute | solution.py:618
  8.1 5.5 %copy-start.24 = (s32[1,16,8]{1,2,0:T(8,128)S(1)}, s32[1,16,8]{1,2,0:T(8,128)}, u32[]{:S(2)}) copy-start(s32[1,16,8]{1,2,0:T(8,128)} %param.11) | copy-start | bytes 1540
  8.1 5.6 %copy-start.25 = (s32[1,16,2]{1,2,0:T(2,128)S(1)}, s32[1,16,2]{1,2,0:T(2,128)}, u32[]{:S(2)}) copy-start(s32[1,16,2]{1,2,0:T(2,128)} %param.13) | copy-start | bytes 388
  11.7 52.5 %collective-permute-start.3 = (f32[28,128,128]{2,1,0:T(8,128)}, f32[28,128,128]{2,1,0:T(8,128)}, u32[]{:S(2)}, u32[]{:S(2)}) collective-permute-start(f32[28,128,128]{2,1,0:T(8,128)} %pack.3.refs_6_), channel_id=1, source_target_pairs={{1,2},{2,1},{5,6},{6,5},{9,10},{10,9},{13,14},{14,13},{17,18},{18,... | collective-permute-start | bytes 5505032 | tf_op jit(solution)/shard_map/ppermute | solution.py:618
  28.8 28.1 %copy-start = (bf16[2,1024,2048]{2,1,0:T(8,128)(2,1)}, bf16[2,1024,2048]{2,1,0:T(8,128)(2,1)S(1)}, u32[]{:S(2)}) copy-start(bf16[2,1024,2048]{2,1,0:T(8,128)(2,1)S(1)} %get-tuple-element.32.refs_3_.refs_4_) | copy-start | bytes 25165828
  60.9 3.3 %copy-start.16 = (f32[1024,2048]{1,0:T(8,128)}, f32[1024,2048]{1,0:T(8,128)S(1)}, u32[]{:S(2)}) copy-start(f32[1024,2048]{1,0:T(8,128)S(1)} %get-tuple-element.35.refs_4_) | copy-start | bytes 25165828
  64.2 51.8 %collective-permute-start.4 = (f32[28,128,128]{2,1,0:T(8,128)}, f32[28,128,128]{2,1,0:T(8,128)}, u32[]{:S(2)}, u32[]{:S(2)}) collective-permute-start(f32[28,128,128]{2,1,0:T(8,128)} %passed.4.refs_2_), channel_id=1, source_target_pairs={{1,0},{2,3},{5,4},{6,7},{9,8},{10,11},{13,12},{14,15},{17,16},{18,... | collective-permute-start | bytes 5505032 | tf_op jit(solution)/shard_map/ppermute | solution.py:618
  72.5 41.8 %collective-permute-start.1 = (f32[12,128,128]{2,1,0:T(8,128)}, f32[12,128,128]{2,1,0:T(8,128)}, u32[]{:S(2)}, u32[]{:S(2)}) collective-permute-start(f32[12,128,128]{2,1,0:T(8,128)} %front.1), channel_id=1, source_target_pairs={{1,2},{2,1},{5,6},{6,5},{9,10},{10,9},{13,14},{14,13},{17,18},{18,... | collective-permute-start | bytes 2359304 | tf_op jit(solution)/shard_map/ppermute | solution.py:618
  74.1 3.4 %copy-start.1 = (bf16[2,1024,2048]{2,1,0:T(8,128)(2,1)S(1)}, bf16[2,1024,2048]{2,1,0:T(8,128)(2,1)}, u32[]{:S(2)}) copy-start(bf16[2,1024,2048]{2,1,0:T(8,128)(2,1)} %copy-done) | copy-start | bytes 25165828
  81.9 3.4 %copy-start.17 = (f32[1024,2048]{1,0:T(8,128)S(1)}, f32[1024,2048]{1,0:T(8,128)}, u32[]{:S(2)}) copy-start(f32[1024,2048]{1,0:T(8,128)} %copy-done.16) | copy-start | bytes 25165828
  111.0 3.3 %copy-start.18 = (f32[1024,2048]{1,0:T(8,128)}, f32[1024,2048]{1,0:T(8,128)S(1)}, u32[]{:S(2)}) copy-start(f32[1024,2048]{1,0:T(8,128)S(1)} %get-tuple-element.41.refs_5_) | copy-start | bytes 25165828
  114.3 35.3 %collective-permute-start.2 = (f32[12,128,128]{2,1,0:T(8,128)}, f32[12,128,128]{2,1,0:T(8,128)}, u32[]{:S(2)}, u32[]{:S(2)}) collective-permute-start(f32[12,128,128]{2,1,0:T(8,128)} %passed.3.refs_4_.refs_2_), channel_id=1, source_target_pairs={{1,0},{2,3},{5,4},{6,7},{9,8},{10,11},{13,12},{14,15},{17,16},{18,... | collective-permute-start | bytes 2359304 | tf_op jit(solution)/shard_map/ppermute | solution.py:618
  116.0 3.4 %copy-start.2 = (bf16[2,1024,2048]{2,1,0:T(8,128)(2,1)S(1)}, bf16[2,1024,2048]{2,1,0:T(8,128)(2,1)}, u32[]{:S(2)}) copy-start(bf16[2,1024,2048]{2,1,0:T(8,128)(2,1)} %copy-done) | copy-start | bytes 25165828
  123.8 3.4 %copy-start.19 = (f32[1024,2048]{1,0:T(8,128)S(1)}, f32[1024,2048]{1,0:T(8,128)}, u32[]{:S(2)}) copy-start(f32[1024,2048]{1,0:T(8,128)} %copy-done.18) | copy-start | bytes 25165828
  146.2 3.3 %copy-start.20 = (f32[1024,2048]{1,0:T(8,128)}, f32[1024,2048]{1,0:T(8,128)S(1)}, u32[]{:S(2)}) copy-start(f32[1024,2048]{1,0:T(8,128)S(1)} %get-tuple-element.45.refs_5_) | copy-start | bytes 25165828
  149.6 3.6 %copy-start.21 = (f32[1024,2048]{1,0:T(8,128)S(1)}, f32[1024,2048]{1,0:T(8,128)}, u32[]{:S(2)}) copy-start(f32[1024,2048]{1,0:T(8,128)} %copy-done.20) | copy-start | bytes 25165828
  153.2 3.4 %copy-start.3 = (bf16[2,1024,2048]{2,1,0:T(8,128)(2,1)S(1)}, bf16[2,1024,2048]{2,1,0:T(8,128)(2,1)}, u32[]{:S(2)}) copy-start(bf16[2,1024,2048]{2,1,0:T(8,128)(2,1)} %copy-done) | copy-start | bytes 25165828
  175.3 8.6 %collective-permute-start.5 = (f32[512,512]{1,0:T(8,128)}, f32[512,512]{1,0:T(8,128)S(1)}, u32[]{:S(2)}, u32[]{:S(2)}) collective-permute-start(f32[512,512]{1,0:T(8,128)} %get-tuple-element.50.refs_0_), channel_id=1, source_target_pairs={{0,4},{4,0},{8,12},{12,8},{16,20},{20,16},{24,28},{28,24},{1,5},{5... | collective-permute-start | bytes 3145736 | tf_op jit(solution)/shard_map/ppermute | solution.py:649
  175.3 2.8 %collective-permute-start.6 = (f32[6,128,128]{2,1,0:T(8,128)S(1)}, f32[6,128,128]{2,1,0:T(8,128)S(1)}, u32[]{:S(2)}, u32[]{:S(2)}) collective-permute-start(f32[6,128,128]{2,1,0:T(8,128)S(1)} %collect.1.refs_13_.refs_2_), channel_id=1, source_target_pairs={{0,4},{4,0},{8,12},{12,8},{16,20},{20,16},{24,28},{28,24},{1,5},{5... | collective-permute-start | bytes 1179656 | tf_op jit(solution)/shard_map/ppermute | solution.py:649
  178.2 5.7 %copy-start.9 = (f32[512,2048]{1,0:T(8,128)S(1)}, f32[512,2048]{1,0:T(8,128)}, u32[]{:S(2)}) copy-start(f32[512,2048]{1,0:T(8,128)} %copy-done.8) | copy-start | bytes 12582916
  178.2 5.7 %copy-start.15 = (f32[512,2048]{1,0:T(8,128)S(1)}, f32[512,2048]{1,0:T(8,128)}, u32[]{:S(2)}) copy-start(f32[512,2048]{1,0:T(8,128)} %copy-done.14) | copy-start | bytes 12582916
  183.9 21.6 %copy-start.22 = (f32[512]{0:T(512)S(1)}, f32[512]{0:T(512)}, u32[]{:S(2)}) copy-start(f32[512]{0:T(512)} %param.15) | copy-start | bytes 6148
  183.9 21.6 %collective-permute-start.7 = (f32[512,2048]{1,0:T(8,128)S(1)}, f32[512,2048]{1,0:T(8,128)S(1)}, u32[]{:S(2)}, u32[]{:S(2)}) collective-permute-start(f32[512,2048]{1,0:T(8,128)S(1)} %get-tuple-element.56.refs_3_), channel_id=1, source_target_pairs={{0,4},{4,0},{8,12},{12,8},{16,20},{20,16},{24,28},{28,24},{1,5},{5... | collective-permute-start | bytes 12582920 | tf_op jit(solution)/shard_map/ppermute | solution.py:649
  184.4 21.2 %collective-permute-start.8 = (f32[512,2048]{1,0:T(8,128)S(1)}, f32[512,2048]{1,0:T(8,128)S(1)}, u32[]{:S(2)}, u32[]{:S(2)}) collective-permute-start(f32[512,2048]{1,0:T(8,128)S(1)} %get-tuple-element.55.refs_2_), channel_id=1, source_target_pairs={{0,4},{4,0},{8,12},{12,8},{16,20},{20,16},{24,28},{28,24},{1,5},{5... | collective-permute-start | bytes 12582920 | tf_op jit(solution)/shard_map/ppermute | solution.py:649
  (11 other events, 21.5 us)

commit v6 on v5

--- a/solution.py
+++ b/solution.py
@@ -9,7 +9,6 @@
 
 F32 = jnp.float32
 BF16 = jnp.bfloat16
-VMEM_LIMIT = 24 * 2**20
 NN = (((1,), (0,)), ((), ()))
 NT = (((1,), (1,)), ((), ()))
 
@@ -33,6 +32,7 @@
 
 
 TILE = (256, 512)
+OWN, PARTNER, SECOND, THIRD, PARENT, CORE, NEAR, EDGE = range(8)
 VMEM = pltpu.VMEM
 STAYS = pl.BlockSpec(memory_space=VMEM)
 
@@ -60,7 +60,7 @@
             out[rows, cols] = value if add is None else add[rows, cols] + value
 
 
-def call(kernel, grid, prefetch, ins, outs, shapes, name, scratch=(), aliases=None, after=(), through=(), keep=False):
+def call(kernel, grid, prefetch, ins, outs, shapes, name, scratch=(), aliases=None, after=(), through=(), keep=False, limit=24):
     n_in, n_out = len(ins), len(outs)
     extra = len(after) + len(through)
     anywhere = pl.BlockSpec(memory_space=pl.ANY)
@@ -85,7 +85,7 @@
         out_shape=[x if isinstance(x, pl.MemoryRef) else jax.ShapeDtypeStruct(*x) for x in shapes]
         + [(VMEM if keep else jax.ShapeDtypeStruct)(x.shape, x.dtype) for x in through],
         input_output_aliases=aliases,
-        compiler_params=pltpu.CompilerParams(vmem_limit_bytes=VMEM_LIMIT),
+        compiler_params=pltpu.CompilerParams(vmem_limit_bytes=limit * 2**20),
         cost_estimate=pl.CostEstimate(flops=1, bytes_accessed=1, transcendentals=0),
         name=name,
     )
@@ -226,6 +226,7 @@
         [whole(n, n)],
         [((n, n), F32)],
         "inverse",
+        limit=10,
     )(mine, other, control_cost[None])[0]
 
 
@@ -242,13 +243,13 @@
         out[t] = tile
 
 
-def pack(where, cost_rows, parent_state, blk, after):
+def pack(where, blocks, cost_rows, parent_state, blk, after):
     rows = cost_rows.shape[0]
     samples = parent_state.shape[2]
-    picks = [0] + list(range(3, where.shape[0]))
+    picks = [OWN, *blocks]
     size = len(lower(rows // blk)) + 2 + (len(picks) - 1) * (rows // blk) ** 2
     specs = [pl.BlockSpec((rows, rows), functools.partial(lambda t, i, where: (0, where[t]), t)) for t in picks]
-    specs.insert(1, pl.BlockSpec((1, rows // 2, samples), lambda i, where: (where[1], where[2], 0)))
+    specs.insert(1, pl.BlockSpec((1, rows // 2, samples), lambda i, where: (where[PARENT], where[CORE], 0)))
     args = [outside(cost_rows)] * len(picks)
     args.insert(1, outside(parent_state))
     return call(
@@ -260,6 +261,7 @@
         [((size, blk, blk), F32)],
         "pack",
         after=after,
+        limit=16,
     )(where, *args)[0]
 
 
@@ -269,7 +271,7 @@
     def kernel(x, out):
         out[...] = x[...]
 
-    return call(kernel, (1,), 0, [whole(*shape)], [whole(*shape)], [(shape, F32)], "front")(message)[0]
+    return call(kernel, (1,), 0, [whole(*shape)], [whole(*shape)], [(shape, F32)], "front", limit=4)(message)[0]
 
 
 def unpack(tiles, step, n, xh, xl):
@@ -286,12 +288,12 @@
 def collect_kernel(where, pair, mid, end, mid_last, end_last, out):
     out[:2] = pair[...]
 
-    @pl.when(where[0] == 1)
+    @pl.when(where[EDGE] == 1)
     def _():
         out[2:4] = end[...]
         out[4:6] = end_last[...]
 
-    @pl.when(where[0] == 0)
+    @pl.when(where[EDGE] == 0)
     def _():
         out[2:4] = mid[...]
         out[4:6] = mid_last[...]
@@ -309,12 +311,13 @@
         [((6, blk, blk), F32)],
         "collect",
         after=[after],
+        limit=4,
     )(where, *messages)[0]
 
 
 def drift_kernel(where, own, mine, other, fh, fl, x_ref, out):
     g = pl.program_id(0)
-    core = where[0]
+    core = where[CORE]
     blk = mine.shape[1]
     rows = own.shape[1]
 
@@ -344,23 +347,24 @@
 def drift(where, parent_state, mine, other, fh, fl, after):
     _, rows, samples = parent_state.shape
     count, blk, _ = mine.shape
-    factor = pl.BlockSpec((rows, rows), lambda g, where: (where[1], where[1 + g]))
+    factor = pl.BlockSpec((rows, rows), lambda g, where: (where[OWN], where[OWN + g]))
     return call(
         drift_kernel,
         (4,),
         1,
-        [pl.BlockSpec((1, rows, samples), lambda g, where: (where[5], 0, 0))]
+        [pl.BlockSpec((1, rows, samples), lambda g, where: (where[PARENT], 0, 0))]
         + [whole(count, blk, blk)] * 2
         + [factor, factor],
-        [pl.BlockSpec((rows, samples), lambda g, where: (where[1 + g], 0)), whole(rows, samples)],
+        [pl.BlockSpec((rows, samples), lambda g, where: (where[OWN + g], 0)), whole(rows, samples)],
         [((4 * rows, samples), F32), ((rows, samples), F32)],
         "drift",
         after=[after],
+        limit=12,
     )(where, outside(parent_state), mine, other, outside(fh), outside(fl))
 
 
 def passed(arrays, *after, keep=False):
-    return call(lambda *_: None, (1,), 0, [], [], [], "passed", after=after, through=arrays, keep=keep)()
+    return call(lambda *_: None, (1,), 0, [], [], [], "passed", after=after, through=arrays, keep=keep, limit=1)()
 
 
 def begin_kernel(steps, where, weight, p_ref, u, fh, fl, bh, bl, n_out, s_out, g_out, h_out, token, mine, pair, ph, pl_):
@@ -420,10 +424,11 @@
         + [((8, 128), F32)],
         "begin",
         [VMEM((tall, rows), F32), VMEM((2, tall, rows), BF16)] + [VMEM((rows, rows), BF16)] * 2,
+        limit=18,
     )(where, weight, outside(cost_rows), u, *[outside(f) for f in (fh, fl, fh, fl)])
 
 
-def stage_kernel(options, size, where, weight, *refs):
+def stage_kernel(options, size, focus, where, weight, *refs):
     arrived = refs[:options]
     u, n_in, fh, fl, bh, bl, s_in, g_in, h_in, *refs = refs[options:]
     if size > 1:
@@ -435,12 +440,12 @@
     rows = xh.shape[0]
     orders = g_out.shape[0]
     tile = fh.shape[1]
-    f = where[1]
+    f = where[focus]
     v = column(u, f, rows)
     for c in range(options):
         for t in range(size):
 
-            @pl.when((g == t) & (where[0] == c))
+            @pl.when((g == t) & ((where[EDGE] == c) | (options == 1)))
             def _():
                 unpack(arrived[c], t, rows // arrived[c].shape[1], xh, xl)
 
@@ -452,7 +457,7 @@
 
         @pl.when((g > 0) & (g < size))
         def _():
-            c = where[1 + g]
+            c = where[focus + g]
             multiply(done, column(u, c, rows), (xh, xl), NT, done)
             multiply(column(n_out, c, rows), v, (xh, xl), NN, column(n_in, c, rows))
 
@@ -468,17 +473,17 @@
         multiply(column(s_out, at, tile), pair.at[:, orders:], (fh, fl), NN, column(s_in, at, tile))
 
 
-def stage(where, weight, arrived, size, u, n, fh, fl, sums, after=(), through=()):
+def stage(where, weight, arrived, focus, size, u, n, fh, fl, sums, after=()):
     tall, width = n.shape
     rows, orders = sums[0].shape[0], sums[1].shape[0]
     tile = 512
-    factor = pl.BlockSpec((rows, tile), lambda g, where, _: (where[1], jnp.maximum(g - size, 0)))
-    control = pl.BlockSpec((rows, orders), lambda g, where, _: (where[1], width // orders))
+    factor = pl.BlockSpec((rows, tile), lambda g, where, _: (where[focus], jnp.maximum(g - size, 0)))
+    control = pl.BlockSpec((rows, orders), lambda g, where, _: (where[focus], width // orders))
     first = 2 + len(arrived)
     more = size > 1
     shapes = [VMEM((rows, width), F32), VMEM((orders, width), F32), VMEM((orders, orders), F32)]
     return call(
-        functools.partial(stage_kernel, len(arrived), size),
+        functools.partial(stage_kernel, len(arrived), size, focus),
         (size + width // tile,),
         2,
         [whole(*x.shape) for x in arrived] + [STAYS, STAYS, factor, factor, control, control] + [STAYS] * 3,
@@ -488,7 +493,7 @@
         [VMEM((tall, rows), F32), VMEM((2, tall, rows), BF16)] + [VMEM((rows, rows), BF16)] * 2,
         {first + 6: 0, first + 7: 1, first + 8: 2, **({first + 1: 3} if more else {})},
         after,
-        through,
+        limit=20,
     )(where, weight, *arrived, u, n, *[outside(f) for f in (fh, fl, fh, fl)], *sums)
 
 
@@ -606,11 +611,8 @@
     return acc[:, :width], jnp.swapaxes(cross.reshape(width, -1), 0, 1)
 
 
-def by_blocks(z, core, parent, weight, cost_rows, parent_state, dense_parts, control_cost, messages):
+def by_blocks(where, weight, cost_rows, parent_state, dense_parts, messages):
     fh, fl, u = dense_parts
-    edge = ((z == 0) | (z == 3)).astype(jnp.int32)
-    left = z < 2
-    second, third = jnp.where(left, 2, 1), jnp.where(left, 3, 0)
     pair, mid = messages
     lead = 2 * mid.shape[0] - pair.shape[0]
 
@@ -625,20 +627,16 @@
 
     pair = moved(pair, (0, 1), (1, 0), (2, 3), (3, 2))
     mid = across(mid)
-    n, *sums, token = begin(z[None], weight, cost_rows, u, fh, fl)
+    n, *sums, token = begin(where, weight, cost_rows, u, fh, fl)
     (mid,) = passed([mid], token)
     end = to_end(mid)
     mid_last = across(front(pair, lead))
-    where = jnp.stack([z * 0, z ^ 1, second, third])
-    *sums, n, token = stage(where, weight, [pair], 3, u, n, fh, fl, sums)
+    *sums, n, token = stage(where, weight, [pair], PARTNER, 3, u, n, fh, fl, sums)
     (mid_last,) = passed([mid_last], token)
     end_last = to_end(mid_last)
-    where = jnp.stack([edge, second, third])
-    *sums, n, token = stage(where, weight, [mid, end], 2, u, n, fh, fl, sums)
-    halves = collect(edge[None], [pair, mid, end, mid_last, end_last], token)
-    where = jnp.stack([edge, third])
-    s, g, h, token = stage(where, weight, [mid_last, end_last], 1, u, n, fh, fl, sums, [halves])
-    where = jnp.stack([core, z, z ^ 1, second, third, parent])
+    *sums, n, token = stage(where, weight, [mid, end], SECOND, 2, u, n, fh, fl, sums)
+    halves = collect(where, [pair, mid, end, mid_last, end_last], token)
+    s, g, h, token = stage(where, weight, [mid_last, end_last], THIRD, 1, u, n, fh, fl, sums, [halves])
     x, y = drift(where, parent_state, halves, swapped(halves), fh, fl, token)
     other = swapped(h)
     return h, other, passed([s, g], other, y, keep=True), x, y
@@ -667,21 +665,19 @@
     parts = lax.axis_size("row")
     z = lax.axis_index("row")
     leaf = lax.axis_index("leaf")
-    core = leaf % 2
     line = parts == 4 and rows == orders
 
+    left = z < 2
+    near = jnp.where(left, 0, 3)
+    edge = ((z == 0) | (z == 3)).astype(jnp.int32)
+    where = jnp.stack([z, z ^ 1, jnp.where(left, 2, 1), 3 - near, leaf // 2, leaf % 2, near, edge])
     sent = []
     if line:
-        left = z < 2
-        near = jnp.where(left, 0, 3)
-        lead = [z, leaf // 2, core]
-        sent.append(pack(jnp.stack(lead + [jnp.where(left, 2, 1), 3 - near]), cost_rows, parent_state, blk, []))
-        sent.append(pack(jnp.stack(lead + [near]), cost_rows, parent_state, blk, sent))
-    fh, fl, u = parts_of = dense(z[None], rows, a_blocks[0], a_cols, b_blocks[0], b_cols, orders, sent)
+        sent.append(pack(where, [SECOND, THIRD], cost_rows, parent_state, blk, []))
+        sent.append(pack(where, [NEAR], cost_rows, parent_state, blk, sent))
+    fh, fl, u = parts_of = dense(where, rows, a_blocks[0], a_cols, b_blocks[0], b_cols, orders, sent)
     if line:
-        h, other_h, own, x, y = by_blocks(
-            z, core, leaf // 2, branch_prob, cost_rows, parent_state, parts_of, control_cost, sent
-        )
+        h, other_h, own, x, y = by_blocks(where, branch_prob, cost_rows, parent_state, parts_of, sent)
     else:
         w = dot3(parted(cost_rows), (fh[:, width:], fl[:, width:]))
         b_rows = [lax.dynamic_slice(f, (0, z * rows), (orders, rows)) for f in u]
@@ -693,7 +689,7 @@
         y = dot3([lax.dynamic_slice(f, (z * rows, 0), (rows, width)) for f in (fh, fl)], parted(x))
     hinv = inverse(h, other_h, control_cost, blk)
     other = tuple(swapped(x) for x in own)
-    gain, pcost, reached = final(z[None], hinv, own, other, state_cost, x, y, fh, fl)
+    gain, pcost, reached = final(where, hinv, own, other, state_cost, x, y, fh, fl)
     return pcost[None], gain[None], reached[None]
 
 

time: 222 us -> 190 us (0.86); the launches traced: 218 us -> 189 us
  local copies, waits for them, and re-layouts: 50.3 us -> 4.45 us
  waiting for transfers between devices: 8.33 us -> 35.4 us
  Pallas kernels: 148 us -> 138 us
    unnamed x54 -> x14, local copies, waits for them, and re-layouts: 50.1 us -> 4.37 us
    ppermute x5, waiting for transfers between devices: 6.06 us -> 32.7 us  [moved(): return lax.ppermute(x, 'row', pairs)]
    pallas_call x15, Pallas kernels: 148 us -> 138 us  [run(): built(*args[:prefetch], *placed, *after, *[resident(x) if keep else x for...]
  transfers between devices with their start and end apart: 9 -> 9, of which waited for: 2 -> 3; matrix products, arithmetic and copies ran while one was open for 0% -> 0% of each run, Pallas kernels for 52% -> 56%
where the time goes in v6:
time: 190 us; the launch traced here: 189 us
  Pallas kernels  138 us (73%)
  waiting for transfers between devices  35.4 us (19%)
  starting transfers between devices  9.75 us (5%)
  local copies, waits for them, and re-layouts  4.45 us (2%)
    pallas_call x15, Pallas kernels, run(): built(*args[:prefetch], *placed, *after, *[resident(x) if keep else x for...  138 us
    ppermute x5, waiting for transfers between devices, moved(): return lax.ppermute(x, 'row', pairs)  32.7 us
    ppermute x5, starting transfers between devices, moved(): return lax.ppermute(x, 'row', pairs)  8.61 us
    unnamed x14, local copies, waits for them, and re-layouts  4.37 us
  transfers between devices with their start and end apart: 9, of which 3 were waited for; matrix products, arithmetic and copies ran while one was open for 0% of the time, Pallas kernels for 56%

profile of v6, /device:TPU:0, one launch (start us, length us, event | category | flops | bytes accessed | tf_op | source)
XLA Modules:
  0.0 189.0 jit_solution(8004480656431955036)
XLA Ops:
  0.7 4.3 %pack.2.refs_4_.refs_5_ = f32[44,128,128]{2,1,0:T(8,128)} custom-call(s32[8]{0:T(128)S(1)} %stack.39.refs_0_, f32[512,2048]{1,0:T(8,128)} %bitcast.18, f32[4,512,128]{2,1,0:T(8,128)} %refs_1_.6, f32[512,2048]{1,0:T(8,128)} %bitcast.19, f32[512,2048]{1,0:T(8,128)} %bitcast.20), custom_call_target="tpu_custom_call" | custom-call | flops 1 | bytes 1 | tf_op jit(solution)/shard_map/pack/pallas_call | solution.py:95
  5.0 3.0 %collective-permute-start = (f32[44,128,128]{2,1,0:T(8,128)}, f32[44,128,128]{2,1,0:T(8,128)S(1)}, u32[]{:S(2)}, u32[]{:S(2)}) collective-permute-start(f32[44,128,128]{2,1,0:T(8,128)} %pack.2.refs_4_.refs_5_), channel_id=1, source_target_pairs={{0,1},{1,0},{2,3},{3,2},{4,5},{5,4},{6,7},{7,6},{8,9},{9,8},{10,11... | collective-permute-start | bytes 8650760 | tf_op jit(solution)/shard_map/ppermute | solution.py:620
  8.0 3.6 %pack.3.refs_6_ = f32[28,128,128]{2,1,0:T(8,128)} custom-call(s32[8]{0:T(128)S(1)} %stack.39.refs_0_, f32[512,2048]{1,0:T(8,128)} %bitcast.21, f32[4,512,128]{2,1,0:T(8,128)} %refs_1_.6, f32[512,2048]{1,0:T(8,128)} %bitcast.22, f32[44,128,128]{2,1,0:T(8,128)} %pack.2.refs_4_.refs_5_), custom_call_target="tpu_custom_call" | custom-call | flops 1 | bytes 1 | tf_op jit(solution)/shard_map/pack/pallas_call | solution.py:95
  11.6 1.9 %collective-permute-start.3 = (f32[28,128,128]{2,1,0:T(8,128)}, f32[28,128,128]{2,1,0:T(8,128)}, u32[]{:S(2)}, u32[]{:S(2)}) collective-permute-start(f32[28,128,128]{2,1,0:T(8,128)} %pack.3.refs_6_), channel_id=1, source_target_pairs={{1,2},{2,1},{5,6},{6,5},{9,10},{10,9},{13,14},{14,13},{17,18},{18,... | collective-permute-start | bytes 5505032 | tf_op jit(solution)/shard_map/ppermute | solution.py:620
  13.7 15.0 %dense.1 = (bf16[2048,2560]{1,0:T(8,128)(2,1)}, bf16[2048,2560]{1,0:T(8,128)(2,1)}, bf16[2,1024,2048]{2,1,0:T(8,128)(2,1)S(1)}) custom-call(s32[8]{0:T(128)S(1)} %stack.39.refs_0_, s32[1,16,8]{2,1,0:T(8,128)S(1)} %copy.27.refs_1_, s32[1,16,2]{2,1,0:T(8,128)S(1)} %copy.28.refs_2_, f32[16,8,128,128]{3,2,1,0:T(8,128)} %bitcast.24, ...), custom_call_target="tpu_custom_call" | custom-call | flops 1 | bytes 1 | tf_op jit(solution)/shard_map/dense/pallas_call | solution.py:95
  29.3 24.7 %begin.1 = (f32[1024,2048]{1,0:T(8,128)S(1)}, f32[512,2048]{1,0:T(8,128)S(1)}, f32[512,2048]{1,0:T(8,128)S(1)}, f32[512,512]{1,0:T(8,128)S(1)}, f32[8,128]{1,0:T(8,128)S(1)}) custom-call(s32[8]{0:T(128)S(1)} %stack.39.refs_0_, f32[1]{0:T(128)S(6)} %copy.44.refs_1_, f32[512,2048]{1,0:T(8,128)} %bitcast.23, ...), custom_call_target="tpu_custom_call" | custom-call | flops 1 | bytes 1 | tf_op jit(solution)/shard_map/begin/pallas_call | solution.py:95
  54.1 1.3 collective-permute-start.4
  55.4 16.2 %collective-permute-done.refs_2_.refs_0_.refs_1_ = f32[44,128,128]{2,1,0:T(8,128)S(1)} collective-permute-done((f32[44,128,128]{2,1,0:T(8,128)}, f32[44,128,128]{2,1,0:T(8,128)S(1)}, u32[]{:S(2)}, u32[]{:S(2)}) %collective-permute-start) | collective-permute-done | bytes 2883616 | tf_op jit(solution)/shard_map/ppermute | solution.py:620
  71.6 0.9 collective-permute-start.1
  72.5 20.3 %stage.3 = (f32[512,2048]{1,0:T(8,128)S(1)}, f32[512,2048]{1,0:T(8,128)S(1)}, f32[512,512]{1,0:T(8,128)S(1)}, f32[1024,2048]{1,0:T(8,128)S(1)}, f32[8,128]{1,0:T(8,128)S(1)}) custom-call(s32[8]{0:T(128)S(1)} %stack.39.refs_0_, f32[1]{0:T(128)S(6)} %copy.44.refs_1_, ...), custom_call_target="tpu_custom_call", output_to_operand_aliasing={{0}: (9, {}), {1}: (10, {}), {2}: (11, {}), {3}: (4, {})} | custom-call | flops 1 | bytes 1 | tf_op jit(solution)/shard_map/stage/pallas_call | solution.py:95
  92.8 1.5 collective-permute-start.2
  94.3 16.5 %collective-permute-done.4.refs_3_ = f32[28,128,128]{2,1,0:T(8,128)S(1)} collective-permute-done((f32[28,128,128]{2,1,0:T(8,128)}, f32[28,128,128]{2,1,0:T(8,128)S(1)}, u32[]{:S(2)}, u32[]{:S(2)}) %collective-permute-start.4) | collective-permute-done | bytes 1835040 | tf_op jit(solution)/shard_map/ppermute | solution.py:620
  110.9 17.3 %stage.4 = (f32[512,2048]{1,0:T(8,128)S(1)}, f32[512,2048]{1,0:T(8,128)S(1)}, f32[512,512]{1,0:T(8,128)S(1)}, f32[1024,2048]{1,0:T(8,128)S(1)}, f32[8,128]{1,0:T(8,128)S(1)}) custom-call(s32[8]{0:T(128)S(1)} %stack.39.refs_0_, f32[1]{0:T(128)S(6)} %copy.44.refs_1_, ...), custom_call_target="tpu_custom_call", output_to_operand_aliasing={{0}: (10, {}), {1}: (11, {}), {2}: (12, {}), {3}: (5, {})} | custom-call | flops 1 | bytes 1 | tf_op jit(solution)/shard_map/stage/pallas_call | solution.py:95
  128.1 1.7 collect.1.refs_13_.refs_2_
  129.9 12.9 %stage.5 = (f32[512,2048]{1,0:T(8,128)S(1)}, f32[512,2048]{1,0:T(8,128)S(1)}, f32[512,512]{1,0:T(8,128)S(1)}, f32[8,128]{1,0:T(8,128)S(1)}) custom-call(s32[8]{0:T(128)S(1)} %stack.39.refs_0_, f32[1]{0:T(128)S(6)} %copy.44.refs_1_, f32[12,128,128]{2,1,0:T(8,128)S(1)} %passed.3.refs_4_.refs_2_, ...), custom_call_target="tpu_custom_call", output_to_operand_aliasing={{0}: (10, {}), {1}: (11, {}), {2}: (12, {})} | custom-call | flops 1 | bytes 1 | tf_op jit(solution)/shard_map/stage/pallas_call | solution.py:95
  142.9 0.5 collective-permute-start.6
  143.4 2.7 %collective-permute-done.6.refs_3_ = f32[6,128,128]{2,1,0:T(8,128)S(1)} collective-permute-done((f32[6,128,128]{2,1,0:T(8,128)S(1)}, f32[6,128,128]{2,1,0:T(8,128)S(1)}, u32[]{:S(2)}, u32[]{:S(2)}) %collective-permute-start.6) | collective-permute-done | bytes 393248 | tf_op jit(solution)/shard_map/ppermute | solution.py:647
  146.1 5.1 %drift.1 = (f32[2048,128]{1,0:T(8,128)S(1)}, f32[512,128]{1,0:T(8,128)S(1)}) custom-call(s32[8]{0:T(128)S(1)} %stack.39.refs_0_, f32[4,512,128]{2,1,0:T(8,128)} %refs_1_.6, f32[6,128,128]{2,1,0:T(8,128)S(1)} %collect.1.refs_13_.refs_2_, f32[6,128,128]{2,1,0:T(8,128)S(1)} %collective-permute-done.6.refs_3_, ...), custom_call_target="tpu_custom_call" | custom-call | flops 1 | bytes 1 | tf_op jit(solution)/shard_map/drift/pallas_call | solution.py:95
  151.2 0.2 collective-permute-start.7
  151.4 2.0 %copy-done = f32[512,2048]{1,0:T(8,128)} copy-done((f32[512,2048]{1,0:T(8,128)}, f32[512,2048]{1,0:T(8,128)S(1)}, u32[]{:S(2)}) %copy-start) | copy-done | bytes 4194328
  153.4 0.4 collective-permute-start.8
  153.8 19.8 %inverse.1.refs_1_ = f32[512,512]{1,0:T(8,128)S(1)} custom-call(f32[512,512]{1,0:T(8,128)S(1)} %get-tuple-element.50.refs_0_, f32[512,512]{1,0:T(8,128)S(1)} %collective-permute-done.5.refs_1_.refs_0_, f32[1,512]{1,0:T(1,128)S(1)} %bitcast.17), custom_call_target="tpu_custom_call" | custom-call | flops 1 | bytes 1 | tf_op jit(solution)/shard_map/inverse/pallas_call | solution.py:95
  173.6 2.2 %copy-done.1 = f32[512,2048]{1,0:T(8,128)S(1)} copy-done((f32[512,2048]{1,0:T(8,128)S(1)}, f32[512,2048]{1,0:T(8,128)}, u32[]{:S(2)}) %copy-start.1) | copy-done | bytes 4194328
  175.8 13.2 %final.1 = (f32[512,512]{1,0:T(8,128)}, f32[512,2048]{1,0:T(8,128)}, f32[512,128]{1,0:T(8,128)}) custom-call(s32[8]{0:T(128)S(1)} %stack.39.refs_0_, f32[512,512]{1,0:T(8,128)S(1)} %inverse.1.refs_1_, f32[512,2048]{1,0:T(8,128)S(1)} %get-tuple-element.55.refs_2_, f32[512,2048]{1,0:T(8,128)S(1)} %copy-done.1, ...), custom_call_target="tpu_custom_call" | custom-call | flops 1 | bytes 1 | tf_op jit(solution)/shard_map/final/pallas_call | solution.py:95
  (24 shorter events, 0.4 us)
Async XLA Ops:
  5.0 8.5 %copy-start.4 = (s32[1,16,8]{1,2,0:T(8,128)S(1)}, s32[1,16,8]{1,2,0:T(8,128)}, u32[]{:S(2)}) copy-start(s32[1,16,8]{1,2,0:T(8,128)} %param.11) | copy-start | bytes 1540
  5.0 8.6 %copy-start.5 = (s32[1,16,2]{1,2,0:T(2,128)S(1)}, s32[1,16,2]{1,2,0:T(2,128)}, u32[]{:S(2)}) copy-start(s32[1,16,2]{1,2,0:T(2,128)} %param.13) | copy-start | bytes 388
  5.0 66.5 %collective-permute-start = (f32[44,128,128]{2,1,0:T(8,128)}, f32[44,128,128]{2,1,0:T(8,128)S(1)}, u32[]{:S(2)}, u32[]{:S(2)}) collective-permute-start(f32[44,128,128]{2,1,0:T(8,128)} %pack.2.refs_4_.refs_5_), channel_id=1, source_target_pairs={{0,1},{1,0},{2,3},{3,2},{4,5},{5,4},{6,7},{7,6},{8,9},{9,8},{10,11... | collective-permute-start | bytes 8650760 | tf_op jit(solution)/shard_map/ppermute | solution.py:620
  11.6 42.4 %collective-permute-start.3 = (f32[28,128,128]{2,1,0:T(8,128)}, f32[28,128,128]{2,1,0:T(8,128)}, u32[]{:S(2)}, u32[]{:S(2)}) collective-permute-start(f32[28,128,128]{2,1,0:T(8,128)} %pack.3.refs_6_), channel_id=1, source_target_pairs={{1,2},{2,1},{5,6},{6,5},{9,10},{10,9},{13,14},{14,13},{17,18},{18,... | collective-permute-start | bytes 5505032 | tf_op jit(solution)/shard_map/ppermute | solution.py:620
  54.1 56.8 %collective-permute-start.4 = (f32[28,128,128]{2,1,0:T(8,128)}, f32[28,128,128]{2,1,0:T(8,128)S(1)}, u32[]{:S(2)}, u32[]{:S(2)}) collective-permute-start(f32[28,128,128]{2,1,0:T(8,128)} %passed.4.refs_2_), channel_id=1, source_target_pairs={{1,0},{2,3},{5,4},{6,7},{9,8},{10,11},{13,12},{14,15},{17,16},{18,... | collective-permute-start | bytes 5505032 | tf_op jit(solution)/shard_map/ppermute | solution.py:620
  71.6 21.2 %collective-permute-start.1 = (f32[12,128,128]{2,1,0:T(8,128)S(1)}, f32[12,128,128]{2,1,0:T(8,128)S(1)}, u32[]{:S(2)}, u32[]{:S(2)}) collective-permute-start(f32[12,128,128]{2,1,0:T(8,128)S(1)} %front.1), channel_id=1, source_target_pairs={{1,2},{2,1},{5,6},{6,5},{9,10},{10,9},{13,14},{14,13},{17,18},{18,... | collective-permute-start | bytes 2359304 | tf_op jit(solution)/shard_map/ppermute | solution.py:620
  92.8 35.3 %collective-permute-start.2 = (f32[12,128,128]{2,1,0:T(8,128)S(1)}, f32[12,128,128]{2,1,0:T(8,128)S(1)}, u32[]{:S(2)}, u32[]{:S(2)}) collective-permute-start(f32[12,128,128]{2,1,0:T(8,128)S(1)} %passed.3.refs_4_.refs_2_), channel_id=1, source_target_pairs={{1,0},{2,3},{5,4},{6,7},{9,8},{10,11},{13,12},{14,15},{17,16},{18,... | collective-permute-start | bytes 2359304 | tf_op jit(solution)/shard_map/ppermute | solution.py:620
  142.8 8.4 %collective-permute-start.5 = (f32[512,512]{1,0:T(8,128)S(1)}, f32[512,512]{1,0:T(8,128)S(1)}, u32[]{:S(2)}, u32[]{:S(2)}) collective-permute-start(f32[512,512]{1,0:T(8,128)S(1)} %get-tuple-element.50.refs_0_), channel_id=1, source_target_pairs={{0,4},{4,0},{8,12},{12,8},{16,20},{20,16},{24,28},{28,24},{1,5},{5... | collective-permute-start | bytes 3145736 | tf_op jit(solution)/shard_map/ppermute | solution.py:647
  142.9 3.2 %collective-permute-start.6 = (f32[6,128,128]{2,1,0:T(8,128)S(1)}, f32[6,128,128]{2,1,0:T(8,128)S(1)}, u32[]{:S(2)}, u32[]{:S(2)}) collective-permute-start(f32[6,128,128]{2,1,0:T(8,128)S(1)} %collect.1.refs_13_.refs_2_), channel_id=1, source_target_pairs={{0,4},{4,0},{8,12},{12,8},{16,20},{20,16},{24,28},{28,24},{1,5},{5... | collective-permute-start | bytes 1179656 | tf_op jit(solution)/shard_map/ppermute | solution.py:647
  151.2 2.6 %copy-start.3 = (f32[512]{0:T(512)S(1)}, f32[512]{0:T(512)}, u32[]{:S(2)}) copy-start(f32[512]{0:T(512)} %param.16) | copy-start | bytes 6148
  151.2 22.4 %copy-start.2 = (f32[512]{0:T(512)S(1)}, f32[512]{0:T(512)}, u32[]{:S(2)}) copy-start(f32[512]{0:T(512)} %param.15) | copy-start | bytes 6148
  151.2 22.4 %collective-permute-start.7 = (f32[512,2048]{1,0:T(8,128)S(1)}, f32[512,2048]{1,0:T(8,128)S(1)}, u32[]{:S(2)}, u32[]{:S(2)}) collective-permute-start(f32[512,2048]{1,0:T(8,128)S(1)} %get-tuple-element.56.refs_3_), channel_id=1, source_target_pairs={{0,4},{4,0},{8,12},{12,8},{16,20},{20,16},{24,28},{28,24},{1,5},{5... | collective-permute-start | bytes 12582920 | tf_op jit(solution)/shard_map/ppermute | solution.py:647
  151.4 2.0 %copy-start = (f32[512,2048]{1,0:T(8,128)}, f32[512,2048]{1,0:T(8,128)S(1)}, u32[]{:S(2)}) copy-start(f32[512,2048]{1,0:T(8,128)S(1)} %get-tuple-element.56.refs_3_) | copy-start | bytes 12582916
  153.4 20.2 %collective-permute-start.8 = (f32[512,2048]{1,0:T(8,128)S(1)}, f32[512,2048]{1,0:T(8,128)S(1)}, u32[]{:S(2)}, u32[]{:S(2)}) collective-permute-start(f32[512,2048]{1,0:T(8,128)S(1)} %get-tuple-element.55.refs_2_), channel_id=1, source_target_pairs={{0,4},{4,0},{8,12},{12,8},{16,20},{20,16},{24,28},{28,24},{1,5},{5... | collective-permute-start | bytes 12582920 | tf_op jit(solution)/shard_map/ppermute | solution.py:647
  173.6 2.2 %copy-start.1 = (f32[512,2048]{1,0:T(8,128)S(1)}, f32[512,2048]{1,0:T(8,128)}, u32[]{:S(2)}) copy-start(f32[512,2048]{1,0:T(8,128)} %copy-done) | copy-start | bytes 12582916

commit v7 on v6

--- a/solution.py
+++ b/solution.py
@@ -32,7 +32,7 @@
 
 
 TILE = (256, 512)
-OWN, PARTNER, SECOND, THIRD, PARENT, CORE, NEAR, EDGE = range(8)
+OWN, PARTNER, SECOND, THIRD, PARENT, CORE, NEAR, EDGE = 0, 4, 5, 6, 7, 8, 9, 10
 VMEM = pltpu.VMEM
 STAYS = pl.BlockSpec(memory_space=VMEM)
 
@@ -235,23 +235,19 @@
     return [block[i * blk : (i + 1) * blk, j * blk : (j + 1) * blk] for i in range(n) for j in range(n)]
 
 
-def pack_kernel(blk, where, own, x_ref, *refs):
+def pack_kernel(blk, where, own, *refs):
     *blocks, out = refs
     diag = [own[i * blk : (i + 1) * blk, j * blk : (j + 1) * blk] for i, j in lower(own.shape[0] // blk)]
-    x = [x_ref[0, :blk], x_ref[0, blk:]]
-    for t, tile in enumerate(diag + x + [tile for block in blocks for tile in tiled(block, blk)]):
+    for t, tile in enumerate(diag + [tile for block in blocks for tile in tiled(block, blk)]):
         out[t] = tile
 
 
-def pack(where, blocks, cost_rows, parent_state, blk, after):
+def pack(where, blocks, cost_rows, blk, after):
     rows = cost_rows.shape[0]
-    samples = parent_state.shape[2]
-    picks = [OWN, *blocks]
-    size = len(lower(rows // blk)) + 2 + (len(picks) - 1) * (rows // blk) ** 2
-    specs = [pl.BlockSpec((rows, rows), functools.partial(lambda t, i, where: (0, where[t]), t)) for t in picks]
-    specs.insert(1, pl.BlockSpec((1, rows // 2, samples), lambda i, where: (where[PARENT], where[CORE], 0)))
-    args = [outside(cost_rows)] * len(picks)
-    args.insert(1, outside(parent_state))
+    size = len(lower(rows // blk)) + len(blocks) * (rows // blk) ** 2
+    specs = [
+        pl.BlockSpec((rows, rows), functools.partial(lambda t, i, where: (0, where[t]), t)) for t in (OWN, *blocks)
+    ]
     return call(
         functools.partial(pack_kernel, blk),
         (1,),
@@ -262,7 +258,26 @@
         "pack",
         after=after,
         limit=16,
-    )(where, *args)[0]
+    )(where, *[outside(cost_rows)] * len(specs))[0]
+
+
+def half_state(where, parent_state, after):
+    _, rows, samples = parent_state.shape
+
+    def kernel(where, x, out):
+        out[...] = x[0]
+
+    return call(
+        kernel,
+        (1,),
+        1,
+        [pl.BlockSpec((1, rows // 2, samples), lambda i, where: (where[PARENT], where[CORE], 0))],
+        [whole(rows // 2, samples)],
+        [((rows // 2, samples), F32)],
+        "half_state",
+        after=after,
+        limit=4,
+    )(where, outside(parent_state))[0]
 
 
 def front(message, size):
@@ -278,48 +293,38 @@
     blk = tiles.shape[1]
     lead = len(lower(n))
     for t, (i, j) in enumerate(lower(n) if step == 0 else [(i, j) for i in range(n) for j in range(n)]):
-        tile = tiles[t if step == 0 else lead + 2 + (step - 1) * n * n + t]
+        tile = tiles[t if step == 0 else lead + (step - 1) * n * n + t]
         places = [(i, j, tile)] + ([(j, i, tile.T)] if step == 0 and i != j else [])
         for r, c, value in places:
             at = slice(r * blk, (r + 1) * blk), slice(c * blk, (c + 1) * blk)
             xh[at], xl[at] = split(value)
 
 
-def collect_kernel(where, pair, mid, end, mid_last, end_last, out):
-    out[:2] = pair[...]
-
-    @pl.when(where[EDGE] == 1)
-    def _():
-        out[2:4] = end[...]
-        out[4:6] = end_last[...]
-
-    @pl.when(where[EDGE] == 0)
-    def _():
-        out[2:4] = mid[...]
-        out[4:6] = mid_last[...]
-
-
-def collect(where, messages, after):
-    blk = messages[0].shape[1]
-    lead = messages[3].shape[0] // 2 - 1
-    return call(
-        collect_kernel,
+def collect(halves, after):
+    count = len(halves)
+    rows, samples = halves[0].shape
+
+    def kernel(*refs):
+        for t in range(count):
+            refs[count][t] = refs[t][...]
+
+    return call(
+        kernel,
         (1,),
-        1,
-        [pl.BlockSpec((2, blk, blk), lambda i, where: (lead, 0, 0))] * 5,
-        [whole(6, blk, blk)],
-        [((6, blk, blk), F32)],
+        0,
+        [whole(rows, samples)] * count,
+        [whole(count, rows, samples)],
+        [((count, rows, samples), F32)],
         "collect",
         after=[after],
         limit=4,
-    )(where, *messages)[0]
+    )(*halves)[0]
 
 
 def drift_kernel(where, own, mine, other, fh, fl, x_ref, out):
     g = pl.program_id(0)
     core = where[CORE]
-    blk = mine.shape[1]
-    rows = own.shape[1]
+    half = mine.shape[1]
 
     @pl.when(g == 0)
     def _():
@@ -329,9 +334,8 @@
 
         @pl.when(g == d + 1)
         def _():
-            for t in range(2):
-                x_ref[pl.ds(pl.multiple_of(core * (rows // 2) + t * blk, blk), blk)] = mine[2 * d + t]
-                x_ref[pl.ds(pl.multiple_of((1 - core) * (rows // 2) + t * blk, blk), blk)] = other[2 * d + t]
+            x_ref[pl.ds(pl.multiple_of(core * half, half), half)] = mine[d]
+            x_ref[pl.ds(pl.multiple_of((1 - core) * half, half), half)] = other[d]
 
     part = dot3((fh[...], fl[...]), split(x_ref[...]))
 
@@ -346,14 +350,13 @@
 
 def drift(where, parent_state, mine, other, fh, fl, after):
     _, rows, samples = parent_state.shape
-    count, blk, _ = mine.shape
     factor = pl.BlockSpec((rows, rows), lambda g, where: (where[OWN], where[OWN + g]))
     return call(
         drift_kernel,
         (4,),
         1,
         [pl.BlockSpec((1, rows, samples), lambda g, where: (where[PARENT], 0, 0))]
-        + [whole(count, blk, blk)] * 2
+        + [whole(*mine.shape)] * 2
         + [factor, factor],
         [pl.BlockSpec((rows, samples), lambda g, where: (where[OWN + g], 0)), whole(rows, samples)],
         [((4 * rows, samples), F32), ((rows, samples), F32)],
@@ -611,7 +614,7 @@
     return acc[:, :width], jnp.swapaxes(cross.reshape(width, -1), 0, 1)
 
 
-def by_blocks(where, weight, cost_rows, parent_state, dense_parts, messages):
+def by_blocks(where, weight, cost_rows, parent_state, dense_parts, messages, half):
     fh, fl, u = dense_parts
     pair, mid = messages
     lead = 2 * mid.shape[0] - pair.shape[0]
@@ -627,19 +630,20 @@
 
     pair = moved(pair, (0, 1), (1, 0), (2, 3), (3, 2))
     mid = across(mid)
+    halves = [moved(half, *[(i, (i + d) % 4) for i in range(4)]) for d in range(1, 4)]
     n, *sums, token = begin(where, weight, cost_rows, u, fh, fl)
-    (mid,) = passed([mid], token)
+    (mid,) = passed([mid], token, *halves)
     end = to_end(mid)
     mid_last = across(front(pair, lead))
     *sums, n, token = stage(where, weight, [pair], PARTNER, 3, u, n, fh, fl, sums)
     (mid_last,) = passed([mid_last], token)
     end_last = to_end(mid_last)
-    *sums, n, token = stage(where, weight, [mid, end], SECOND, 2, u, n, fh, fl, sums)
-    halves = collect(where, [pair, mid, end, mid_last, end_last], token)
-    s, g, h, token = stage(where, weight, [mid_last, end_last], THIRD, 1, u, n, fh, fl, sums, [halves])
+    halves = collect(halves, token)
     x, y = drift(where, parent_state, halves, swapped(halves), fh, fl, token)
+    *sums, n, token = stage(where, weight, [mid, end], SECOND, 2, u, n, fh, fl, sums, [y])
+    s, g, h, token = stage(where, weight, [mid_last, end_last], THIRD, 1, u, n, fh, fl, sums)
     other = swapped(h)
-    return h, other, passed([s, g], other, y, keep=True), x, y
+    return h, other, passed([s, g], other, keep=True), x, y
 
 
 def swapped(x):
@@ -670,14 +674,16 @@
     left = z < 2
     near = jnp.where(left, 0, 3)
     edge = ((z == 0) | (z == 3)).astype(jnp.int32)
-    where = jnp.stack([z, z ^ 1, jnp.where(left, 2, 1), 3 - near, leaf // 2, leaf % 2, near, edge])
+    before = [(z - d) % 4 for d in range(4)]
+    where = jnp.stack([*before, z ^ 1, jnp.where(left, 2, 1), 3 - near, leaf // 2, leaf % 2, near, edge])
     sent = []
     if line:
-        sent.append(pack(where, [SECOND, THIRD], cost_rows, parent_state, blk, []))
-        sent.append(pack(where, [NEAR], cost_rows, parent_state, blk, sent))
+        sent.append(pack(where, [SECOND, THIRD], cost_rows, blk, []))
+        sent.append(pack(where, [NEAR], cost_rows, blk, sent))
+        sent.append(half_state(where, parent_state, sent[1:]))
     fh, fl, u = parts_of = dense(where, rows, a_blocks[0], a_cols, b_blocks[0], b_cols, orders, sent)
     if line:
-        h, other_h, own, x, y = by_blocks(where, branch_prob, cost_rows, parent_state, parts_of, sent)
+        h, other_h, own, x, y = by_blocks(where, branch_prob, cost_rows, parent_state, parts_of, sent[:2], sent[2])
     else:
         w = dot3(parted(cost_rows), (fh[:, width:], fl[:, width:]))
         b_rows = [lax.dynamic_slice(f, (0, z * rows), (orders, rows)) for f in u]

time: 190 us -> 191 us (level)
  starting transfers between devices: 9.75 us -> 13.9 us
  waiting for transfers between devices: 35.4 us -> 32 us
    ppermute x5 -> x8, waiting for transfers between devices: 32.7 us -> 27.7 us  [moved(): return lax.ppermute(x, 'row', pairs)]
    ppermute x5 -> x8, starting transfers between devices: 8.61 us -> 13.3 us  [moved(): return lax.ppermute(x, 'row', pairs)]
    pallas_call x15 -> x16, Pallas kernels: 138 us -> 139 us  [run(): built(*args[:prefetch], *placed, *after, *[resident(x) if keep else x for...]
  transfers between devices with their start and end apart: 9 -> 12, of which waited for: 3 -> 6; matrix products, arithmetic and copies ran while one was open for 0% -> 0% of each run, Pallas kernels for 56% -> 58%
where the time goes in v7:
time: 191 us
  Pallas kernels  139 us (73%)
  waiting for transfers between devices  32 us (17%)
  starting transfers between devices  13.9 us (7%)
  local copies, waits for them, and re-layouts  4.46 us (2%)
    pallas_call x16, Pallas kernels, run(): built(*args[:prefetch], *placed, *after, *[resident(x) if keep else x for...  139 us
    ppermute x8, waiting for transfers between devices, moved(): return lax.ppermute(x, 'row', pairs)  27.7 us
    ppermute x8, starting transfers between devices, moved(): return lax.ppermute(x, 'row', pairs)  13.3 us
    ppermute x4, waiting for transfers between devices, swapped(): return lax.ppermute(x, 'leaf', [(i, i ^ 1) for i in range(n)])  4.37 us
    unnamed x14, local copies, waits for them, and re-layouts  4.37 us
  transfers between devices with their start and end apart: 12, of which 6 were waited for; matrix products, arithmetic and copies ran while one was open for 0% of the time, Pallas kernels for 58%

profile of v7, /device:TPU:0, one launch (start us, length us, event | category | flops | bytes accessed | tf_op | source)
XLA Modules:
  0.0 190.6 jit_solution(5351063378275326465)
XLA Ops:
  0.8 2.6 %pack.2.refs_3_.refs_5_ = f32[42,128,128]{2,1,0:T(8,128)S(1)} custom-call(s32[11]{0:T(128)S(1)} %stack.51.refs_0_, f32[512,2048]{1,0:T(8,128)} %bitcast.21, f32[512,2048]{1,0:T(8,128)} %bitcast.22, f32[512,2048]{1,0:T(8,128)} %bitcast.23), custom_call_target="tpu_custom_call" | custom-call | flops 1 | bytes 1 | tf_op jit(solution)/shard_map/pack/pallas_call | solution.py:95
  3.4 3.1 %collective-permute-start = (f32[42,128,128]{2,1,0:T(8,128)S(1)}, f32[42,128,128]{2,1,0:T(8,128)}, u32[]{:S(2)}, u32[]{:S(2)}) collective-permute-start(f32[42,128,128]{2,1,0:T(8,128)S(1)} %pack.2.refs_3_.refs_5_), channel_id=1, source_target_pairs={{0,1},{1,0},{2,3},{3,2},{4,5},{5,4},{6,7},{7,6},{8,9},{9,8},{10,11... | collective-permute-start | bytes 8257544 | tf_op jit(solution)/shard_map/ppermute | solution.py:623
  6.5 3.4 %pack.3.refs_2_.refs_6_ = f32[26,128,128]{2,1,0:T(8,128)} custom-call(s32[11]{0:T(128)S(1)} %stack.51.refs_0_, f32[512,2048]{1,0:T(8,128)} %bitcast.24, f32[512,2048]{1,0:T(8,128)} %bitcast.25, f32[42,128,128]{2,1,0:T(8,128)S(1)} %pack.2.refs_3_.refs_5_), custom_call_target="tpu_custom_call" | custom-call | flops 1 | bytes 1 | tf_op jit(solution)/shard_map/pack/pallas_call | solution.py:95
  10.0 2.0 %collective-permute-start.6 = (f32[26,128,128]{2,1,0:T(8,128)}, f32[26,128,128]{2,1,0:T(8,128)}, u32[]{:S(2)}, u32[]{:S(2)}) collective-permute-start(f32[26,128,128]{2,1,0:T(8,128)} %pack.3.refs_2_.refs_6_), channel_id=1, source_target_pairs={{1,2},{2,1},{5,6},{6,5},{9,10},{10,9},{13,14},{14,13},{17,18},{18,... | collective-permute-start | bytes 5111816 | tf_op jit(solution)/shard_map/ppermute | solution.py:623
  11.9 1.5 half_state.1.refs_7_
  13.4 2.5 %collective-permute-start.5 = (f32[256,128]{1,0:T(8,128)S(1)}, f32[256,128]{1,0:T(8,128)S(1)}, u32[]{:S(2)}, u32[]{:S(2)}) collective-permute-start(f32[256,128]{1,0:T(8,128)S(1)} %half_state.1.refs_7_), channel_id=1, source_target_pairs={{0,3},{1,0},{2,1},{3,2},{4,7},{5,4},{6,5},{7,6},{8,11},{9,8},{10,9... | collective-permute-start | bytes 393224 | tf_op jit(solution)/shard_map/ppermute | solution.py:623
  15.8 2.1 %collective-permute-start.4 = (f32[256,128]{1,0:T(8,128)S(1)}, f32[256,128]{1,0:T(8,128)S(1)}, u32[]{:S(2)}, u32[]{:S(2)}) collective-permute-start(f32[256,128]{1,0:T(8,128)S(1)} %half_state.1.refs_7_), channel_id=1, source_target_pairs={{0,2},{1,3},{2,0},{3,1},{4,6},{5,7},{6,4},{7,5},{8,10},{9,11},{10,... | collective-permute-start | bytes 393224 | tf_op jit(solution)/shard_map/ppermute | solution.py:623
  18.1 15.0 %dense.1 = (bf16[2048,2560]{1,0:T(8,128)(2,1)}, bf16[2048,2560]{1,0:T(8,128)(2,1)}, bf16[2,1024,2048]{2,1,0:T(8,128)(2,1)S(1)}) custom-call(s32[11]{0:T(128)S(1)} %stack.51.refs_0_, s32[1,16,8]{2,1,0:T(8,128)S(1)} %copy.27.refs_1_, s32[1,16,2]{2,1,0:T(8,128)S(1)} %copy.28.refs_2_, f32[16,8,128,128]{3,2,1,0:T(8,128)} %bitcast.27, ...), custom_call_target="tpu_custom_call" | custom-call | flops 1 | bytes 1 | tf_op jit(solution)/shard_map/dense/pallas_call | solution.py:95
  33.7 24.7 %begin.1 = (f32[1024,2048]{1,0:T(8,128)S(1)}, f32[512,2048]{1,0:T(8,128)S(1)}, f32[512,2048]{1,0:T(8,128)S(1)}, f32[512,512]{1,0:T(8,128)S(1)}, f32[8,128]{1,0:T(8,128)S(1)}) custom-call(s32[11]{0:T(128)S(1)} %stack.51.refs_0_, f32[1]{0:T(128)S(6)} %copy.44.refs_1_, f32[512,2048]{1,0:T(8,128)} %bitcast.26, ...), custom_call_target="tpu_custom_call" | custom-call | flops 1 | bytes 1 | tf_op jit(solution)/shard_map/begin/pallas_call | solution.py:95
  58.4 13.4 %collective-permute-done.5.refs_3_.refs_2_ = f32[256,128]{1,0:T(8,128)S(1)} collective-permute-done((f32[256,128]{1,0:T(8,128)S(1)}, f32[256,128]{1,0:T(8,128)S(1)}, u32[]{:S(2)}, u32[]{:S(2)}) %collective-permute-start.5) | collective-permute-done | bytes 131104 | tf_op jit(solution)/shard_map/ppermute | solution.py:623
  72.2 4.6 %collective-permute-done.3.refs_1_.refs_0_ = f32[256,128]{1,0:T(8,128)S(1)} collective-permute-done((f32[256,128]{1,0:T(8,128)S(1)}, f32[256,128]{1,0:T(8,128)S(1)}, u32[]{:S(2)}, u32[]{:S(2)}) %collective-permute-start.3) | collective-permute-done | bytes 131104 | tf_op jit(solution)/shard_map/ppermute | solution.py:623
  76.8 1.3 collective-permute-start.7
  80.1 21.1 %stage.3 = (f32[512,2048]{1,0:T(8,128)S(1)}, f32[512,2048]{1,0:T(8,128)S(1)}, f32[512,512]{1,0:T(8,128)S(1)}, f32[1024,2048]{1,0:T(8,128)S(1)}, f32[8,128]{1,0:T(8,128)S(1)}) custom-call(s32[11]{0:T(128)S(1)} %stack.51.refs_0_, f32[1]{0:T(128)S(6)} %copy.44.refs_1_, ...), custom_call_target="tpu_custom_call", output_to_operand_aliasing={{0}: (9, {}), {1}: (10, {}), {2}: (11, {}), {3}: (4, {})} | custom-call | flops 1 | bytes 1 | tf_op jit(solution)/shard_map/stage/pallas_call | solution.py:95
  101.3 1.5 collective-permute-start.2
  102.9 1.7 collective-permute-done.8.refs_3_
  104.6 5.1 %drift.1 = (f32[2048,128]{1,0:T(8,128)S(1)}, f32[512,128]{1,0:T(8,128)S(1)}) custom-call(s32[11]{0:T(128)S(1)} %stack.51.refs_0_, f32[4,512,128]{2,1,0:T(8,128)} %refs_1_.8, f32[3,256,128]{2,1,0:T(8,128)S(1)} %collect.1.refs_2_, f32[3,256,128]{2,1,0:T(8,128)S(1)} %collective-permute-done.8.refs_3_, ...), custom_call_target="tpu_custom_call" | custom-call | flops 1 | bytes 1 | tf_op jit(solution)/shard_map/drift/pallas_call | solution.py:95
  109.7 9.3 %collective-permute-done.7.refs_3_ = f32[26,128,128]{2,1,0:T(8,128)S(1)} collective-permute-done((f32[26,128,128]{2,1,0:T(8,128)}, f32[26,128,128]{2,1,0:T(8,128)S(1)}, u32[]{:S(2)}, u32[]{:S(2)}) %collective-permute-start.7) | collective-permute-done | bytes 1703968 | tf_op jit(solution)/shard_map/ppermute | solution.py:623
  119.0 17.8 %stage.4 = (f32[512,2048]{1,0:T(8,128)S(1)}, f32[512,2048]{1,0:T(8,128)S(1)}, f32[512,512]{1,0:T(8,128)S(1)}, f32[1024,2048]{1,0:T(8,128)S(1)}, f32[8,128]{1,0:T(8,128)}) custom-call(s32[11]{0:T(128)S(1)} %stack.51.refs_0_, f32[1]{0:T(128)S(6)} %copy.44.refs_1_, ...), custom_call_target="tpu_custom_call", output_to_operand_aliasing={{0}: (10, {}), {1}: (11, {}), {2}: (12, {}), {3}: (5, {})} | custom-call | flops 1 | bytes 1 | tf_op jit(solution)/shard_map/stage/pallas_call | solution.py:95
  136.8 13.4 %stage.5 = (f32[512,2048]{1,0:T(8,128)S(1)}, f32[512,2048]{1,0:T(8,128)S(1)}, f32[512,512]{1,0:T(8,128)S(1)}, f32[8,128]{1,0:T(8,128)}) custom-call(s32[11]{0:T(128)S(1)} %stack.51.refs_0_, f32[1]{0:T(128)S(6)} %copy.44.refs_1_, f32[10,128,128]{2,1,0:T(8,128)S(1)} %passed.3.refs_2_, ...), custom_call_target="tpu_custom_call", output_to_operand_aliasing={{0}: (10, {}), {1}: (11, {}), {2}: (12, {})} | custom-call | flops 1 | bytes 1 | tf_op jit(solution)/shard_map/stage/pallas_call | solution.py:95
  150.3 2.7 %collective-permute-done.9.refs_1_.refs_0_ = f32[512,512]{1,0:T(8,128)S(1)} collective-permute-done((f32[512,512]{1,0:T(8,128)S(1)}, f32[512,512]{1,0:T(8,128)S(1)}, u32[]{:S(2)}, u32[]{:S(2)}) %collective-permute-start.9) | collective-permute-done | bytes 1048608 | tf_op jit(solution)/shard_map/ppermute | solution.py:651
  153.4 2.0 %copy-done = f32[512,2048]{1,0:T(8,128)} copy-done((f32[512,2048]{1,0:T(8,128)}, f32[512,2048]{1,0:T(8,128)S(1)}, u32[]{:S(2)}) %copy-start) | copy-done | bytes 4194328
  155.5 20.0 %inverse.1.refs_1_ = f32[512,512]{1,0:T(8,128)S(1)} custom-call(f32[512,512]{1,0:T(8,128)S(1)} %get-tuple-element.48.refs_0_, f32[512,512]{1,0:T(8,128)S(1)} %collective-permute-done.9.refs_1_.refs_0_, f32[1,512]{1,0:T(1,128)S(1)} %bitcast.20), custom_call_target="tpu_custom_call" | custom-call | flops 1 | bytes 1 | tf_op jit(solution)/shard_map/inverse/pallas_call | solution.py:95
  175.5 2.2 %copy-done.1 = f32[512,2048]{1,0:T(8,128)S(1)} copy-done((f32[512,2048]{1,0:T(8,128)S(1)}, f32[512,2048]{1,0:T(8,128)}, u32[]{:S(2)}) %copy-start.1) | copy-done | bytes 4194328
  177.7 12.9 %final.1 = (f32[512,512]{1,0:T(8,128)}, f32[512,2048]{1,0:T(8,128)}, f32[512,128]{1,0:T(8,128)}) custom-call(s32[11]{0:T(128)S(1)} %stack.51.refs_0_, f32[512,512]{1,0:T(8,128)S(1)} %inverse.1.refs_1_, f32[512,2048]{1,0:T(8,128)S(1)} %get-tuple-element.51.refs_2_, f32[512,2048]{1,0:T(8,128)S(1)} %copy-done.1, ...), custom_call_target="tpu_custom_call" | custom-call | flops 1 | bytes 1 | tf_op jit(solution)/shard_map/final/pallas_call | solution.py:95
  (31 shorter events, 3.3 us)
Async XLA Ops:
  3.4 14.5 %copy-start.4 = (s32[1,16,8]{1,2,0:T(8,128)S(1)}, s32[1,16,8]{1,2,0:T(8,128)}, u32[]{:S(2)}) copy-start(s32[1,16,8]{1,2,0:T(8,128)} %param.11) | copy-start | bytes 1540
  3.4 14.6 %copy-start.5 = (s32[1,16,2]{1,2,0:T(2,128)S(1)}, s32[1,16,2]{1,2,0:T(2,128)}, u32[]{:S(2)}) copy-start(s32[1,16,2]{1,2,0:T(2,128)} %param.13) | copy-start | bytes 388
  3.4 74.7 %collective-permute-start = (f32[42,128,128]{2,1,0:T(8,128)S(1)}, f32[42,128,128]{2,1,0:T(8,128)}, u32[]{:S(2)}, u32[]{:S(2)}) collective-permute-start(f32[42,128,128]{2,1,0:T(8,128)S(1)} %pack.2.refs_3_.refs_5_), channel_id=1, source_target_pairs={{0,1},{1,0},{2,3},{3,2},{4,5},{5,4},{6,7},{7,6},{8,9},{9,8},{10,11... | collective-permute-start | bytes 8257544 | tf_op jit(solution)/shard_map/ppermute | solution.py:623
  10.0 66.8 %collective-permute-start.6 = (f32[26,128,128]{2,1,0:T(8,128)}, f32[26,128,128]{2,1,0:T(8,128)}, u32[]{:S(2)}, u32[]{:S(2)}) collective-permute-start(f32[26,128,128]{2,1,0:T(8,128)} %pack.3.refs_2_.refs_6_), channel_id=1, source_target_pairs={{1,2},{2,1},{5,6},{6,5},{9,10},{10,9},{13,14},{14,13},{17,18},{18,... | collective-permute-start | bytes 5111816 | tf_op jit(solution)/shard_map/ppermute | solution.py:623
  13.4 58.4 %collective-permute-start.5 = (f32[256,128]{1,0:T(8,128)S(1)}, f32[256,128]{1,0:T(8,128)S(1)}, u32[]{:S(2)}, u32[]{:S(2)}) collective-permute-start(f32[256,128]{1,0:T(8,128)S(1)} %half_state.1.refs_7_), channel_id=1, source_target_pairs={{0,3},{1,0},{2,1},{3,2},{4,7},{5,4},{6,5},{7,6},{8,11},{9,8},{10,9... | collective-permute-start | bytes 393224 | tf_op jit(solution)/shard_map/ppermute | solution.py:623
  15.8 56.4 %collective-permute-start.4 = (f32[256,128]{1,0:T(8,128)S(1)}, f32[256,128]{1,0:T(8,128)S(1)}, u32[]{:S(2)}, u32[]{:S(2)}) collective-permute-start(f32[256,128]{1,0:T(8,128)S(1)} %half_state.1.refs_7_), channel_id=1, source_target_pairs={{0,2},{1,3},{2,0},{3,1},{4,6},{5,7},{6,4},{7,5},{8,10},{9,11},{10,... | collective-permute-start | bytes 393224 | tf_op jit(solution)/shard_map/ppermute | solution.py:623
  17.9 58.9 %collective-permute-start.3 = (f32[256,128]{1,0:T(8,128)S(1)}, f32[256,128]{1,0:T(8,128)S(1)}, u32[]{:S(2)}, u32[]{:S(2)}) collective-permute-start(f32[256,128]{1,0:T(8,128)S(1)} %half_state.1.refs_7_), channel_id=1, source_target_pairs={{0,1},{1,2},{2,3},{3,0},{4,5},{5,6},{6,7},{7,4},{8,9},{9,10},{10,1... | collective-permute-start | bytes 393224 | tf_op jit(solution)/shard_map/ppermute | solution.py:623
  76.8 42.2 %collective-permute-start.7 = (f32[26,128,128]{2,1,0:T(8,128)}, f32[26,128,128]{2,1,0:T(8,128)S(1)}, u32[]{:S(2)}, u32[]{:S(2)}) collective-permute-start(f32[26,128,128]{2,1,0:T(8,128)} %passed.4.refs_2_), channel_id=1, source_target_pairs={{1,0},{2,3},{5,4},{6,7},{9,8},{10,11},{13,12},{14,15},{17,16},{18,... | collective-permute-start | bytes 5111816 | tf_op jit(solution)/shard_map/ppermute | solution.py:623
  79.2 22.0 %collective-permute-start.1 = (f32[10,128,128]{2,1,0:T(8,128)S(1)}, f32[10,128,128]{2,1,0:T(8,128)S(1)}, u32[]{:S(2)}, u32[]{:S(2)}) collective-permute-start(f32[10,128,128]{2,1,0:T(8,128)S(1)} %front.1), channel_id=1, source_target_pairs={{1,2},{2,1},{5,6},{6,5},{9,10},{10,9},{13,14},{14,13},{17,18},{18,... | collective-permute-start | bytes 1966088 | tf_op jit(solution)/shard_map/ppermute | solution.py:623
  101.3 35.5 %collective-permute-start.2 = (f32[10,128,128]{2,1,0:T(8,128)S(1)}, f32[10,128,128]{2,1,0:T(8,128)S(1)}, u32[]{:S(2)}, u32[]{:S(2)}) collective-permute-start(f32[10,128,128]{2,1,0:T(8,128)S(1)} %passed.3.refs_2_), channel_id=1, source_target_pairs={{1,0},{2,3},{5,4},{6,7},{9,8},{10,11},{13,12},{14,15},{17,16},{18,... | collective-permute-start | bytes 1966088 | tf_op jit(solution)/shard_map/ppermute | solution.py:623
  102.8 1.8 collective-permute-start.8
  150.3 2.7 %collective-permute-start.9 = (f32[512,512]{1,0:T(8,128)S(1)}, f32[512,512]{1,0:T(8,128)S(1)}, u32[]{:S(2)}, u32[]{:S(2)}) collective-permute-start(f32[512,512]{1,0:T(8,128)S(1)} %get-tuple-element.48.refs_0_), channel_id=1, source_target_pairs={{0,4},{4,0},{8,12},{12,8},{16,20},{20,16},{24,28},{28,24},{1,5},{5... | collective-permute-start | bytes 3145736 | tf_op jit(solution)/shard_map/ppermute | solution.py:651
  152.9 2.5 %copy-start.3 = (f32[512]{0:T(512)S(1)}, f32[512]{0:T(512)}, u32[]{:S(2)}) copy-start(f32[512]{0:T(512)} %param.16) | copy-start | bytes 6148
  152.9 22.6 %copy-start.2 = (f32[512]{0:T(512)S(1)}, f32[512]{0:T(512)}, u32[]{:S(2)}) copy-start(f32[512]{0:T(512)} %param.15) | copy-start | bytes 6148
  152.9 22.5 %collective-permute-start.11 = (f32[512,2048]{1,0:T(8,128)S(1)}, f32[512,2048]{1,0:T(8,128)S(1)}, u32[]{:S(2)}, u32[]{:S(2)}) collective-permute-start(f32[512,2048]{1,0:T(8,128)S(1)} %get-tuple-element.51.refs_2_), channel_id=1, source_target_pairs={{0,4},{4,0},{8,12},{12,8},{16,20},{20,16},{24,28},{28,24},{1,5},{5... | collective-permute-start | bytes 12582920 | tf_op jit(solution)/shard_map/ppermute | solution.py:651
  153.1 22.4 %collective-permute-start.10 = (f32[512,2048]{1,0:T(8,128)S(1)}, f32[512,2048]{1,0:T(8,128)S(1)}, u32[]{:S(2)}, u32[]{:S(2)}) collective-permute-start(f32[512,2048]{1,0:T(8,128)S(1)} %get-tuple-element.52.refs_3_), channel_id=1, source_target_pairs={{0,4},{4,0},{8,12},{12,8},{16,20},{20,16},{24,28},{28,24},{1,5},{5... | collective-permute-start | bytes 12582920 | tf_op jit(solution)/shard_map/ppermute | solution.py:651
  153.4 2.0 %copy-start = (f32[512,2048]{1,0:T(8,128)}, f32[512,2048]{1,0:T(8,128)S(1)}, u32[]{:S(2)}) copy-start(f32[512,2048]{1,0:T(8,128)S(1)} %get-tuple-element.52.refs_3_) | copy-start | bytes 12582916
  175.5 2.2 %copy-start.1 = (f32[512,2048]{1,0:T(8,128)S(1)}, f32[512,2048]{1,0:T(8,128)}, u32[]{:S(2)}) copy-start(f32[512,2048]{1,0:T(8,128)} %copy-done) | copy-start | bytes 12582916

commit v8 on v6

--- a/solution.py
+++ b/solution.py
@@ -226,8 +226,33 @@
         [whole(n, n)],
         [((n, n), F32)],
         "inverse",
-        limit=10,
+        limit=6,
     )(mine, other, control_cost[None])[0]
+
+
+def folded(block, blk):
+    n = block.shape[0] // blk
+    half = blk // 2
+    tiles = {(i, j): block[i * blk : (i + 1) * blk, j * blk : (j + 1) * blk] for i, j in lower(n)}
+    last = tiles.pop((n - 1, n - 1))
+    for d, (r, c) in enumerate(((0, 0), (half, 0), (half, half))):
+        tile, part = tiles[d, d], last[r : r + half, c : c + half]
+        top = jnp.concatenate((tile[:half, :half], part), axis=1)
+        tiles[d, d] = jnp.concatenate((top, tile[half:]), axis=0)
+    return list(tiles.values())
+
+
+def unfolded(tiles, n):
+    half = tiles.shape[1] // 2
+    out = {place: tiles[t] for t, place in enumerate(lower(n)[:-1])}
+    parts = [out[d, d][:half, half:] for d in range(3)]
+    for d in range(3):
+        tile = out[d, d]
+        top = jnp.concatenate((tile[:half, :half], tile[half:, :half].T), axis=1)
+        out[d, d] = jnp.concatenate((top, tile[half:]), axis=0)
+    top = jnp.concatenate((parts[0], parts[1].T), axis=1)
+    out[n - 1, n - 1] = jnp.concatenate((top, jnp.concatenate(parts[1:], axis=1)), axis=0)
+    return [out[place] for place in lower(n)]
 
 
 def tiled(block, blk):
@@ -237,7 +262,7 @@
 
 def pack_kernel(blk, where, own, x_ref, *refs):
     *blocks, out = refs
-    diag = [own[i * blk : (i + 1) * blk, j * blk : (j + 1) * blk] for i, j in lower(own.shape[0] // blk)]
+    diag = folded(own[...], blk)
     x = [x_ref[0, :blk], x_ref[0, blk:]]
     for t, tile in enumerate(diag + x + [tile for block in blocks for tile in tiled(block, blk)]):
         out[t] = tile
@@ -247,7 +272,7 @@
     rows = cost_rows.shape[0]
     samples = parent_state.shape[2]
     picks = [OWN, *blocks]
-    size = len(lower(rows // blk)) + 2 + (len(picks) - 1) * (rows // blk) ** 2
+    size = len(lower(rows // blk)) + 1 + (len(picks) - 1) * (rows // blk) ** 2
     specs = [pl.BlockSpec((rows, rows), functools.partial(lambda t, i, where: (0, where[t]), t)) for t in picks]
     specs.insert(1, pl.BlockSpec((1, rows // 2, samples), lambda i, where: (where[PARENT], where[CORE], 0)))
     args = [outside(cost_rows)] * len(picks)
@@ -276,9 +301,10 @@
 
 def unpack(tiles, step, n, xh, xl):
     blk = tiles.shape[1]
-    lead = len(lower(n))
+    lead = len(lower(n)) - 1
+    diag = unfolded(tiles, n) if step == 0 else None
     for t, (i, j) in enumerate(lower(n) if step == 0 else [(i, j) for i in range(n) for j in range(n)]):
-        tile = tiles[t if step == 0 else lead + 2 + (step - 1) * n * n + t]
+        tile = diag[t] if step == 0 else tiles[lead + 2 + (step - 1) * n * n + t]
         places = [(i, j, tile)] + ([(j, i, tile.T)] if step == 0 and i != j else [])
         for r, c, value in places:
             at = slice(r * blk, (r + 1) * blk), slice(c * blk, (c + 1) * blk)
@@ -286,32 +312,33 @@
 
 
 def collect_kernel(where, pair, mid, end, mid_last, end_last, out):
-    out[:2] = pair[...]
+    lead = mid_last.shape[0] - 2
+    out[:2] = pair[lead : lead + 2]
 
     @pl.when(where[EDGE] == 1)
     def _():
-        out[2:4] = end[...]
-        out[4:6] = end_last[...]
+        out[2:4] = end[lead : lead + 2]
+        out[4:6] = end_last[lead : lead + 2]
 
     @pl.when(where[EDGE] == 0)
     def _():
-        out[2:4] = mid[...]
-        out[4:6] = mid_last[...]
+        out[2:4] = mid[lead : lead + 2]
+        out[4:6] = mid_last[lead : lead + 2]
 
 
 def collect(where, messages, after):
     blk = messages[0].shape[1]
-    lead = messages[3].shape[0] // 2 - 1
+    lead = messages[3].shape[0] - 2
     return call(
         collect_kernel,
         (1,),
         1,
-        [pl.BlockSpec((2, blk, blk), lambda i, where: (lead, 0, 0))] * 5,
+        [pl.BlockSpec((lead + 2, blk, blk), lambda i, where: (0, 0, 0))] * 5,
         [whole(6, blk, blk)],
         [((6, blk, blk), F32)],
         "collect",
         after=[after],
-        limit=4,
+        limit=10,
     )(where, *messages)[0]
 
 
@@ -537,7 +564,8 @@
         [whole(orders, rows), s_spec, whole(rows, samples)],
         [((orders, rows), F32), ((rows, width), F32), ((rows, samples), F32)],
         "final",
-        [pltpu.VMEM((2, rows, orders), BF16), pltpu.VMEM((orders, samples), F32)],
+        limit=16,
+        scratch=[pltpu.VMEM((2, rows, orders), BF16), pltpu.VMEM((orders, samples), F32)],
     )(where, hinv, *own, other[1], *other, state_cost[None], x, y, outside(fh), outside(fl))
 
 

time: 190 us -> 182 us (0.958)
  waiting for transfers between devices: 35.4 us -> 30.2 us
  local copies, waits for them, and re-layouts: 4.45 us -> 0.34 us
    ppermute x5, waiting for transfers between devices: 32.7 us -> 27.5 us  [moved(): return lax.ppermute(x, 'row', pairs)]
    unnamed x14 -> x10, local copies, waits for them, and re-layouts: 4.37 us -> 0.25 us
  transfers between devices with their start and end apart: 9 -> 9, of which waited for: 3 -> 3; matrix products, arithmetic and copies ran while one was open for 0% -> 0% of each run, Pallas kernels for 56% -> 60%
where the time goes in v8:
time: 182 us; the launch traced here: 181 us
  Pallas kernels  139 us (76%)
  waiting for transfers between devices  30.2 us (17%)
  starting transfers between devices  9.88 us (5%)
    pallas_call x15, Pallas kernels, run(): built(*args[:prefetch], *placed, *after, *[resident(x) if keep else x for...  139 us
    ppermute x5, waiting for transfers between devices, moved(): return lax.ppermute(x, 'row', pairs)  27.5 us
    ppermute x5, starting transfers between devices, moved(): return lax.ppermute(x, 'row', pairs)  8.74 us
  transfers between devices with their start and end apart: 9, of which 3 were waited for; matrix products, arithmetic and copies ran while one was open for 0% of the time, Pallas kernels for 60%

profile of v8, /device:TPU:0, one launch (start us, length us, event | category | flops | bytes accessed | tf_op | source)
XLA Modules:
  0.0 181.4 jit_solution(5948919193016028036)
XLA Ops:
  0.7 0.1 stack.39.refs_0_
  0.7 2.7 %pack.2.refs_4_.refs_5_ = f32[43,128,128]{2,1,0:T(8,128)S(1)} custom-call(s32[8]{0:T(128)S(1)} %stack.39.refs_0_, f32[512,2048]{1,0:T(8,128)} %bitcast.18, f32[4,512,128]{2,1,0:T(8,128)} %refs_1_.6, f32[512,2048]{1,0:T(8,128)} %bitcast.19, f32[512,2048]{1,0:T(8,128)} %bitcast.20), custom_call_target="tpu_custom_call" | custom-call | flops 1 | bytes 1 | tf_op jit(solution)/shard_map/pack/pallas_call | solution.py:95
  3.5 3.1 %collective-permute-start = (f32[43,128,128]{2,1,0:T(8,128)S(1)}, f32[43,128,128]{2,1,0:T(8,128)}, u32[]{:S(2)}, u32[]{:S(2)}) collective-permute-start(f32[43,128,128]{2,1,0:T(8,128)S(1)} %pack.2.refs_4_.refs_5_), channel_id=1, source_target_pairs={{0,1},{1,0},{2,3},{3,2},{4,5},{5,4},{6,7},{7,6},{8,9},{9,8},{10,11... | collective-permute-start | bytes 8454152 | tf_op jit(solution)/shard_map/ppermute | solution.py:648
  6.6 3.6 %pack.3.refs_6_ = f32[27,128,128]{2,1,0:T(8,128)} custom-call(s32[8]{0:T(128)S(1)} %stack.39.refs_0_, f32[512,2048]{1,0:T(8,128)} %bitcast.21, f32[4,512,128]{2,1,0:T(8,128)} %refs_1_.6, f32[512,2048]{1,0:T(8,128)} %bitcast.22, f32[43,128,128]{2,1,0:T(8,128)S(1)} %pack.2.refs_4_.refs_5_), custom_call_target="tpu_custom_call" | custom-call | flops 1 | bytes 1 | tf_op jit(solution)/shard_map/pack/pallas_call | solution.py:95
  10.2 2.0 %collective-permute-start.3 = (f32[27,128,128]{2,1,0:T(8,128)}, f32[27,128,128]{2,1,0:T(8,128)}, u32[]{:S(2)}, u32[]{:S(2)}) collective-permute-start(f32[27,128,128]{2,1,0:T(8,128)} %pack.3.refs_6_), channel_id=1, source_target_pairs={{1,2},{2,1},{5,6},{6,5},{9,10},{10,9},{13,14},{14,13},{17,18},{18,... | collective-permute-start | bytes 5308424 | tf_op jit(solution)/shard_map/ppermute | solution.py:648
  12.3 15.0 %dense.1 = (bf16[2048,2560]{1,0:T(8,128)(2,1)}, bf16[2048,2560]{1,0:T(8,128)(2,1)}, bf16[2,1024,2048]{2,1,0:T(8,128)(2,1)S(1)}) custom-call(s32[8]{0:T(128)S(1)} %stack.39.refs_0_, s32[1,16,8]{2,1,0:T(8,128)S(1)} %copy.27.refs_1_, s32[1,16,2]{2,1,0:T(8,128)S(1)} %copy.28.refs_2_, f32[16,8,128,128]{3,2,1,0:T(8,128)} %bitcast.24, ...), custom_call_target="tpu_custom_call" | custom-call | flops 1 | bytes 1 | tf_op jit(solution)/shard_map/dense/pallas_call | solution.py:95
  27.9 24.7 %begin.1 = (f32[1024,2048]{1,0:T(8,128)S(1)}, f32[512,2048]{1,0:T(8,128)S(1)}, f32[512,2048]{1,0:T(8,128)S(1)}, f32[512,512]{1,0:T(8,128)S(1)}, f32[8,128]{1,0:T(8,128)S(1)}) custom-call(s32[8]{0:T(128)S(1)} %stack.39.refs_0_, f32[1]{0:T(128)S(6)} %copy.44.refs_1_, f32[512,2048]{1,0:T(8,128)} %bitcast.23, ...), custom_call_target="tpu_custom_call" | custom-call | flops 1 | bytes 1 | tf_op jit(solution)/shard_map/begin/pallas_call | solution.py:95
  52.6 1.3 collective-permute-start.4
  53.9 14.7 %collective-permute-done.refs_2_.refs_0_.refs_1_ = f32[43,128,128]{2,1,0:T(8,128)} collective-permute-done((f32[43,128,128]{2,1,0:T(8,128)S(1)}, f32[43,128,128]{2,1,0:T(8,128)}, u32[]{:S(2)}, u32[]{:S(2)}) %collective-permute-start) | collective-permute-done | bytes 2818080 | tf_op jit(solution)/shard_map/ppermute | solution.py:648
  68.6 1.2 front.1
  69.8 0.9 collective-permute-start.1
  70.7 21.4 %stage.3 = (f32[512,2048]{1,0:T(8,128)S(1)}, f32[512,2048]{1,0:T(8,128)S(1)}, f32[512,512]{1,0:T(8,128)S(1)}, f32[1024,2048]{1,0:T(8,128)S(1)}, f32[8,128]{1,0:T(8,128)S(1)}) custom-call(s32[8]{0:T(128)S(1)} %stack.39.refs_0_, f32[1]{0:T(128)S(6)} %copy.44.refs_1_, ...), custom_call_target="tpu_custom_call", output_to_operand_aliasing={{0}: (9, {}), {1}: (10, {}), {2}: (11, {}), {3}: (4, {})} | custom-call | flops 1 | bytes 1 | tf_op jit(solution)/shard_map/stage/pallas_call | solution.py:95
  92.1 1.5 collective-permute-start.2
  93.6 12.8 %collective-permute-done.4.refs_3_ = f32[27,128,128]{2,1,0:T(8,128)S(1)} collective-permute-done((f32[27,128,128]{2,1,0:T(8,128)}, f32[27,128,128]{2,1,0:T(8,128)S(1)}, u32[]{:S(2)}, u32[]{:S(2)}) %collective-permute-start.4) | collective-permute-done | bytes 1769504 | tf_op jit(solution)/shard_map/ppermute | solution.py:648
  106.4 17.5 %stage.4 = (f32[512,2048]{1,0:T(8,128)S(1)}, f32[512,2048]{1,0:T(8,128)S(1)}, f32[512,512]{1,0:T(8,128)S(1)}, f32[1024,2048]{1,0:T(8,128)S(1)}, f32[8,128]{1,0:T(8,128)S(1)}) custom-call(s32[8]{0:T(128)S(1)} %stack.39.refs_0_, f32[1]{0:T(128)S(6)} %copy.44.refs_1_, ...), custom_call_target="tpu_custom_call", output_to_operand_aliasing={{0}: (10, {}), {1}: (11, {}), {2}: (12, {}), {3}: (5, {})} | custom-call | flops 1 | bytes 1 | tf_op jit(solution)/shard_map/stage/pallas_call | solution.py:95
  123.9 2.2 %collect.1.refs_13_.refs_2_ = f32[6,128,128]{2,1,0:T(8,128)S(1)} custom-call(s32[8]{0:T(128)S(1)} %stack.39.refs_0_, f32[43,128,128]{2,1,0:T(8,128)} %collective-permute-done.refs_2_.refs_0_.refs_1_, f32[27,128,128]{2,1,0:T(8,128)} %passed.4.refs_2_, f32[27,128,128]{2,1,0:T(8,128)S(1)} %collective-permute-done.4.refs_3_, ...), custom_call_target="tpu_custom_call" | custom-call | flops 1 | bytes 1 | tf_op jit(solution)/shard_map/collect/pallas_call | solution.py:95
  126.1 13.1 %stage.5 = (f32[512,2048]{1,0:T(8,128)S(1)}, f32[512,2048]{1,0:T(8,128)S(1)}, f32[512,512]{1,0:T(8,128)S(1)}, f32[8,128]{1,0:T(8,128)S(1)}) custom-call(s32[8]{0:T(128)S(1)} %stack.39.refs_0_, f32[1]{0:T(128)S(6)} %copy.44.refs_1_, f32[11,128,128]{2,1,0:T(8,128)S(1)} %passed.3.refs_4_.refs_2_, ...), custom_call_target="tpu_custom_call", output_to_operand_aliasing={{0}: (10, {}), {1}: (11, {}), {2}: (12, {})} | custom-call | flops 1 | bytes 1 | tf_op jit(solution)/shard_map/stage/pallas_call | solution.py:95
  139.3 0.5 collective-permute-start.6
  139.8 2.7 %collective-permute-done.6.refs_3_ = f32[6,128,128]{2,1,0:T(8,128)S(1)} collective-permute-done((f32[6,128,128]{2,1,0:T(8,128)S(1)}, f32[6,128,128]{2,1,0:T(8,128)S(1)}, u32[]{:S(2)}, u32[]{:S(2)}) %collective-permute-start.6) | collective-permute-done | bytes 393248 | tf_op jit(solution)/shard_map/ppermute | solution.py:675
  142.5 5.1 %drift.1 = (f32[2048,128]{1,0:T(8,128)S(1)}, f32[512,128]{1,0:T(8,128)S(1)}) custom-call(s32[8]{0:T(128)S(1)} %stack.39.refs_0_, f32[4,512,128]{2,1,0:T(8,128)} %refs_1_.6, f32[6,128,128]{2,1,0:T(8,128)S(1)} %collect.1.refs_13_.refs_2_, f32[6,128,128]{2,1,0:T(8,128)S(1)} %collective-permute-done.6.refs_3_, ...), custom_call_target="tpu_custom_call" | custom-call | flops 1 | bytes 1 | tf_op jit(solution)/shard_map/drift/pallas_call | solution.py:95
  147.7 0.2 collective-permute-start.7
  147.9 0.4 collective-permute-start.8
  148.3 19.8 %inverse.1.refs_1_ = f32[512,512]{1,0:T(8,128)S(1)} custom-call(f32[512,512]{1,0:T(8,128)S(1)} %get-tuple-element.50.refs_0_, f32[512,512]{1,0:T(8,128)S(1)} %collective-permute-done.5.refs_1_.refs_0_, f32[1,512]{1,0:T(1,128)S(1)} %bitcast.17), custom_call_target="tpu_custom_call" | custom-call | flops 1 | bytes 1 | tf_op jit(solution)/shard_map/inverse/pallas_call | solution.py:95
  168.2 13.2 %final.1 = (f32[512,512]{1,0:T(8,128)}, f32[512,2048]{1,0:T(8,128)}, f32[512,128]{1,0:T(8,128)}) custom-call(s32[8]{0:T(128)S(1)} %stack.39.refs_0_, f32[512,512]{1,0:T(8,128)S(1)} %inverse.1.refs_1_, f32[512,2048]{1,0:T(8,128)S(1)} %get-tuple-element.55.refs_2_, f32[512,2048]{1,0:T(8,128)S(1)} %get-tuple-element.56.refs_3_, ...), custom_call_target="tpu_custom_call" | custom-call | flops 1 | bytes 1 | tf_op jit(solution)/shard_map/final/pallas_call | solution.py:95
  (20 shorter events, 0.3 us)
Async XLA Ops:
  3.5 8.6 %copy-start.2 = (s32[1,16,8]{1,2,0:T(8,128)S(1)}, s32[1,16,8]{1,2,0:T(8,128)}, u32[]{:S(2)}) copy-start(s32[1,16,8]{1,2,0:T(8,128)} %param.11) | copy-start | bytes 1540
  3.5 8.7 %copy-start.3 = (s32[1,16,2]{1,2,0:T(2,128)S(1)}, s32[1,16,2]{1,2,0:T(2,128)}, u32[]{:S(2)}) copy-start(s32[1,16,2]{1,2,0:T(2,128)} %param.13) | copy-start | bytes 388
  3.5 65.1 %collective-permute-start = (f32[43,128,128]{2,1,0:T(8,128)S(1)}, f32[43,128,128]{2,1,0:T(8,128)}, u32[]{:S(2)}, u32[]{:S(2)}) collective-permute-start(f32[43,128,128]{2,1,0:T(8,128)S(1)} %pack.2.refs_4_.refs_5_), channel_id=1, source_target_pairs={{0,1},{1,0},{2,3},{3,2},{4,5},{5,4},{6,7},{7,6},{8,9},{9,8},{10,11... | collective-permute-start | bytes 8454152 | tf_op jit(solution)/shard_map/ppermute | solution.py:648
  10.2 42.5 %collective-permute-start.3 = (f32[27,128,128]{2,1,0:T(8,128)}, f32[27,128,128]{2,1,0:T(8,128)}, u32[]{:S(2)}, u32[]{:S(2)}) collective-permute-start(f32[27,128,128]{2,1,0:T(8,128)} %pack.3.refs_6_), channel_id=1, source_target_pairs={{1,2},{2,1},{5,6},{6,5},{9,10},{10,9},{13,14},{14,13},{17,18},{18,... | collective-permute-start | bytes 5308424 | tf_op jit(solution)/shard_map/ppermute | solution.py:648
  52.6 53.8 %collective-permute-start.4 = (f32[27,128,128]{2,1,0:T(8,128)}, f32[27,128,128]{2,1,0:T(8,128)S(1)}, u32[]{:S(2)}, u32[]{:S(2)}) collective-permute-start(f32[27,128,128]{2,1,0:T(8,128)} %passed.4.refs_2_), channel_id=1, source_target_pairs={{1,0},{2,3},{5,4},{6,7},{9,8},{10,11},{13,12},{14,15},{17,16},{18,... | collective-permute-start | bytes 5308424 | tf_op jit(solution)/shard_map/ppermute | solution.py:648
  69.8 22.3 %collective-permute-start.1 = (f32[11,128,128]{2,1,0:T(8,128)S(1)}, f32[11,128,128]{2,1,0:T(8,128)S(1)}, u32[]{:S(2)}, u32[]{:S(2)}) collective-permute-start(f32[11,128,128]{2,1,0:T(8,128)S(1)} %front.1), channel_id=1, source_target_pairs={{1,2},{2,1},{5,6},{6,5},{9,10},{10,9},{13,14},{14,13},{17,18},{18,... | collective-permute-start | bytes 2162696 | tf_op jit(solution)/shard_map/ppermute | solution.py:648
  92.1 31.8 %collective-permute-start.2 = (f32[11,128,128]{2,1,0:T(8,128)S(1)}, f32[11,128,128]{2,1,0:T(8,128)S(1)}, u32[]{:S(2)}, u32[]{:S(2)}) collective-permute-start(f32[11,128,128]{2,1,0:T(8,128)S(1)} %passed.3.refs_4_.refs_2_), channel_id=1, source_target_pairs={{1,0},{2,3},{5,4},{6,7},{9,8},{10,11},{13,12},{14,15},{17,16},{18,... | collective-permute-start | bytes 2162696 | tf_op jit(solution)/shard_map/ppermute | solution.py:648
  139.3 8.4 %collective-permute-start.5 = (f32[512,512]{1,0:T(8,128)S(1)}, f32[512,512]{1,0:T(8,128)S(1)}, u32[]{:S(2)}, u32[]{:S(2)}) collective-permute-start(f32[512,512]{1,0:T(8,128)S(1)} %get-tuple-element.50.refs_0_), channel_id=1, source_target_pairs={{0,4},{4,0},{8,12},{12,8},{16,20},{20,16},{24,28},{28,24},{1,5},{5... | collective-permute-start | bytes 3145736 | tf_op jit(solution)/shard_map/ppermute | solution.py:675
  139.3 3.2 %collective-permute-start.6 = (f32[6,128,128]{2,1,0:T(8,128)S(1)}, f32[6,128,128]{2,1,0:T(8,128)S(1)}, u32[]{:S(2)}, u32[]{:S(2)}) collective-permute-start(f32[6,128,128]{2,1,0:T(8,128)S(1)} %collect.1.refs_13_.refs_2_), channel_id=1, source_target_pairs={{0,4},{4,0},{8,12},{12,8},{16,20},{20,16},{24,28},{28,24},{1,5},{5... | collective-permute-start | bytes 1179656 | tf_op jit(solution)/shard_map/ppermute | solution.py:675
  147.6 0.7 copy-start.1
  147.7 20.5 %copy-start = (f32[512]{0:T(512)S(1)}, f32[512]{0:T(512)}, u32[]{:S(2)}) copy-start(f32[512]{0:T(512)} %param.15) | copy-start | bytes 6148
  147.7 20.5 %collective-permute-start.7 = (f32[512,2048]{1,0:T(8,128)S(1)}, f32[512,2048]{1,0:T(8,128)S(1)}, u32[]{:S(2)}, u32[]{:S(2)}) collective-permute-start(f32[512,2048]{1,0:T(8,128)S(1)} %get-tuple-element.56.refs_3_), channel_id=1, source_target_pairs={{0,4},{4,0},{8,12},{12,8},{16,20},{20,16},{24,28},{28,24},{1,5},{5... | collective-permute-start | bytes 12582920 | tf_op jit(solution)/shard_map/ppermute | solution.py:675
  147.9 20.3 %collective-permute-start.8 = (f32[512,2048]{1,0:T(8,128)S(1)}, f32[512,2048]{1,0:T(8,128)S(1)}, u32[]{:S(2)}, u32[]{:S(2)}) collective-permute-start(f32[512,2048]{1,0:T(8,128)S(1)} %get-tuple-element.55.refs_2_), channel_id=1, source_target_pairs={{0,4},{4,0},{8,12},{12,8},{16,20},{20,16},{24,28},{28,24},{1,5},{5... | collective-permute-start | bytes 12582920 | tf_op jit(solution)/shard_map/ppermute | solution.py:675
